TPU v7x, 512 devices: a whole 4x8x8 slice. The times are simulated.
512 devices in a mesh: span: 16 (over y, x_lo), fsdp: 32 (over x_hi, z, core).
Axes of the slice: x: 4 (x_hi: 2, x_lo: 2; x = x_hi * 2 + x_lo), y: 8, z: 8, core: 2. Of those that a mesh axis runs over, the one named last changes fastest.
Arguments:
- tokens: bfloat16 [8192, 6144], P('span', 'fsdp'), may hold values from -64 to 64
- queries: bfloat16 [8192, 4096], P('span', 'fsdp'), may hold values from -12 to 12
- key_weight: bfloat16 [6144, 4096], P('span', 'fsdp'), may hold values from -0.076546554 to 0.076546554
- value_weight: bfloat16 [6144, 4096], P('span', 'fsdp'), may hold values from -0.078125 to 0.078125
- modulation: bfloat16 [8, 12288], replicated, may hold values from -3 to 3
- levels: int32 [16], replicated, may hold values from 0 to 7
- visible: int32 [16, 16], replicated, may hold values from 0 to 1, as said below
- counts: int32 [16], replicated, may hold values from 256 to 512, as said below
Outputs:
- attended: bfloat16 [8192, 4096], P('span', 'fsdp')
Inputs may be any that keep to these rules, and one draw needn't show every extreme that they name: visible[c, b] is 1 only where b < c, and always where b = c - 1. The live tokens of a span are its first counts[c] slots; some span is full.
All inputs are finite; a program needn't handle non-finite values.
Results may differ from a plain program's by a relative error of at most 0.0078.
Values may be sent and summed in bfloat16 or wider, within the bound.
No kernel may reach another device: no remote copies, remote signals or barrier semaphores. Data moves between devices by JAX's collectives and lax.ppermute only.
A program may use at most 64 MiB of HBM per device.

v0:
```python
import jax
import jax.numpy as jnp
from jax import lax
from jax.sharding import PartitionSpec as P

HD = 128


neg_big = -1e30
epsilon = 1e-06


def attend_block(running, key_block, first_row, query_heads, counts, span_len):
    best_score, denominator, accumulated = running
    width_keys = key_block.shape[1]
    key_pos = first_row + jnp.arange(width_keys, dtype=jnp.int32)
    key_span = key_pos // span_len
    span_ids = jnp.arange(counts.shape[0], dtype=jnp.int32)
    limits = jnp.sum(jnp.where(key_span[:, None] == span_ids[None, :], counts[None, :], 0), axis=1)
    live_keys = key_pos - key_span * span_len < limits
    scores = jnp.einsum(
        "qhd,khd->hqk", query_heads, key_block[0], preferred_element_type=jnp.float32
    )
    scores = jnp.where(live_keys[None, None, :], scores * query_heads.shape[2] ** (-0.5), neg_big)
    new_best = jnp.maximum(best_score, jnp.max(scores, axis=2))
    weights = jnp.where(live_keys[None, None, :], jnp.exp(scores - new_best[:, :, None]), 0.0)
    fading = jnp.exp(best_score - new_best)
    denominator = denominator * fading + jnp.sum(weights, axis=2)
    update = jnp.einsum(
        "hqk,khd->qhd",
        weights.astype(jnp.bfloat16),
        key_block[1],
        preferred_element_type=jnp.float32,
    )
    accumulated = accumulated * jnp.transpose(fading)[:, :, None] + update
    return (new_best, denominator, accumulated)


def on_device(tokens, queries, key_weight, value_weight, modulation, levels, visible, counts):
    span_id = lax.axis_index("span")
    span_count = lax.axis_size("span")
    slot_id = lax.axis_index("fsdp")
    span_len = tokens.shape[0]
    piece_width = tokens.shape[1]
    model_width = piece_width * lax.axis_size("fsdp")
    head_size = HD
    level_hot = (jnp.arange(modulation.shape[0], dtype=jnp.int32) == levels[span_id]).astype(
        jnp.bfloat16
    )
    mod_row = jnp.dot(level_hot[None, :], modulation, preferred_element_type=jnp.float32)[0]
    shift_row = lax.dynamic_slice_in_dim(mod_row, slot_id * piece_width, piece_width)
    scale_row = lax.dynamic_slice_in_dim(mod_row, model_width + slot_id * piece_width, piece_width)
    widened = tokens.astype(jnp.float32)
    row_sum, row_square = lax.psum(
        (jnp.sum(widened, axis=1), jnp.sum(widened * widened, axis=1)), "fsdp"
    )
    row_mean = row_sum / model_width
    variance = row_square / model_width - row_mean * row_mean
    normed = (
        (widened - row_mean[:, None]) * lax.rsqrt(variance + epsilon)[:, None] * (1.0 + scale_row)
        + shift_row
    ).astype(jnp.bfloat16)
    full_key, full_value = (
        lax.all_gather(key_weight, "span", axis=0, tiled=True),
        lax.all_gather(value_weight, "span", axis=0, tiled=True),
    )
    piece = lax.all_gather(normed, "fsdp", axis=1, tiled=True)
    key_part = jnp.dot(piece, full_key, preferred_element_type=jnp.float32)
    value_part = jnp.dot(piece, full_value, preferred_element_type=jnp.float32)
    local_heads = key_weight.shape[1] // head_size
    kv_heads = (
        jnp.stack([key_part, value_part])
        .astype(jnp.bfloat16)
        .reshape(2, span_len, local_heads, head_size)
    )
    query_heads = queries.reshape(span_len, local_heads, head_size)
    vis_row = visible[span_id]
    seen_spans = jnp.where(jnp.arange(span_count, dtype=jnp.int32) == span_id, 1, vis_row)
    start_state = (
        jnp.full((local_heads, span_len), neg_big, jnp.float32),
        jnp.zeros((local_heads, span_len), jnp.float32),
        jnp.zeros((span_len, local_heads, head_size), jnp.float32),
    )
    key_piece = lax.all_gather(kv_heads, "span", axis=1, tiled=True)
    piece_rows = key_piece.shape[1]
    step_rows = min(piece_rows, span_len)

    def one_block(turn_number, inner_state):
        offset = turn_number * step_rows
        key_block = lax.dynamic_slice_in_dim(key_piece, offset, step_rows, 1)

        def absorb(carried):
            return attend_block(carried, key_block, offset, query_heads, counts, span_len)

        def unchanged(carried):
            return carried

        return lax.cond(seen_spans[offset // span_len] == 1, absorb, unchanged, inner_state)

    running = lax.fori_loop(0, piece_rows // step_rows, one_block, start_state)
    best_score, denominator, accumulated = running
    attended = accumulated / jnp.transpose(denominator)[:, :, None]
    live_rows = jnp.arange(span_len, dtype=jnp.int32) < counts[span_id]
    attended = jnp.where(live_rows[:, None, None], attended, 0.0)
    return attended.reshape(span_len, local_heads * head_size).astype(jnp.bfloat16)


def solution(mesh):
    return jax.shard_map(
        on_device,
        mesh=mesh,
        in_specs=(
            P("span", "fsdp"),
            P("span", "fsdp"),
            P("span", "fsdp"),
            P("span", "fsdp"),
            P(),
            P(),
            P(),
            P(),
        ),
        out_specs=P("span", "fsdp"),
        check_vma=False,
    )
```

profile of v0, /device:TPU:56, one launch (start us, length us, event | category | flops | bytes accessed | tf_op | source)
XLA Modules:
  0.0 422.6 jit_solution(881812608816450142)
XLA Ops:
  6.5 0.7 all-gather.7.cloned.1.call-update
  7.3 1.2 dynamic_slice.40
  8.6 1.0 convert_reduce_fusion
  9.6 76.2 %all-reduce = (f32[512]{0:T(512)S(1)}, f32[512]{0:T(512)S(1)}) all-reduce(f32[512]{0:T(512)S(1)} %get-tuple-element.326, f32[512]{0:T(512)S(1)} %get-tuple-element.325), channel_id=1, replica_groups=mesh['span'=16,'fsdp'=32] {'fsdp'}, use_global_device_ids=true, to_apply=%region_3.0 | all-reduce | flops 1024 | bytes 8192 | tf_op jit(solution)/shard_map/psum | solution.py:54
  85.7 0.8 fusion.23
  86.7 1.7 fusion.20
  88.5 0.7 all-gather.9.cloned.1.call-update
  89.2 101.3 %all-gather.5.cloned.1.call-done = bf16[512,6144]{0,1:T(8,128)(2,1)} async-done(((bf16[512,192]{0,1:T(8,128)(2,1)}), bf16[512,6144]{0,1:T(8,128)(2,1)}) %all-gather.5.cloned.1.call-update) | async-done | bytes 6291472 | tf_op jit(solution)/shard_map/all_gather | solution.py:67
  190.5 5.1 %fusion.15 = bf16[1,512,1,128]{3,1,2,0:T(8,128)(2,1)S(1)} fusion(bf16[512,6144]{0,1:T(8,128)(2,1)} %all-gather.5.cloned.1.call-done, bf16[6144,128]{1,0:T(8,128)(2,1)} %all-gather.7.cloned.1.call-done), kind=kOutput, calls=%fused_computation.32 | convolution fusion | flops 805371904 | bytes 7995392 | tf_op jit(solution)/shard_map/dot_general | solution.py:68
  195.6 64.4 %all-gather.9.cloned.1.call-done = bf16[6144,128]{1,0:T(8,128)(2,1)} async-done(((bf16[384,128]{1,0:T(8,128)(2,1)}), bf16[6144,128]{1,0:T(8,128)(2,1)}) %all-gather.9.cloned.1.call-update) | async-done | bytes 1572880 | tf_op jit(solution)/shard_map/all_gather | solution.py:65
  260.0 5.1 %fusion.16 = bf16[1,512,1,128]{3,1,2,0:T(8,128)(2,1)S(1)} fusion(bf16[512,6144]{0,1:T(8,128)(2,1)} %all-gather.5.cloned.1.call-done, bf16[6144,128]{1,0:T(8,128)(2,1)} %all-gather.9.cloned.1.call-done), kind=kOutput, calls=%fused_computation.33 | convolution fusion | flops 805371904 | bytes 7995392 | tf_op jit(solution)/shard_map/dot_general | solution.py:69
  265.1 0.7 pad_maximum_fusion
  265.8 0.6 dynamic_slice.38
  266.4 0.7 compare_select_fusion
  267.7 101.5 %all-gather.11.cloned.1.call-done = bf16[2,8192,1,128]{3,1,2,0:T(8,128)(2,1)} async-done(((bf16[2,512,1,128]{3,1,2,0:T(8,128)(2,1)}), bf16[2,8192,1,128]{3,1,2,0:T(8,128)(2,1)}) %all-gather.11.cloned.1.call-update) | async-done | bytes 4194320 | tf_op jit(solution)/shard_map/all_gather | solution.py:84
  369.2 45.8 %while.19 = (s32[]{:T(128)}, f32[1,512]{1,0:T(1,128)S(1)}, f32[1,512]{1,0:T(1,128)S(1)}, f32[512,1,128]{0,2,1:T(8,128)S(1)}, s32[16]{0:T(128)S(1)}, /*index=5*/s...) while((s32[]{:T(128)}, f32[1,512]{1,0:T(1,128)S(1)}, ...), condition=%wide.region_10.11_spmd, body=%wide.region_4.10_spmd.sunk | while | flops 136751120 | bytes 4106852 | solution.py:100
  370.4 3.0 conditional.2
  370.6 1.2 fusion.28
  372.1 1.3 fusion.1
  373.4 0.6 dynamic_slice.47
  374.6 0.6 dynamic_slice.47
  377.1 0.6 dynamic_slice.47
  378.2 3.0 conditional.2
  378.4 1.2 fusion.28
  379.8 1.3 fusion.1
  381.2 0.6 dynamic_slice.47
  384.8 3.0 conditional.2
  384.9 1.2 fusion.28
  386.4 1.3 fusion.1
  388.9 2.9 conditional.2
  389.1 1.2 fusion.28
  390.6 1.3 fusion.1
  394.3 2.9 conditional.2
  394.4 1.2 fusion.28
  395.9 1.3 fusion.1
  398.4 2.9 conditional.2
  398.6 1.2 fusion.28
  400.1 1.3 fusion.1
  402.6 3.0 conditional.2
  402.7 1.2 fusion.28
  404.2 1.3 fusion.1
  406.7 3.0 conditional.2
  406.9 1.2 fusion.28
  408.4 1.3 fusion.1
  410.9 2.9 conditional.2
  411.0 1.2 fusion.28
  412.5 1.3 fusion.1
  415.2 0.9 fusion.22
  (102 shorter events, 11.3 us)
Async XLA Ops:
  6.5 79.2 %copy-start = (bf16[8,12288]{1,0:T(8,128)(2,1)S(1)}, bf16[8,12288]{1,0:T(8,128)(2,1)}, u32[]{:S(2)}) copy-start(bf16[8,12288]{1,0:T(8,128)(2,1)} %param.16) | copy-start | bytes 589828
  6.5 82.7 %all-gather.7.cloned.1.call-start = ((), (), s32[]{:S(2)}) async-start(), calls=%async_computation.1 | async-start | bytes 1671168 | tf_op jit(solution)/shard_map/all_gather | solution.py:64
  7.3 183.3 %all-gather.5.cloned.1.call-start = ((), (), s32[]{:S(2)}) async-start(), calls=%async_computation | async-start | bytes 6488064 | tf_op jit(solution)/shard_map/all_gather | solution.py:67
  88.4 171.6 %all-gather.9.cloned.1.call-start = ((), (), s32[]{:S(2)}) async-start(), calls=%async_computation.2 | async-start | bytes 1671168 | tf_op jit(solution)/shard_map/all_gather | solution.py:65
  89.2 280.0 %all-gather.11.cloned.1.call-start = ((), (), s32[]{:S(2)}) async-start(), calls=%async_computation.3 | async-start | bytes 4456448 | tf_op jit(solution)/shard_map/all_gather | solution.py:84
  195.6 70.2 %copy-start.2 = (s32[16]{0:T(128)S(1)}, s32[16]{0:T(128)}, u32[]{:S(2)}) copy-start(s32[16]{0:T(128)} %param.19) | copy-start | bytes 196
  195.6 173.6 %copy-start.1 = (bf16[512,128]{1,0:T(8,128)(2,1)S(1)}, bf16[512,128]{1,0:T(8,128)(2,1)}, u32[]{:S(2)}) copy-start(bf16[512,128]{1,0:T(8,128)(2,1)} %param.13) | copy-start | bytes 393220
Sparse Core Ops, SparseCore 0:
  9.4 75.4 all-gather.6
  88.5 101.9 all-gather.4
  192.6 67.3 all-gather.8
  266.0 103.1 all-gather.10
where the time goes:
time: 423 us
  waiting for transfers between devices  269 us (64%)
  blocking collectives  76.2 us (18%)
  matrix products  33.8 us (8%)
  between operations  13.2 us (3%)
  local copies, waits for them, and re-layouts  11.3 us (3%)
  loops' own time  10.5 us (2%)
  other arithmetic  8.85 us (2%)
    all_gather x1, waiting for transfers between devices, on_device(): key_piece = lax.all_gather(kv_heads, 'span', axis=1, tiled=True)  101 us
    all_gather x1, waiting for transfers between devices, on_device(): piece = lax.all_gather(normed, 'fsdp', axis=1, tiled=True)  101 us
    psum x1, blocking collectives, on_device(): lax.psum((jnp.sum(widened, axis=1), jnp.sum(widened * widened, axis=1)),...  76.2 us
    all_gather x1, waiting for transfers between devices, on_device(): lax.all_gather(value_weight, 'span', axis=0, tiled=True)  64.4 us
    dot_general x9, matrix products, attend_block(): jnp.einsum('hqk,khd->qhd', weights.astype(jnp.bfloat16), key_block[1], pr...  11.8 us
    dot_general x9, matrix products, attend_block(): jnp.einsum('qhd,khd->hqk', query_heads, key_block[0], preferred_element_t...  11 us
    another operation x1, loops' own time, on_device(): running = lax.fori_loop(0, piece_rows // step_rows, one_block, start_state)  9.9 us
    dynamic_slice x16, local copies, waits for them, and re-layouts, one_block(): seen_spans[offset // span_len] == 1  9.27 us
  transfers between devices with their start and end apart: 4, of which 3 were waited for; matrix products, arithmetic and copies ran while one was open for 3% of the time, Pallas kernels for 0%

commit v1 on v0

v1 whole, which is shorter than its diff:
```python
import functools

import jax
import jax.numpy as jnp
from jax import lax
from jax.experimental import pallas as pl
from jax.experimental.pallas import tpu as pltpu
from jax.sharding import Mesh, PartitionSpec as P

HD = 128
EPSILON = 1e-06
NEG_BIG = -1e30
LOG2E = 1.4426950408889634
SPAN_AXES = ("yh", "yl", "xl")
FSDP_AXES = ("xh", "z", "c")
SIZES = (4, 2, 2, 2, 8, 2)
QUAD = 4
STAT_ROWS = 16

VMEM = pl.BlockSpec(memory_space=pltpu.VMEM)
SMEM = pl.BlockSpec(memory_space=pltpu.SMEM)


def params(mib=24):
    return pltpu.CompilerParams(vmem_limit_bytes=mib * 1024 * 1024)


def shifted(value, axis, size, by):
    return lax.ppermute(value, axis, [(i, (i + by) % size) for i in range(size)])


def sums_kernel(count, *refs):
    out = refs[-1]
    total = jnp.zeros((1, out.shape[1]), jnp.float32)
    square = jnp.zeros((1, out.shape[1]), jnp.float32)
    for ref in refs[:count]:
        block = ref[...].astype(jnp.float32)
        total += jnp.sum(block, axis=0, keepdims=True)
        square += jnp.sum(block * block, axis=0, keepdims=True)
    if len(refs) > count + 1:
        total += refs[count][0:1, :]
        square += refs[count][1:2, :]
    out[...] = jnp.zeros_like(out)
    out[0:1, :] = total
    out[1:2, :] = square


def row_sums(pieces, earlier=None):
    rest = () if earlier is None else (earlier,)
    width = pieces[0].shape[1]
    return pl.pallas_call(
        functools.partial(sums_kernel, len(pieces)),
        out_shape=jax.ShapeDtypeStruct((8, width), jnp.float32),
        in_specs=[VMEM] * (len(pieces) + len(rest)),
        out_specs=VMEM,
        compiler_params=params(),
    )(*pieces, *rest)


def gathered_weights(index_ref, w_ref, head, group):
    blocks = []
    for offset in (2 * group, 2 * group + 1):
        blocks.append(w_ref[index_ref[offset], head])
        blocks.append(w_ref[index_ref[8 + offset], head])
    return jnp.concatenate(blocks, axis=0)


def norm_kernel(
    index_ref, own_ref, other_ref, scale_ref, shift_ref,
    a0, b0, r1u, r2u, r3u, r4u, r5u, r1d, r2d, r3d, r4d, r5d,
    w_ref, normed_ref, part_ref,
):
    model_width = 2.0 * normed_ref.shape[1]
    stats = own_ref[...] + other_ref[...]
    mean = stats[0:1, :] / model_width
    variance = stats[1:2, :] / model_width - mean * mean
    rstd = lax.rsqrt(variance + EPSILON)
    columns = jnp.transpose(jnp.concatenate([mean, rstd, jnp.zeros((6, mean.shape[1]), jnp.float32)], axis=0))
    mean_col, rstd_col = columns[:, 0:1], columns[:, 1:2]
    feats = a0.shape[0]
    half = feats // 2
    two = 2 * feats
    pairs = [
        [a0[...], b0[...]],
        [r1u[...], r2u[feats:two, :]],
        [r2u[0:feats, :], r3u[feats:two, :]],
        [r3u[0:feats, :], r4u[half : half + feats, :]],
        [r4d[feats : feats + half, :], r4u[0:half, :], r5d[...], r5u[...]],
        [r3d[feats:two, :], r4d[0:feats, :]],
        [r2d[feats:two, :], r3d[0:feats, :]],
        [r1d[...], r2d[0:feats, :]],
    ]
    for offset, pair in enumerate(pairs):
        block = jnp.transpose(jnp.concatenate(pair, axis=0)).astype(jnp.float32)
        block = (block - mean_col) * rstd_col * (1.0 + scale_ref[offset : offset + 1, :]) + shift_ref[
            offset : offset + 1, :
        ]
        normed_ref[:, offset * two : (offset + 1) * two] = block.astype(jnp.bfloat16)
    project(index_ref, 17, normed_ref, w_ref, part_ref)


def project(index_ref, which, normed_ref, w_ref, part_ref):
    head = index_ref[which]
    for group in range(4):
        depth = normed_ref.shape[1] // 4
        product = jnp.dot(
            normed_ref[:, group * depth : (group + 1) * depth],
            gathered_weights(index_ref, w_ref, head, group),
            preferred_element_type=jnp.float32,
        )
        if group == 0:
            part_ref[...] = product
        else:
            part_ref[...] += product


def keep_kernel(index_ref, normed_ref, w_ref, part_ref):
    project(index_ref, 16, normed_ref, w_ref, part_ref)


def join_kernel(mine_ref, theirs_ref, out_ref):
    rows = mine_ref.shape[0]
    total = (mine_ref[...] + theirs_ref[...]).astype(jnp.bfloat16)
    keys = total[:, 0:HD]
    blocks = [jnp.transpose(total[b * HD : (b + 1) * HD, HD : 2 * HD]) for b in range(rows // HD)]
    packed = jnp.concatenate([keys] + blocks, axis=0)
    for copy in range(out_ref.shape[0]):
        out_ref[copy] = packed


def attend_kernel(seen_ref, live_ref, q_ref, kv_ref, out_ref, q_t, best, total, acc):
    span_len = q_ref.shape[1]
    factor = LOG2E * HD ** (-0.5)
    for i in range(QUAD):
        q_t[...] = jnp.transpose(q_ref[i])
        best[...] = jnp.full_like(best, NEG_BIG)
        total[...] = jnp.zeros_like(total)
        acc[...] = jnp.zeros_like(acc)
        for j in range(QUAD):

            @pl.when(seen_ref[i, j] == 1)
            def _():
                scores = jnp.dot(kv_ref[j, 0:span_len, :], q_t[...], preferred_element_type=jnp.float32)
                live = lax.broadcasted_iota(jnp.int32, scores.shape, 0) < live_ref[j]
                scores = jnp.where(live, scores * factor, NEG_BIG)
                top = jnp.maximum(best[0:1, :], jnp.max(scores, axis=0, keepdims=True))
                weights = jnp.where(live, jnp.exp2(scores - top), 0.0)
                fading = jnp.exp2(best[0:1, :] - top)
                total[0:1, :] = total[0:1, :] * fading + jnp.sum(weights, axis=0, keepdims=True)
                best[0:1, :] = top
                values = jnp.concatenate(
                    [kv_ref[j, span_len + b * HD : span_len + (b + 1) * HD, :] for b in range(span_len // HD)],
                    axis=1,
                )
                acc[...] = acc[...] * fading + jnp.dot(
                    values, weights.astype(jnp.bfloat16), preferred_element_type=jnp.float32
                )

        out_ref[i, 0:HD, :] = acc[...].astype(jnp.bfloat16)
        rows = []
        for value in (best[0:1, :], total[0:1, :]):
            for _part in range(3):
                part = value.astype(jnp.bfloat16).astype(jnp.float32)
                rows.append(part)
                value = value - part
        rows.append(jnp.zeros((STAT_ROWS - 6, span_len), jnp.float32))
        out_ref[i, HD : HD + STAT_ROWS, :] = jnp.concatenate(rows, axis=0).astype(jnp.bfloat16)


def merge_kernel(live_ref, part_ref, out_ref):
    span_len = out_ref.shape[0]
    bests, totals = [], []
    for j in range(QUAD):
        stat = part_ref[j, HD : HD + STAT_ROWS, :].astype(jnp.float32)
        bests.append((stat[0:1] + stat[1:2]) + stat[2:3])
        totals.append((stat[3:4] + stat[4:5]) + stat[5:6])
    top = functools.reduce(jnp.maximum, bests)
    share = [jnp.exp2(b - top) for b in bests]
    total = sum(s * t for s, t in zip(share, totals))
    result = sum(s * part_ref[j, 0:HD, :].astype(jnp.float32) for j, s in enumerate(share))
    slot = lax.broadcasted_iota(jnp.int32, total.shape, 1)
    result = jnp.where(slot < live_ref[0], result / total, 0.0)
    out_ref[...] = jnp.transpose(result).astype(jnp.bfloat16)


def on_device(tokens, queries, key_weight, value_weight, modulation, levels, visible, counts):
    span_id = lax.axis_index(SPAN_AXES)
    quad = lax.axis_index("yh")
    place = lax.axis_index(("yl", "xl"))
    xh, z, core = lax.axis_index("xh"), lax.axis_index("z"), lax.axis_index("c")
    span_len, feats = tokens.shape
    depth = key_weight.shape[0]
    half = feats // 2

    both = jnp.concatenate([key_weight, value_weight], axis=1).reshape(2, depth // 2, 2 * HD)
    spread = jnp.broadcast_to(both[None], (2, 2, depth // 2, 2 * HD)).reshape(4, depth // 2, 2 * HD)
    local_w = lax.all_to_all(spread, ("xl", "c"), 0, 0, tiled=True)
    all_w = lax.all_gather(local_w, ("yh", "yl"), axis=0, tiled=True).reshape(16, 2, depth // 2, 2 * HD)

    a0 = jnp.transpose(tokens)
    up = functools.partial(shifted, axis="z", size=8, by=1)
    down = functools.partial(shifted, axis="z", size=8, by=-1)
    r1u, r1d = up(a0), down(a0)
    b0 = shifted(a0, "xh", 2, 1)
    r2u, r2d = up(jnp.concatenate([r1u, b0], axis=0)), down(jnp.concatenate([b0, r1d], axis=0))
    r3u, r3d = up(r2u), down(r2d)
    r4u, r4d = up(r3u[half:]), down(r3d[: half + feats])
    r5u, r5d = up(r4u[feats:]), down(r4d[:half])
    early = row_sums([a0, b0, r1u, r1d, r2u, r2d, r3u, r3d])
    own_sums = row_sums([r4u, r4d, r5u, r5d], early)
    other_sums = shifted(own_sums, "c", 2, 1)

    mod_row = lax.dynamic_index_in_dim(modulation, levels[span_id], 0, keepdims=False)
    table = mod_row.reshape(2, 2, 8, 2, feats)
    table = lax.dynamic_index_in_dim(table, core, 3, keepdims=False)
    ring_z = (z - jnp.arange(8, dtype=jnp.int32)) % 8
    ring_x = jnp.stack([xh, 1 - xh])
    table = jnp.take(jnp.take(table, ring_x, axis=1), ring_z, axis=2)
    table = jnp.transpose(table, (0, 2, 1, 3)).reshape(2, 8, 2 * feats).astype(jnp.float32)
    index = jnp.concatenate(
        [xh * 8 + ring_z, (1 - xh) * 8 + ring_z, jnp.stack([core, 1 - core])]
    ).astype(jnp.int32)

    part_type = jax.ShapeDtypeStruct((span_len, 2 * HD), jnp.float32)
    normed, theirs = pl.pallas_call(
        norm_kernel,
        out_shape=(jax.ShapeDtypeStruct((span_len, 16 * feats), jnp.bfloat16), part_type),
        in_specs=[SMEM] + [VMEM] * 17,
        out_specs=(VMEM, VMEM),
        compiler_params=params(32),
    )(index, own_sums, other_sums, table[1], table[0], a0, b0, r1u, r2u, r3u, r4u, r5u, r1d, r2d, r3d, r4d, r5d, all_w)
    received = shifted(theirs, "c", 2, 1)
    mine = pl.pallas_call(
        keep_kernel,
        out_shape=part_type,
        in_specs=[SMEM, VMEM, VMEM],
        out_specs=VMEM,
        compiler_params=params(),
    )(index, normed, all_w)
    packed = pl.pallas_call(
        join_kernel,
        out_shape=jax.ShapeDtypeStruct((QUAD, 2 * span_len, HD), jnp.bfloat16),
        in_specs=[VMEM, VMEM],
        out_specs=VMEM,
        compiler_params=params(),
    )(mine, received)

    kv = lax.all_to_all(packed, ("yl", "xl"), 0, 0, tiled=True)
    q_all = lax.all_to_all(jnp.broadcast_to(queries[None], (QUAD, span_len, HD)), "yh", 0, 0, tiled=True)
    q_spans = jnp.arange(QUAD, dtype=jnp.int32) * QUAD + place
    k_spans = jnp.arange(QUAD, dtype=jnp.int32) + QUAD * quad
    seen = jnp.where(q_spans[:, None] == k_spans[None, :], 1, visible[q_spans][:, k_spans]).astype(jnp.int32)
    partial = pl.pallas_call(
        attend_kernel,
        out_shape=jax.ShapeDtypeStruct((QUAD, HD + STAT_ROWS, span_len), jnp.bfloat16),
        in_specs=[SMEM, SMEM, VMEM, VMEM],
        out_specs=VMEM,
        scratch_shapes=[
            pltpu.VMEM((HD, span_len), jnp.bfloat16),
            pltpu.VMEM((8, span_len), jnp.float32),
            pltpu.VMEM((8, span_len), jnp.float32),
            pltpu.VMEM((HD, span_len), jnp.float32),
        ],
        compiler_params=params(),
    )(seen, counts[k_spans], q_all, kv)
    parts = lax.all_to_all(partial, "yh", 0, 0, tiled=True)
    return pl.pallas_call(
        merge_kernel,
        out_shape=jax.ShapeDtypeStruct((span_len, HD), jnp.bfloat16),
        in_specs=[SMEM, VMEM],
        out_specs=VMEM,
        compiler_params=params(),
    )(lax.dynamic_slice_in_dim(counts, span_id, 1), parts)


def solution(mesh):
    fine = Mesh(mesh.devices.reshape(SIZES), SPAN_AXES + FSDP_AXES)
    spread = P(SPAN_AXES, FSDP_AXES)
    return jax.shard_map(
        on_device,
        mesh=fine,
        in_specs=(spread, spread, spread, spread, P(), P(), P(), P()),
        out_specs=spread,
        check_vma=False,
    )
```

time: 423 us -> 172 us (0.41)
  the two profiles are of different devices: /device:TPU:56 before, /device:TPU:8 now
where the time goes in v1:
time: 172 us; the launch traced here: 171 us
  starting transfers between devices  65.4 us (38%)
  waiting for transfers between devices  46.3 us (27%)
  Pallas kernels  16.9 us (10%)
  between operations  15.7 us (9%)
  local copies, waits for them, and re-layouts  14.7 us (9%)
  blocking collectives  10.5 us (6%)
    ppermute x13, starting transfers between devices, shifted(): lax.ppermute(value, axis, [(i, (i + by) % size) for i in range(size)])  50.8 us
    ppermute x13, waiting for transfers between devices, shifted(): lax.ppermute(value, axis, [(i, (i + by) % size) for i in range(size)])  18 us
    all_to_all x1, waiting for transfers between devices, on_device(): parts = lax.all_to_all(partial, 'yh', 0, 0, tiled=True)  16.6 us
    all_to_all x1, waiting for transfers between devices, on_device(): kv = lax.all_to_all(packed, ('yl', 'xl'), 0, 0, tiled=True)  11.6 us
    all_to_all x1, blocking collectives, on_device(): local_w = lax.all_to_all(spread, ('xl', 'c'), 0, 0, tiled=True)  10.5 us
    pallas_call x1, Pallas kernels, on_device(): pl.pallas_call(attend_kernel, out_shape=jax.ShapeDtypeStruct((QUAD, HD +...  9.7 us
    unnamed x23, local copies, waits for them, and re-layouts  6.67 us
    all_to_all x1, starting transfers between devices, on_device(): lax.all_to_all(jnp.broadcast_to(queries[None], (QUAD, span_len, HD)), 'yh...  6.21 us
  transfers between devices with their start and end apart: 17, of which 9 were waited for; matrix products, arithmetic and copies ran while one was open for 5% of the time, Pallas kernels for 3%

profile of v1, /device:TPU:8, one launch (start us, length us, event | category | flops | bytes accessed | tf_op | source)
XLA Modules:
  0.0 171.1 jit_solution(7022716869126300157)
XLA Ops:
  6.5 1.0 pad_maximum_fusion.2
  7.6 10.5 %all_to_all.20 = bf16[4,192,256]{2,1,0:T(8,128)(2,1)} all-to-all(bf16[4,192,256]{2,1,0:T(8,128)(2,1)S(1)} %bitcast.39), channel_id=1, replica_groups=mesh['yh'=4,'yl'=2,'xl'=2,'xh'=2,'z'=8,'c'=2] {'xl','c'}, dimensions={0} | all-to-all | bytes 786432 | tf_op jit(solution)/shard_map/all_to_all | solution.py:197
  18.1 4.3 %collective-permute-start = (bf16[192,512]{1,0:T(8,128)(2,1)}, bf16[192,512]{1,0:T(8,128)(2,1)S(1)}, u32[]{:S(2)}, u32[]{:S(2)}) collective-permute-start(bf16[192,512]{1,0:T(8,128)(2,1)} %bitcast.34), channel_id=1, source_target_pairs={{0,2},{2,4},{4,6},{6,8},{8,10},{10,12},{12,14},{14,0},{1,3},{3,5},... | collective-permute-start | bytes 589832 | tf_op jit(solution)/shard_map/ppermute | solution.py:29
  22.4 4.9 %collective-permute-start.1 = (bf16[192,512]{1,0:T(8,128)(2,1)}, bf16[192,512]{1,0:T(8,128)(2,1)S(1)}, u32[]{:S(2)}, u32[]{:S(2)}) collective-permute-start(bf16[192,512]{1,0:T(8,128)(2,1)} %bitcast.35), channel_id=1, source_target_pairs={{0,16},{16,0},{1,17},{17,1},{2,18},{18,2},{3,19},{19,3},{4,20},{20... | collective-permute-start | bytes 589832 | tf_op jit(solution)/shard_map/ppermute | solution.py:29
  27.4 8.6 %collective-permute-start.5 = (bf16[192,512]{1,0:T(8,128)(2,1)}, bf16[192,512]{1,0:T(8,128)(2,1)S(1)}, u32[]{:S(2)}, u32[]{:S(2)}) collective-permute-start(bf16[192,512]{1,0:T(8,128)(2,1)} %bitcast.36), channel_id=1, source_target_pairs={{0,14},{2,0},{4,2},{6,4},{8,6},{10,8},{12,10},{14,12},{1,15},{3,1}... | collective-permute-start | bytes 589832 | tf_op jit(solution)/shard_map/ppermute | solution.py:29
  36.0 1.8 %broadcast_in_dim.41 = bf16[4,512,128]{2,1,0:T(8,128)(2,1)} broadcast(bf16[512,128]{1,0:T(8,128)(2,1)} %param.9), dimensions={1,2} | broadcast | bytes 655360 | tf_op jit(solution)/shard_map/broadcast_in_dim | solution.py:249
  37.7 6.2 %all-to-all-start = ((bf16[4,512,128]{2,1,0:T(8,128)(2,1)}), bf16[4,512,128]{2,1,0:T(8,128)(2,1)S(1)}, u32[]{:S(2)}, u32[]{:S(2)}) async-start(bf16[4,512,128]{2,1,0:T(8,128)(2,1)} %broadcast_in_dim.41), calls=%async_computation | async-start | bytes 1048576 | tf_op jit(solution)/shard_map/all_to_all | solution.py:249
  43.9 0.6 dynamic_slice.15
  46.8 1.9 %collective-permute-start.2 = (bf16[384,512]{1,0:T(8,128)(2,1)S(1)}, bf16[384,512]{1,0:T(8,128)(2,1)S(1)}, u32[]{:S(2)}, u32[]{:S(2)}) collective-permute-start(bf16[384,512]{1,0:T(8,128)(2,1)S(1)} %get-tuple-element.10), channel_id=1, source_target_pairs={{0,2},{2,4},{4,6},{6,8},{8,10},{10,12},{12,14},{14,0},{1,3},{3,5},... | collective-permute-start | bytes 1179656 | tf_op jit(solution)/shard_map/ppermute | solution.py:29
  48.8 5.1 %collective-permute-start.6 = (bf16[384,512]{1,0:T(8,128)(2,1)S(1)}, bf16[384,512]{1,0:T(8,128)(2,1)S(1)}, u32[]{:S(2)}, u32[]{:S(2)}) collective-permute-start(bf16[384,512]{1,0:T(8,128)(2,1)S(1)} %get-tuple-element.9), channel_id=1, source_target_pairs={{0,14},{2,0},{4,2},{6,4},{8,6},{10,8},{12,10},{14,12},{1,15},{3,1}... | collective-permute-start | bytes 1179656 | tf_op jit(solution)/shard_map/ppermute | solution.py:29
  54.1 0.5 gather_fusion.3
  54.7 4.9 %collective-permute-done.2.refs_4_.r2u = bf16[384,512]{1,0:T(8,128)(2,1)S(1)} collective-permute-done((bf16[384,512]{1,0:T(8,128)(2,1)S(1)}, bf16[384,512]{1,0:T(8,128)(2,1)S(1)}, u32[]{:S(2)}, u32[]{:S(2)}) %collective-permute-start.2) | collective-permute-done | bytes 393248 | tf_op jit(solution)/shard_map/ppermute | solution.py:29
  59.6 1.9 %collective-permute-start.3 = (bf16[384,512]{1,0:T(8,128)(2,1)S(1)}, bf16[384,512]{1,0:T(8,128)(2,1)S(1)}, u32[]{:S(2)}, u32[]{:S(2)}) collective-permute-start(bf16[384,512]{1,0:T(8,128)(2,1)S(1)} %collective-permute-done.2.refs_4_.r2u), channel_id=1, source_target_pairs={{0,2},{2,4},{4,6},{6,8},{8,10},{10,12},{12,14},{14,0},{1,3},{3,5},... | collective-permute-start | bytes 1179656 | tf_op jit(solution)/shard_map/ppermute | solution.py:29
  61.5 5.1 %collective-permute-start.7 = (bf16[384,512]{1,0:T(8,128)(2,1)S(1)}, bf16[384,512]{1,0:T(8,128)(2,1)S(1)}, u32[]{:S(2)}, u32[]{:S(2)}) collective-permute-start(bf16[384,512]{1,0:T(8,128)(2,1)S(1)} %collective-permute-done.6.refs_5_.r2d), channel_id=1, source_target_pairs={{0,14},{2,0},{4,2},{6,4},{8,6},{10,8},{12,10},{14,12},{1,15},{3,1}... | collective-permute-start | bytes 1179656 | tf_op jit(solution)/shard_map/ppermute | solution.py:29
  66.8 0.6 gather_fusion.4
  67.4 5.2 %collective-permute-done.7.refs_7_.r3d = bf16[384,512]{1,0:T(8,128)(2,1)S(1)} collective-permute-done((bf16[384,512]{1,0:T(8,128)(2,1)S(1)}, bf16[384,512]{1,0:T(8,128)(2,1)S(1)}, u32[]{:S(2)}, u32[]{:S(2)}) %collective-permute-start.7) | collective-permute-done | bytes 393248 | tf_op jit(solution)/shard_map/ppermute | solution.py:29
  72.6 0.7 slice.37
  73.3 5.6 %collective-permute-start.8 = (bf16[288,512]{1,0:T(8,128)(2,1)}, bf16[288,512]{1,0:T(8,128)(2,1)S(1)}, u32[]{:S(2)}, u32[]{:S(2)}) collective-permute-start(bf16[288,512]{1,0:T(8,128)(2,1)} %slice.37), channel_id=1, source_target_pairs={{0,14},{2,0},{4,2},{6,4},{8,6},{10,8},{12,10},{14,12},{1,15},{3,1}... | collective-permute-start | bytes 884744 | tf_op jit(solution)/shard_map/ppermute | solution.py:29
  78.9 0.7 slice.36
  79.7 1.9 %collective-permute-start.4 = (bf16[288,512]{1,0:T(8,128)(2,1)}, bf16[288,512]{1,0:T(8,128)(2,1)S(1)}, u32[]{:S(2)}, u32[]{:S(2)}) collective-permute-start(bf16[288,512]{1,0:T(8,128)(2,1)} %slice.36), channel_id=1, source_target_pairs={{0,2},{2,4},{4,6},{6,8},{8,10},{10,12},{12,14},{14,0},{1,3},{3,5},... | collective-permute-start | bytes 884744 | tf_op jit(solution)/shard_map/ppermute | solution.py:29
  81.7 1.8 %collective-permute-done.8.refs_1_.r4d = bf16[288,512]{1,0:T(8,128)(2,1)S(1)} collective-permute-done((bf16[288,512]{1,0:T(8,128)(2,1)}, bf16[288,512]{1,0:T(8,128)(2,1)S(1)}, u32[]{:S(2)}, u32[]{:S(2)}) %collective-permute-start.8) | collective-permute-done | bytes 294944 | tf_op jit(solution)/shard_map/ppermute | solution.py:29
  83.4 5.5 %collective-permute-start.10 = (bf16[96,512]{1,0:T(8,128)(2,1)S(1)}, bf16[96,512]{1,0:T(8,128)(2,1)S(1)}, u32[]{:S(2)}, u32[]{:S(2)}) collective-permute-start(bf16[96,512]{1,0:T(8,128)(2,1)S(1)} %slice.39), channel_id=1, source_target_pairs={{0,14},{2,0},{4,2},{6,4},{8,6},{10,8},{12,10},{14,12},{1,15},{3,1}... | collective-permute-start | bytes 294920 | tf_op jit(solution)/shard_map/ppermute | solution.py:29
  88.9 0.7 collective-permute-done.4.refs_0_.r4u
  89.7 1.9 %collective-permute-start.9 = (bf16[96,512]{1,0:T(8,128)(2,1)S(1)}, bf16[96,512]{1,0:T(8,128)(2,1)S(1)}, u32[]{:S(2)}, u32[]{:S(2)}) collective-permute-start(bf16[96,512]{1,0:T(8,128)(2,1)S(1)} %slice.38), channel_id=1, source_target_pairs={{0,2},{2,4},{4,6},{6,8},{8,10},{10,12},{12,14},{14,0},{1,3},{3,5},... | collective-permute-start | bytes 294920 | tf_op jit(solution)/shard_map/ppermute | solution.py:29
  91.7 0.9 copy-done.2
  93.0 4.4 %collective-permute-done.9.refs_2_.r5u = bf16[96,512]{1,0:T(8,128)(2,1)S(1)} collective-permute-done((bf16[96,512]{1,0:T(8,128)(2,1)S(1)}, bf16[96,512]{1,0:T(8,128)(2,1)S(1)}, u32[]{:S(2)}, u32[]{:S(2)}) %collective-permute-start.9) | collective-permute-done | bytes 98336 | tf_op jit(solution)/shard_map/ppermute | solution.py:29
  97.6 0.5 copy-done.6
  98.1 0.6 copy-done.4
  98.7 1.9 %collective-permute-start.11 = (f32[8,512]{1,0:T(8,128)S(1)}, f32[8,512]{1,0:T(8,128)S(1)}, u32[]{:S(2)}, u32[]{:S(2)}) collective-permute-start(f32[8,512]{1,0:T(8,128)S(1)} %shard_map.83.own_ref), channel_id=1, source_target_pairs={{0,1},{1,0},{2,3},{3,2},{4,5},{5,4},{6,7},{7,6},{8,9},{9,8},{10,11... | collective-permute-start | bytes 49160 | tf_op jit(solution)/shard_map/ppermute | solution.py:29
  100.9 0.9 collective-permute-done.11.other_ref
  101.8 1.9 %copy-done.1 = bf16[32,192,256]{2,1,0:T(8,128)(2,1)S(1)} copy-done((bf16[32,192,256]{2,1,0:T(8,128)(2,1)S(1)}, bf16[32,192,256]{2,1,0:T(8,128)(2,1)}, u32[]{:S(2)}) %copy-start.1) | copy-done | bytes 3145752
  103.7 0.9 copy-done.3
  104.6 0.9 copy-done.5
  105.5 0.9 copy-done.7
  106.4 2.5 %shard_map.84 = (bf16[512,3072]{1,0:T(8,128)(2,1)S(1)}, f32[512,256]{1,0:T(8,128)S(1)}) custom-call(s32[18]{0:T(128)S(1)} %pad_add_fusion.index_ref, f32[8,512]{1,0:T(8,128)S(1)} %shard_map.83.own_ref, f32[8,512]{1,0:T(8,128)S(1)} %collective-permute-done.11.other_ref, f32[8,384]{1,0:T(8,128)S(1)} %squeeze.17.scale_ref, f32[8,384]{1,0:T(8,128)S(1)} %squeeze.18.shift_ref, ...), custom_call_target="tpu_custom_call" | custom-call | tf_op jit(solution)/shard_map/pallas_call | solution.py:225
  108.9 2.1 %collective-permute-start.12 = (f32[512,256]{1,0:T(8,128)S(1)}, f32[512,256]{1,0:T(8,128)S(1)}, u32[]{:S(2)}, u32[]{:S(2)}) collective-permute-start(f32[512,256]{1,0:T(8,128)S(1)} %get-tuple-element.8), channel_id=1, source_target_pairs={{0,1},{1,0},{2,3},{3,2},{4,5},{5,4},{6,7},{7,6},{8,9},{9,8},{10,11... | collective-permute-start | bytes 1572872 | tf_op jit(solution)/shard_map/ppermute | solution.py:29
  110.9 1.5 shard_map.85.mine_ref
  112.7 1.1 shard_map.86
  113.8 4.9 %all-to-all-start.2 = ((bf16[4,1024,128]{2,1,0:T(8,128)(2,1)}), bf16[4,1024,128]{2,1,0:T(8,128)(2,1)S(1)}, u32[]{:S(2)}, u32[]{:S(2)}) async-start(bf16[4,1024,128]{2,1,0:T(8,128)(2,1)} %shard_map.86), calls=%async_computation.2 | async-start | bytes 2097152 | tf_op jit(solution)/shard_map/all_to_all | solution.py:248
  118.8 0.6 gather_fusion
  119.4 0.6 gather_fusion.1
  120.1 0.6 gather_fusion.2
  120.8 11.6 %all-to-all-done.2.kv_ref = bf16[4,1024,128]{2,1,0:T(8,128)(2,1)S(1)} async-done(((bf16[4,1024,128]{2,1,0:T(8,128)(2,1)}), bf16[4,1024,128]{2,1,0:T(8,128)(2,1)S(1)}, u32[]{:S(2)}, u32[]{:S(2)}) %all-to-all-start.2) | async-done | bytes 1048608 | tf_op jit(solution)/shard_map/all_to_all | solution.py:248
  132.4 9.7 %shard_map.87 = bf16[4,144,512]{2,1,0:T(8,128)(2,1)} custom-call(s32[4,4]{1,0:T(4,128)S(1)} %bitcast_select_fusion.seen_ref, s32[4]{0:T(128)S(1)} %gather_fusion.2, bf16[4,512,128]{2,1,0:T(8,128)(2,1)S(1)} %all-to-all-done.q_ref, bf16[4,1024,128]{2,1,0:T(8,128)(2,1)S(1)} %all-to-all-done.2.kv_ref), custom_call_target="tpu_custom_call" | custom-call | tf_op jit(solution)/shard_map/pallas_call | solution.py:253
  142.1 3.5 %all-to-all-start.3 = ((bf16[4,144,512]{2,1,0:T(8,128)(2,1)}), bf16[4,144,512]{2,1,0:T(8,128)(2,1)S(1)}, u32[]{:S(2)}, u32[]{:S(2)}) async-start(bf16[4,144,512]{2,1,0:T(8,128)(2,1)} %shard_map.87), calls=%async_computation.3 | async-start | bytes 1179648 | tf_op jit(solution)/shard_map/all_to_all | solution.py:266
  145.6 0.6 dynamic_slice.14.live_ref
  146.2 16.6 %all-to-all-done.3.part_ref = bf16[4,144,512]{2,1,0:T(8,128)(2,1)S(1)} async-done(((bf16[4,144,512]{2,1,0:T(8,128)(2,1)}), bf16[4,144,512]{2,1,0:T(8,128)(2,1)S(1)}, u32[]{:S(2)}, u32[]{:S(2)}) %all-to-all-start.3) | async-done | bytes 589856 | tf_op jit(solution)/shard_map/all_to_all | solution.py:266
  162.8 1.5 shard_map.88
  (57 shorter events, 2.2 us)
Async XLA Ops:
  6.5 39.9 %copy-start = (bf16[8,12288]{1,0:T(8,128)(2,1)S(1)}, bf16[8,12288]{1,0:T(8,128)(2,1)}, u32[]{:S(2)}) copy-start(bf16[8,12288]{1,0:T(8,128)(2,1)} %param.12) | copy-start | bytes 589828
  6.5 37.4 %copy-start.10 = (s32[16]{0:T(128)S(1)}, s32[16]{0:T(128)}, u32[]{:S(2)}) copy-start(s32[16]{0:T(128)} %param.13) | copy-start | bytes 196
  6.5 95.2 %all-gather.2.cloned.1.call-start = ((), (), s32[]{:S(2)}) async-start(), calls=%async_computation.4 | async-start | bytes 3538944 | tf_op jit(solution)/shard_map/all_gather | solution.py:198
  18.1 28.6 %collective-permute-start = (bf16[192,512]{1,0:T(8,128)(2,1)}, bf16[192,512]{1,0:T(8,128)(2,1)S(1)}, u32[]{:S(2)}, u32[]{:S(2)}) collective-permute-start(bf16[192,512]{1,0:T(8,128)(2,1)} %bitcast.34), channel_id=1, source_target_pairs={{0,2},{2,4},{4,6},{6,8},{8,10},{10,12},{12,14},{14,0},{1,3},{3,5},... | collective-permute-start | bytes 589832 | tf_op jit(solution)/shard_map/ppermute | solution.py:29
  22.4 24.3 %collective-permute-start.1 = (bf16[192,512]{1,0:T(8,128)(2,1)}, bf16[192,512]{1,0:T(8,128)(2,1)S(1)}, u32[]{:S(2)}, u32[]{:S(2)}) collective-permute-start(bf16[192,512]{1,0:T(8,128)(2,1)} %bitcast.35), channel_id=1, source_target_pairs={{0,16},{16,0},{1,17},{17,1},{2,18},{18,2},{3,19},{19,3},{4,20},{20... | collective-permute-start | bytes 589832 | tf_op jit(solution)/shard_map/ppermute | solution.py:29
  27.4 19.4 %collective-permute-start.5 = (bf16[192,512]{1,0:T(8,128)(2,1)}, bf16[192,512]{1,0:T(8,128)(2,1)S(1)}, u32[]{:S(2)}, u32[]{:S(2)}) collective-permute-start(bf16[192,512]{1,0:T(8,128)(2,1)} %bitcast.36), channel_id=1, source_target_pairs={{0,14},{2,0},{4,2},{6,4},{8,6},{10,8},{12,10},{14,12},{1,15},{3,1}... | collective-permute-start | bytes 589832 | tf_op jit(solution)/shard_map/ppermute | solution.py:29
  37.7 76.1 %all-to-all-start = ((bf16[4,512,128]{2,1,0:T(8,128)(2,1)}), bf16[4,512,128]{2,1,0:T(8,128)(2,1)S(1)}, u32[]{:S(2)}, u32[]{:S(2)}) async-start(bf16[4,512,128]{2,1,0:T(8,128)(2,1)} %broadcast_in_dim.41), calls=%async_computation | async-start | bytes 1048576 | tf_op jit(solution)/shard_map/all_to_all | solution.py:249
  46.8 12.7 %collective-permute-start.2 = (bf16[384,512]{1,0:T(8,128)(2,1)S(1)}, bf16[384,512]{1,0:T(8,128)(2,1)S(1)}, u32[]{:S(2)}, u32[]{:S(2)}) collective-permute-start(bf16[384,512]{1,0:T(8,128)(2,1)S(1)} %get-tuple-element.10), channel_id=1, source_target_pairs={{0,2},{2,4},{4,6},{6,8},{8,10},{10,12},{12,14},{14,0},{1,3},{3,5},... | collective-permute-start | bytes 1179656 | tf_op jit(solution)/shard_map/ppermute | solution.py:29
  48.8 12.7 %collective-permute-start.6 = (bf16[384,512]{1,0:T(8,128)(2,1)S(1)}, bf16[384,512]{1,0:T(8,128)(2,1)S(1)}, u32[]{:S(2)}, u32[]{:S(2)}) collective-permute-start(bf16[384,512]{1,0:T(8,128)(2,1)S(1)} %get-tuple-element.9), channel_id=1, source_target_pairs={{0,14},{2,0},{4,2},{6,4},{8,6},{10,8},{12,10},{14,12},{1,15},{3,1}... | collective-permute-start | bytes 1179656 | tf_op jit(solution)/shard_map/ppermute | solution.py:29
  59.6 19.3 %collective-permute-start.3 = (bf16[384,512]{1,0:T(8,128)(2,1)S(1)}, bf16[384,512]{1,0:T(8,128)(2,1)S(1)}, u32[]{:S(2)}, u32[]{:S(2)}) collective-permute-start(bf16[384,512]{1,0:T(8,128)(2,1)S(1)} %collective-permute-done.2.refs_4_.r2u), channel_id=1, source_target_pairs={{0,2},{2,4},{4,6},{6,8},{8,10},{10,12},{12,14},{14,0},{1,3},{3,5},... | collective-permute-start | bytes 1179656 | tf_op jit(solution)/shard_map/ppermute | solution.py:29
  61.5 11.1 %collective-permute-start.7 = (bf16[384,512]{1,0:T(8,128)(2,1)S(1)}, bf16[384,512]{1,0:T(8,128)(2,1)S(1)}, u32[]{:S(2)}, u32[]{:S(2)}) collective-permute-start(bf16[384,512]{1,0:T(8,128)(2,1)S(1)} %collective-permute-done.6.refs_5_.r2d), channel_id=1, source_target_pairs={{0,14},{2,0},{4,2},{6,4},{8,6},{10,8},{12,10},{14,12},{1,15},{3,1}... | collective-permute-start | bytes 1179656 | tf_op jit(solution)/shard_map/ppermute | solution.py:29
  73.3 10.1 %collective-permute-start.8 = (bf16[288,512]{1,0:T(8,128)(2,1)}, bf16[288,512]{1,0:T(8,128)(2,1)S(1)}, u32[]{:S(2)}, u32[]{:S(2)}) collective-permute-start(bf16[288,512]{1,0:T(8,128)(2,1)} %slice.37), channel_id=1, source_target_pairs={{0,14},{2,0},{4,2},{6,4},{8,6},{10,8},{12,10},{14,12},{1,15},{3,1}... | collective-permute-start | bytes 884744 | tf_op jit(solution)/shard_map/ppermute | solution.py:29
  79.7 10.0 %collective-permute-start.4 = (bf16[288,512]{1,0:T(8,128)(2,1)}, bf16[288,512]{1,0:T(8,128)(2,1)S(1)}, u32[]{:S(2)}, u32[]{:S(2)}) collective-permute-start(bf16[288,512]{1,0:T(8,128)(2,1)} %slice.36), channel_id=1, source_target_pairs={{0,2},{2,4},{4,6},{6,8},{8,10},{10,12},{12,14},{14,0},{1,3},{3,5},... | collective-permute-start | bytes 884744 | tf_op jit(solution)/shard_map/ppermute | solution.py:29
  83.4 9.6 %collective-permute-start.10 = (bf16[96,512]{1,0:T(8,128)(2,1)S(1)}, bf16[96,512]{1,0:T(8,128)(2,1)S(1)}, u32[]{:S(2)}, u32[]{:S(2)}) collective-permute-start(bf16[96,512]{1,0:T(8,128)(2,1)S(1)} %slice.39), channel_id=1, source_target_pairs={{0,14},{2,0},{4,2},{6,4},{8,6},{10,8},{12,10},{14,12},{1,15},{3,1}... | collective-permute-start | bytes 294920 | tf_op jit(solution)/shard_map/ppermute | solution.py:29
  89.7 7.7 %collective-permute-start.9 = (bf16[96,512]{1,0:T(8,128)(2,1)S(1)}, bf16[96,512]{1,0:T(8,128)(2,1)S(1)}, u32[]{:S(2)}, u32[]{:S(2)}) collective-permute-start(bf16[96,512]{1,0:T(8,128)(2,1)S(1)} %slice.38), channel_id=1, source_target_pairs={{0,2},{2,4},{4,6},{6,8},{8,10},{10,12},{12,14},{14,0},{1,3},{3,5},... | collective-permute-start | bytes 294920 | tf_op jit(solution)/shard_map/ppermute | solution.py:29
  91.6 0.9 copy-start.2
  97.4 0.6 copy-start.6
  98.1 0.7 copy-start.4
  98.7 3.1 %collective-permute-start.11 = (f32[8,512]{1,0:T(8,128)S(1)}, f32[8,512]{1,0:T(8,128)S(1)}, u32[]{:S(2)}, u32[]{:S(2)}) collective-permute-start(f32[8,512]{1,0:T(8,128)S(1)} %shard_map.83.own_ref), channel_id=1, source_target_pairs={{0,1},{1,0},{2,3},{3,2},{4,5},{5,4},{6,7},{7,6},{8,9},{9,8},{10,11... | collective-permute-start | bytes 49160 | tf_op jit(solution)/shard_map/ppermute | solution.py:29
  101.8 1.9 %copy-start.1 = (bf16[32,192,256]{2,1,0:T(8,128)(2,1)S(1)}, bf16[32,192,256]{2,1,0:T(8,128)(2,1)}, u32[]{:S(2)}) copy-start(bf16[32,192,256]{2,1,0:T(8,128)(2,1)} %all-gather.2.cloned.1.call-done) | copy-start | bytes 9437188
  103.7 0.9 copy-start.3
  104.6 0.9 copy-start.5
  105.5 0.9 copy-start.7
  108.9 3.8 %collective-permute-start.12 = (f32[512,256]{1,0:T(8,128)S(1)}, f32[512,256]{1,0:T(8,128)S(1)}, u32[]{:S(2)}, u32[]{:S(2)}) collective-permute-start(f32[512,256]{1,0:T(8,128)S(1)} %get-tuple-element.8), channel_id=1, source_target_pairs={{0,1},{1,0},{2,3},{3,2},{4,5},{5,4},{6,7},{7,6},{8,9},{9,8},{10,11... | collective-permute-start | bytes 1572872 | tf_op jit(solution)/shard_map/ppermute | solution.py:29
  112.5 6.3 %copy-start.9 = (s32[16,16]{1,0:T(8,128)S(1)}, s32[16,16]{1,0:T(8,128)}, u32[]{:S(2)}) copy-start(s32[16,16]{1,0:T(8,128)} %param.14) | copy-start | bytes 3076
  112.5 7.6 %copy-start.8 = (s32[16]{0:T(128)S(1)}, s32[16]{0:T(128)}, u32[]{:S(2)}) copy-start(s32[16]{0:T(128)} %param.15) | copy-start | bytes 196
  113.8 18.6 %all-to-all-start.2 = ((bf16[4,1024,128]{2,1,0:T(8,128)(2,1)}), bf16[4,1024,128]{2,1,0:T(8,128)(2,1)S(1)}, u32[]{:S(2)}, u32[]{:S(2)}) async-start(bf16[4,1024,128]{2,1,0:T(8,128)(2,1)} %shard_map.86), calls=%async_computation.2 | async-start | bytes 2097152 | tf_op jit(solution)/shard_map/all_to_all | solution.py:248
  142.1 20.7 %all-to-all-start.3 = ((bf16[4,144,512]{2,1,0:T(8,128)(2,1)}), bf16[4,144,512]{2,1,0:T(8,128)(2,1)S(1)}, u32[]{:S(2)}, u32[]{:S(2)}) async-start(bf16[4,144,512]{2,1,0:T(8,128)(2,1)} %shard_map.87), calls=%async_computation.3 | async-start | bytes 1179648 | tf_op jit(solution)/shard_map/all_to_all | solution.py:266
Sparse Core Ops, SparseCore 0:
  18.3 63.0 all-gather.1

commit v2 on v1

v2 whole, which is shorter than its diff:
```python
import functools

import jax
import jax.numpy as jnp
from jax import lax
from jax.experimental import pallas as pl
from jax.experimental.pallas import tpu as pltpu
from jax.sharding import Mesh, PartitionSpec as P

HD = 128
EPSILON = 1e-06
NEG_BIG = -1e30
LOG2E = 1.4426950408889634
SPAN_AXES = ("yh", "yl", "xl")
FSDP_AXES = ("xh", "z", "c")
SIZES = (4, 2, 2, 2, 8, 2)
QUAD = 4
RING = 8
STAT_ROWS = 16
SPAN, YH, PLACE, Y, XL, XH, Z, CORE, LEVEL = range(9)

VMEM = pl.BlockSpec(memory_space=pltpu.VMEM)
SMEM = pl.BlockSpec(memory_space=pltpu.SMEM)
ANY = pl.BlockSpec(memory_space=pl.ANY)


def params(mib=24):
    return pltpu.CompilerParams(vmem_limit_bytes=mib * 1024 * 1024)


def shifted(value, axis, size, by):
    return lax.ppermute(value, axis, [(i, (i + by) % size) for i in range(size)])


def moved(value, by):
    return lax.ppermute(value, "yh", [(i, i + by) for i in range(QUAD) if 0 <= i + by < QUAD])


def fetch(refs, held, sems):
    copies = [pltpu.make_async_copy(ref, held.at[k], sems.at[k]) for k, ref in enumerate(refs)]
    for copy in copies:
        copy.start()
    return copies


def split_kernel(ids_ref, key_ref, value_ref, own_ref, other_ref):
    rows = own_ref.shape[0]
    for part, out in ((ids_ref[CORE], own_ref), (1 - ids_ref[CORE], other_ref)):
        first = pl.multiple_of(part * rows, 16)
        out[:, 0:HD] = key_ref[pl.ds(first, rows), :]
        out[:, HD : 2 * HD] = value_ref[pl.ds(first, rows), :]


def sums_kernel(count, has_earlier, *refs):
    pieces = refs[:count]
    out, held, sems = refs[-3], refs[-2], refs[-1]
    copies = fetch(pieces, held, sems)
    total = jnp.zeros((1, out.shape[1]), jnp.float32)
    square = jnp.zeros((1, out.shape[1]), jnp.float32)
    for k, copy in enumerate(copies):
        copy.wait()
        block = held[k].astype(jnp.float32)
        total += jnp.sum(block, axis=0, keepdims=True)
        square += jnp.sum(block * block, axis=0, keepdims=True)
    if has_earlier:
        total += refs[count][0:1, :]
        square += refs[count][1:2, :]
    out[...] = jnp.zeros_like(out)
    out[0:1, :] = total
    out[1:2, :] = square


def row_sums(pieces, earlier=None):
    rest = () if earlier is None else (earlier,)
    rows, width = pieces[0].shape
    return pl.pallas_call(
        functools.partial(sums_kernel, len(pieces), bool(rest)),
        out_shape=jax.ShapeDtypeStruct((8, width), jnp.float32),
        in_specs=[ANY] * len(pieces) + [VMEM] * len(rest),
        out_specs=VMEM,
        scratch_shapes=[
            pltpu.VMEM((len(pieces), rows, width), pieces[0].dtype),
            pltpu.SemaphoreType.DMA((len(pieces),)),
        ],
        compiler_params=params(),
    )(*pieces, *rest)


def norm_kernel(ids_ref, own_ref, other_ref, table_ref, *refs):
    pieces = refs[:RING]
    normed_ref, held, sems = refs[RING:]
    copies = fetch(pieces, held, sems)
    feats = held.shape[1] // 2
    model_width = 4.0 * RING * feats
    stats = own_ref[...] + other_ref[...]
    mean = stats[0:1, :] / model_width
    variance = stats[1:2, :] / model_width - mean * mean
    rstd = lax.rsqrt(variance + EPSILON)
    columns = jnp.transpose(jnp.concatenate([mean, rstd, jnp.zeros((6, mean.shape[1]), jnp.float32)], axis=0))
    mean_col, rstd_col = columns[:, 0:1], columns[:, 1:2]
    blocks = table_ref.shape[0] // 2
    for slot, copy in enumerate(copies):
        copy.wait()
        for part in range(2):
            x_at = jnp.where(part == 0, ids_ref[XH], 1 - ids_ref[XH])
            z_at = lax.rem(ids_ref[Z] + slot, RING)
            row = x_at * (2 * RING) + z_at * 2 + ids_ref[CORE]
            shift = table_ref[pl.ds(row, 1), :]
            scale = table_ref[pl.ds(blocks + row, 1), :]
            block = jnp.transpose(held[slot, part * feats : (part + 1) * feats, :]).astype(jnp.float32)
            block = (block - mean_col) * rstd_col * (1.0 + scale) + shift
            normed_ref[slot, part] = block.astype(jnp.bfloat16)


def add_products(ids_ref, normed_ref, weights, slot, parts):
    y_at = lax.rem(ids_ref[Y] + slot, RING)
    half = y_at // (RING // 2)
    part = jnp.where(half == ids_ref[XH], 0, 1)
    for head in range(2):
        for side in range(2):
            xl_at = ids_ref[XL] if side == 0 else 1 - ids_ref[XL]
            z_at = 2 * (y_at - half * (RING // 2)) + xl_at
            place = lax.rem(z_at + RING - ids_ref[Z], RING)
            product = jnp.dot(normed_ref[place, part], weights[2 * side + head], preferred_element_type=jnp.float32)
            parts[head] = product if parts[head] is None else parts[head] + product


def project_kernel(slots, has_earlier, ids_ref, normed_ref, *refs):
    pieces = refs[: len(slots)]
    out_keep, out_send, held, sems = refs[-4:]
    copies = fetch(pieces, held, sems)
    if has_earlier:
        parts = [refs[len(slots)][...], refs[len(slots) + 1][...]]
    else:
        parts = [None, None]
    for k, slot in enumerate(slots):
        copies[k].wait()
        add_products(ids_ref, normed_ref, held.at[k], slot, parts)
    out_keep[...] = parts[0]
    out_send[...] = parts[1]


def project(ids, normed, slots, pieces, earlier=()):
    part = jax.ShapeDtypeStruct((normed.shape[2], 2 * HD), jnp.float32)
    return pl.pallas_call(
        functools.partial(project_kernel, slots, bool(earlier)),
        out_shape=(part, part),
        in_specs=[SMEM, VMEM] + [ANY] * len(pieces) + [VMEM] * len(earlier),
        out_specs=(VMEM, VMEM),
        scratch_shapes=[
            pltpu.VMEM((len(pieces),) + pieces[0].shape, pieces[0].dtype),
            pltpu.SemaphoreType.DMA((len(pieces),)),
        ],
        compiler_params=params(),
    )(ids, normed, *pieces, *earlier)


def join_kernel(mine_ref, theirs_ref, out_ref):
    rows = mine_ref.shape[0]
    total = (mine_ref[...] + theirs_ref[...]).astype(jnp.bfloat16)
    out_ref[0:rows, :] = total[:, 0:HD]
    for b in range(rows // HD):
        out_ref[rows + b * HD : rows + (b + 1) * HD, :] = jnp.transpose(
            total[b * HD : (b + 1) * HD, HD : 2 * HD]
        )


def attend_kernel(later, ids_ref, visible_ref, counts_ref, q_ref, kv0, kv1, kv2, kv3, out_ref, q_t, stat, acc):
    span_len = q_ref.shape[0]
    factor = LOG2E * HD ** (-0.5)
    quad = ids_ref[YH]

    @pl.when(quad + later < QUAD)
    def _():
        q_span = (quad + later) * QUAD + ids_ref[PLACE]
        q_t[...] = jnp.transpose(q_ref[...])
        stat[0:1, :] = jnp.full((1, span_len), NEG_BIG, jnp.float32)
        stat[8:9, :] = jnp.zeros((1, span_len), jnp.float32)
        acc[...] = jnp.zeros_like(acc)
        for flip, kv_ref in enumerate((kv0, kv1, kv2, kv3)):
            k_span = quad * QUAD + (ids_ref[PLACE] ^ flip)
            seen = visible_ref[q_span, k_span] == 1
            if later == 0:
                seen = (k_span == q_span) if flip == 0 else jnp.logical_and(seen, k_span < q_span)

            @pl.when(seen)
            def _():
                scores = jnp.dot(kv_ref[0:span_len, :], q_t[...], preferred_element_type=jnp.float32)
                live = lax.broadcasted_iota(jnp.int32, scores.shape, 0) < counts_ref[k_span]
                scores = jnp.where(live, scores * factor, NEG_BIG)
                best = stat[0:1, :]
                top = jnp.maximum(best, jnp.max(scores, axis=0, keepdims=True))
                weights = jnp.exp2(scores - top)
                fading = jnp.exp2(best - top)
                stat[8:9, :] = stat[8:9, :] * fading + jnp.sum(weights, axis=0, keepdims=True)
                stat[0:1, :] = top
                values = jnp.concatenate(
                    [kv_ref[span_len + b * HD : span_len + (b + 1) * HD, :] for b in range(span_len // HD)],
                    axis=1,
                )
                acc[...] = acc[...] * fading + jnp.dot(
                    values, weights.astype(jnp.bfloat16), preferred_element_type=jnp.float32
                )

        out_ref[0:HD, :] = acc[...].astype(jnp.bfloat16)
        rows = []
        for value in (stat[0:1, :], stat[8:9, :]):
            for _part in range(3):
                part = value.astype(jnp.bfloat16).astype(jnp.float32)
                rows.append(part)
                value = value - part
        rows.append(jnp.zeros((STAT_ROWS - 6, span_len), jnp.float32))
        out_ref[HD : HD + STAT_ROWS, :] = jnp.concatenate(rows, axis=0).astype(jnp.bfloat16)

    @pl.when(quad + later >= QUAD)
    def _():
        out_ref[...] = jnp.zeros_like(out_ref)


def attend(later, ids, visible, counts, q, kvs):
    span_len = q.shape[0]
    return pl.pallas_call(
        functools.partial(attend_kernel, later),
        out_shape=jax.ShapeDtypeStruct((HD + STAT_ROWS, span_len), jnp.bfloat16),
        in_specs=[SMEM] * 3 + [VMEM] * 5,
        out_specs=VMEM,
        scratch_shapes=[
            pltpu.VMEM((HD, span_len), jnp.bfloat16),
            pltpu.VMEM((16, span_len), jnp.float32),
            pltpu.VMEM((HD, span_len), jnp.float32),
        ],
        compiler_params=params(16),
    )(ids, visible, counts, q, *kvs)


def merge_kernel(ids_ref, counts_ref, part0, part1, part2, part3, out_ref):
    span_len = out_ref.shape[0]
    parts = (part0, part1, part2, part3)
    bests, totals = [], []
    for earlier, part in enumerate(parts):
        stat = part[HD : HD + STAT_ROWS, :].astype(jnp.float32)
        sent = ids_ref[YH] >= earlier
        bests.append(jnp.where(sent, (stat[0:1] + stat[1:2]) + stat[2:3], NEG_BIG))
        totals.append(jnp.where(sent, (stat[3:4] + stat[4:5]) + stat[5:6], 0.0))
    top = functools.reduce(jnp.maximum, bests)
    share = [jnp.exp2(b - top) for b in bests]
    total = sum(s * t for s, t in zip(share, totals))
    result = sum(s * part[0:HD, :].astype(jnp.float32) for s, part in zip(share, parts))
    slot = lax.broadcasted_iota(jnp.int32, total.shape, 1)
    result = jnp.where(slot < counts_ref[ids_ref[SPAN]], result / total, 0.0)
    out_ref[...] = jnp.transpose(result).astype(jnp.bfloat16)


def on_device(tokens, queries, key_weight, value_weight, modulation, levels, visible, counts):
    span_id = lax.axis_index(SPAN_AXES)
    ids = jnp.stack(
        [
            span_id,
            lax.axis_index("yh"),
            lax.axis_index(("yl", "xl")),
            lax.axis_index(("yh", "yl")),
            lax.axis_index("xl"),
            lax.axis_index("xh"),
            lax.axis_index("z"),
            lax.axis_index("c"),
        ]
    ).astype(jnp.int32)
    span_len, feats = tokens.shape
    depth = key_weight.shape[0] // 2

    w_type = jax.ShapeDtypeStruct((depth, 2 * HD), jnp.bfloat16)
    w_own, w_other = pl.pallas_call(
        split_kernel,
        out_shape=(w_type, w_type),
        in_specs=[SMEM, VMEM, VMEM],
        out_specs=(VMEM, VMEM),
        compiler_params=params(8),
    )(ids, key_weight, value_weight)
    w_chip = jnp.stack([w_own, shifted(w_other, "c", 2, 1)])
    w0 = jnp.concatenate([w_chip, shifted(w_chip, "xl", 2, 1)], axis=0)

    a0 = jnp.transpose(tokens)
    x0 = jnp.concatenate([a0, shifted(a0, "xh", 2, 1)], axis=0)

    x_up, x_down, w_up, w_down = [x0], [x0], [w0], [w0]
    y_axes = ("yh", "yl")
    for step in range(4):
        x_up.append(shifted(x_up[-1], "z", RING, 1))
        if step < 3:
            w_up.append(shifted(w_up[-1], y_axes, RING, 1))
            x_down.append(shifted(x_down[-1], "z", RING, -1))
        w_down.append(shifted(w_down[-1], y_axes, RING, -1))
    x_slots = [x0, x_down[1], x_down[2], x_down[3], x_up[4], x_up[3], x_up[2], x_up[1]]
    w_slots = [w0, w_down[1], w_down[2], w_down[3], w_down[4], w_up[3], w_up[2], w_up[1]]

    early = row_sums(x_slots[:4] + x_slots[5:])
    own_sums = row_sums([x_slots[4]], early)
    other_sums = shifted(own_sums, "c", 2, 1)
    mod_row = lax.dynamic_index_in_dim(modulation, levels[span_id], 0, keepdims=False)
    table = mod_row.astype(jnp.float32).reshape(-1, feats)
    normed = pl.pallas_call(
        norm_kernel,
        out_shape=jax.ShapeDtypeStruct((RING, 2, span_len, feats), jnp.bfloat16),
        in_specs=[SMEM] + [VMEM] * 3 + [ANY] * RING,
        out_specs=VMEM,
        scratch_shapes=[
            pltpu.VMEM((RING, 2 * feats, span_len), jnp.bfloat16),
            pltpu.SemaphoreType.DMA((RING,)),
        ],
        compiler_params=params(),
    )(ids, own_sums, other_sums, table, *x_slots)
    first = (0, 1, 2, 3, 5, 6, 7)
    parts = project(ids, normed, first, [w_slots[s] for s in first])
    mine, theirs = project(ids, normed, (4,), [w_slots[4]], parts)
    kv0 = pl.pallas_call(
        join_kernel,
        out_shape=jax.ShapeDtypeStruct((2 * span_len, HD), jnp.bfloat16),
        in_specs=[VMEM, VMEM],
        out_specs=VMEM,
        compiler_params=params(),
    )(mine, shifted(theirs, "c", 2, 1))

    kv1 = shifted(kv0, "xl", 2, 1)
    kv2 = shifted(kv0, "yl", 2, 1)
    kv3 = lax.ppermute(kv0, ("yl", "xl"), [(i, 3 - i) for i in range(4)])
    kvs = (kv0, kv1, kv2, kv3)
    parts = [None] * QUAD
    for later in (3, 2, 1, 0):
        q = moved(queries, -later) if later else queries
        part = attend(later, ids, visible, counts, q, kvs)
        parts[later] = moved(part, later) if later else part
    return pl.pallas_call(
        merge_kernel,
        out_shape=jax.ShapeDtypeStruct((span_len, HD), jnp.bfloat16),
        in_specs=[SMEM, SMEM] + [VMEM] * QUAD,
        out_specs=VMEM,
        compiler_params=params(8),
    )(ids, counts, *parts)


def solution(mesh):
    fine = Mesh(mesh.devices.reshape(SIZES), SPAN_AXES + FSDP_AXES)
    spread = P(SPAN_AXES, FSDP_AXES)
    return jax.shard_map(
        on_device,
        mesh=fine,
        in_specs=(spread, spread, spread, spread, P(), P(), P(), P()),
        out_specs=spread,
        check_vma=False,
    )
```

time: 172 us -> 151 us (0.88)
  the two profiles are of different devices: /device:TPU:8 before, /device:TPU:47 now
where the time goes in v2:
time: 151 us; the launch traced here: 150 us
  starting transfers between devices  83 us (55%)
  waiting for transfers between devices  31.1 us (21%)
  Pallas kernels  22 us (15%)
  local copies, waits for them, and re-layouts  8.43 us (6%)
  other arithmetic  2.71 us (2%)
  between operations  2.51 us (2%)
    ppermute x21, starting transfers between devices, shifted(): lax.ppermute(value, axis, [(i, (i + by) % size) for i in range(size)])  71.3 us
    ppermute x6, waiting for transfers between devices, moved(): lax.ppermute(value, 'yh', [(i, i + by) for i in range(QUAD) if 0 <= i + b...  15 us
    ppermute x21, waiting for transfers between devices, shifted(): lax.ppermute(value, axis, [(i, (i + by) % size) for i in range(size)])  10.3 us
    ppermute x6, starting transfers between devices, moved(): lax.ppermute(value, 'yh', [(i, i + by) for i in range(QUAD) if 0 <= i + b...  9.08 us
    pallas_call x4, Pallas kernels, attend(): pl.pallas_call(functools.partial(attend_kernel, later), out_shape=jax.Sha...  7.48 us
    ppermute x1, waiting for transfers between devices, on_device(): kv3 = lax.ppermute(kv0, ('yl', 'xl'), [(i, 3 - i) for i in range(4)])  5.78 us
    pallas_call x2, Pallas kernels, project(): pl.pallas_call(functools.partial(project_kernel, slots, bool(earlier)), o...  5.64 us
    unnamed x30, local copies, waits for them, and re-layouts  5.6 us
  transfers between devices with their start and end apart: 28, of which 8 were waited for; matrix products, arithmetic and copies ran while one was open for 4% of the time, Pallas kernels for 12%

profile of v2, /device:TPU:47, one launch (start us, length us, event | category | flops | bytes accessed | tf_op | source)
XLA Modules:
  0.0 149.7 jit_solution(4834019005649452646)
XLA Ops:
  0.1 0.9 copy-done.9
  1.0 0.9 copy-done.10
  2.5 2.6 %collective-permute-start.9 = (bf16[192,256]{1,0:T(8,128)(2,1)S(1)}, bf16[192,256]{1,0:T(8,128)(2,1)S(1)}, u32[]{:S(2)}, u32[]{:S(2)}) collective-permute-start(bf16[192,256]{1,0:T(8,128)(2,1)S(1)} %get-tuple-element.12), channel_id=1, source_target_pairs={{0,1},{1,0},{2,3},{3,2},{4,5},{5,4},{6,7},{7,6},{8,9},{9,8},{10,11... | collective-permute-start | bytes 294920 | tf_op jit(solution)/shard_map/ppermute | solution.py:32
  5.1 3.0 %collective-permute-start = (bf16[192,512]{1,0:T(8,128)(2,1)}, bf16[192,512]{1,0:T(8,128)(2,1)S(1)}, u32[]{:S(2)}, u32[]{:S(2)}) collective-permute-start(bf16[192,512]{1,0:T(8,128)(2,1)} %bitcast.16), channel_id=1, source_target_pairs={{0,16},{16,0},{1,17},{17,1},{2,18},{18,2},{3,19},{19,3},{4,20},{20... | collective-permute-start | bytes 589832 | tf_op jit(solution)/shard_map/ppermute | solution.py:32
  8.1 1.9 %collective-permute-start.10 = (bf16[2,192,256]{2,1,0:T(8,128)(2,1)S(1)}, bf16[2,192,256]{2,1,0:T(8,128)(2,1)S(1)}, u32[]{:S(2)}, u32[]{:S(2)}) collective-permute-start(bf16[2,192,256]{2,1,0:T(8,128)(2,1)S(1)} %pad_maximum_fusion.2), channel_id=1, source_target_pairs={{0,32},{32,0},{1,33},{33,1},{2,34},{34,2},{3,35},{35,3},{4,36},{36... | collective-permute-start | bytes 589832 | tf_op jit(solution)/shard_map/ppermute | solution.py:32
  10.1 5.1 %collective-permute-done = bf16[192,512]{1,0:T(8,128)(2,1)S(1)} collective-permute-done((bf16[192,512]{1,0:T(8,128)(2,1)}, bf16[192,512]{1,0:T(8,128)(2,1)S(1)}, u32[]{:S(2)}, u32[]{:S(2)}) %collective-permute-start) | collective-permute-done | bytes 196640 | tf_op jit(solution)/shard_map/ppermute | solution.py:32
  15.2 1.0 pad_maximum_fusion.refs_0_
  16.1 4.0 %collective-permute-start.1 = (bf16[384,512]{1,0:T(8,128)(2,1)S(1)}, bf16[384,512]{1,0:T(8,128)(2,1)S(1)}, u32[]{:S(2)}, u32[]{:S(2)}) collective-permute-start(bf16[384,512]{1,0:T(8,128)(2,1)S(1)} %pad_maximum_fusion.refs_0_), channel_id=1, source_target_pairs={{0,2},{2,4},{4,6},{6,8},{8,10},{10,12},{12,14},{14,0},{1,3},{3,5},... | collective-permute-start | bytes 1179656 | tf_op jit(solution)/shard_map/ppermute | solution.py:32
  20.2 3.0 %collective-permute-start.11 = (bf16[4,192,256]{2,1,0:T(8,128)(2,1)S(1)}, bf16[4,192,256]{2,1,0:T(8,128)(2,1)S(1)}, u32[]{:S(2)}, u32[]{:S(2)}) collective-permute-start(bf16[4,192,256]{2,1,0:T(8,128)(2,1)S(1)} %pad_maximum_fusion.1.refs_0_), channel_id=1, source_target_pairs={{0,448},{64,0},{128,64},{192,128},{256,192},{320,256},{384,320},{4... | collective-permute-start | bytes 1179656 | tf_op jit(solution)/shard_map/ppermute | solution.py:32
  23.2 8.6 %collective-permute-start.5 = (bf16[384,512]{1,0:T(8,128)(2,1)S(1)}, bf16[384,512]{1,0:T(8,128)(2,1)S(1)}, u32[]{:S(2)}, u32[]{:S(2)}) collective-permute-start(bf16[384,512]{1,0:T(8,128)(2,1)S(1)} %pad_maximum_fusion.refs_0_), channel_id=1, source_target_pairs={{0,14},{2,0},{4,2},{6,4},{8,6},{10,8},{12,10},{14,12},{1,15},{3,1}... | collective-permute-start | bytes 1179656 | tf_op jit(solution)/shard_map/ppermute | solution.py:32
  31.8 3.3 %collective-permute-done.1.refs_6_.refs_7_ = bf16[384,512]{1,0:T(8,128)(2,1)S(1)} collective-permute-done((bf16[384,512]{1,0:T(8,128)(2,1)S(1)}, bf16[384,512]{1,0:T(8,128)(2,1)S(1)}, u32[]{:S(2)}, u32[]{:S(2)}) %collective-permute-start.1) | collective-permute-done | bytes 393248 | tf_op jit(solution)/shard_map/ppermute | solution.py:32
  35.1 1.9 %collective-permute-start.2 = (bf16[384,512]{1,0:T(8,128)(2,1)S(1)}, bf16[384,512]{1,0:T(8,128)(2,1)S(1)}, u32[]{:S(2)}, u32[]{:S(2)}) collective-permute-start(bf16[384,512]{1,0:T(8,128)(2,1)S(1)} %collective-permute-done.1.refs_6_.refs_7_), channel_id=1, source_target_pairs={{0,2},{2,4},{4,6},{6,8},{8,10},{10,12},{12,14},{14,0},{1,3},{3,5},... | collective-permute-start | bytes 1179656 | tf_op jit(solution)/shard_map/ppermute | solution.py:32
  37.0 2.3 %collective-permute-start.15 = (bf16[4,192,256]{2,1,0:T(8,128)(2,1)S(1)}, bf16[4,192,256]{2,1,0:T(8,128)(2,1)S(1)}, u32[]{:S(2)}, u32[]{:S(2)}) collective-permute-start(bf16[4,192,256]{2,1,0:T(8,128)(2,1)S(1)} %pad_maximum_fusion.1.refs_0_), channel_id=1, source_target_pairs={{0,64},{64,128},{128,192},{192,256},{256,320},{320,384},{384,448},... | collective-permute-start | bytes 1179656 | tf_op jit(solution)/shard_map/ppermute | solution.py:32
  39.3 3.0 %collective-permute-start.12 = (bf16[4,192,256]{2,1,0:T(8,128)(2,1)S(1)}, bf16[4,192,256]{2,1,0:T(8,128)(2,1)S(1)}, u32[]{:S(2)}, u32[]{:S(2)}) collective-permute-start(bf16[4,192,256]{2,1,0:T(8,128)(2,1)S(1)} %collective-permute-done.11.refs_1_), channel_id=1, source_target_pairs={{0,448},{64,0},{128,64},{192,128},{256,192},{320,256},{384,320},{4... | collective-permute-start | bytes 1179656 | tf_op jit(solution)/shard_map/ppermute | solution.py:32
  43.0 4.6 %collective-permute-start.6 = (bf16[384,512]{1,0:T(8,128)(2,1)S(1)}, bf16[384,512]{1,0:T(8,128)(2,1)S(1)}, u32[]{:S(2)}, u32[]{:S(2)}) collective-permute-start(bf16[384,512]{1,0:T(8,128)(2,1)S(1)} %collective-permute-done.5.refs_1_), channel_id=1, source_target_pairs={{0,14},{2,0},{4,2},{6,4},{8,6},{10,8},{12,10},{14,12},{1,15},{3,1}... | collective-permute-start | bytes 1179656 | tf_op jit(solution)/shard_map/ppermute | solution.py:32
  47.6 1.9 %collective-permute-start.3 = (bf16[384,512]{1,0:T(8,128)(2,1)S(1)}, bf16[384,512]{1,0:T(8,128)(2,1)S(1)}, u32[]{:S(2)}, u32[]{:S(2)}) collective-permute-start(bf16[384,512]{1,0:T(8,128)(2,1)S(1)} %collective-permute-done.2.refs_5_.refs_6_), channel_id=1, source_target_pairs={{0,2},{2,4},{4,6},{6,8},{8,10},{10,12},{12,14},{14,0},{1,3},{3,5},... | collective-permute-start | bytes 1179656 | tf_op jit(solution)/shard_map/ppermute | solution.py:32
  49.6 2.3 %collective-permute-start.16 = (bf16[4,192,256]{2,1,0:T(8,128)(2,1)S(1)}, bf16[4,192,256]{2,1,0:T(8,128)(2,1)}, u32[]{:S(2)}, u32[]{:S(2)}) collective-permute-start(bf16[4,192,256]{2,1,0:T(8,128)(2,1)S(1)} %collective-permute-done.15.refs_6_), channel_id=1, source_target_pairs={{0,64},{64,128},{128,192},{192,256},{256,320},{320,384},{384,448},... | collective-permute-start | bytes 1179656 | tf_op jit(solution)/shard_map/ppermute | solution.py:32
  52.6 3.8 %collective-permute-start.13 = (bf16[4,192,256]{2,1,0:T(8,128)(2,1)S(1)}, bf16[4,192,256]{2,1,0:T(8,128)(2,1)}, u32[]{:S(2)}, u32[]{:S(2)}) collective-permute-start(bf16[4,192,256]{2,1,0:T(8,128)(2,1)S(1)} %collective-permute-done.12.refs_2_), channel_id=1, source_target_pairs={{0,448},{64,0},{128,64},{192,128},{256,192},{320,256},{384,320},{4... | collective-permute-start | bytes 1179656 | tf_op jit(solution)/shard_map/ppermute | solution.py:32
  57.2 4.6 %collective-permute-start.7 = (bf16[384,512]{1,0:T(8,128)(2,1)S(1)}, bf16[384,512]{1,0:T(8,128)(2,1)S(1)}, u32[]{:S(2)}, u32[]{:S(2)}) collective-permute-start(bf16[384,512]{1,0:T(8,128)(2,1)S(1)} %collective-permute-done.6.refs_2_), channel_id=1, source_target_pairs={{0,14},{2,0},{4,2},{6,4},{8,6},{10,8},{12,10},{14,12},{1,15},{3,1}... | collective-permute-start | bytes 1179656 | tf_op jit(solution)/shard_map/ppermute | solution.py:32
  61.8 1.9 %collective-permute-start.4 = (bf16[384,512]{1,0:T(8,128)(2,1)S(1)}, bf16[384,512]{1,0:T(8,128)(2,1)S(1)}, u32[]{:S(2)}, u32[]{:S(2)}) collective-permute-start(bf16[384,512]{1,0:T(8,128)(2,1)S(1)} %collective-permute-done.3.refs_4_.refs_5_), channel_id=1, source_target_pairs={{0,2},{2,4},{4,6},{6,8},{8,10},{10,12},{12,14},{14,0},{1,3},{3,5},... | collective-permute-start | bytes 1179656 | tf_op jit(solution)/shard_map/ppermute | solution.py:32
  63.7 1.9 %collective-permute-start.17 = (bf16[4,192,256]{2,1,0:T(8,128)(2,1)}, bf16[4,192,256]{2,1,0:T(8,128)(2,1)}, u32[]{:S(2)}, u32[]{:S(2)}) collective-permute-start(bf16[4,192,256]{2,1,0:T(8,128)(2,1)} %collective-permute-done.16.refs_5_), channel_id=1, source_target_pairs={{0,64},{64,128},{128,192},{192,256},{256,320},{320,384},{384,448},... | collective-permute-start | bytes 1179656 | tf_op jit(solution)/shard_map/ppermute | solution.py:32
  65.7 4.6 %collective-permute-start.14 = (bf16[4,192,256]{2,1,0:T(8,128)(2,1)}, bf16[4,192,256]{2,1,0:T(8,128)(2,1)}, u32[]{:S(2)}, u32[]{:S(2)}) collective-permute-start(bf16[4,192,256]{2,1,0:T(8,128)(2,1)} %collective-permute-done.13.refs_3_), channel_id=1, source_target_pairs={{0,448},{64,0},{128,64},{192,128},{256,192},{320,256},{384,320},{4... | collective-permute-start | bytes 1179656 | tf_op jit(solution)/shard_map/ppermute | solution.py:32
  70.3 1.9 %shard_map.82.refs_1_ = f32[8,512]{1,0:T(8,128)S(1)} custom-call(bf16[384,512]{1,0:T(8,128)(2,1)S(1)} %pad_maximum_fusion.refs_0_, bf16[384,512]{1,0:T(8,128)(2,1)S(1)} %collective-permute-done.5.refs_1_, bf16[384,512]{1,0:T(8,128)(2,1)S(1)} %collective-permute-done.6.refs_2_, bf16[384,512]{1,0:T(8,128)(2,1)S(1)} %collective-permute-done.7.refs_3_, ...), custom_call_target="tpu_custom_call" | custom-call | tf_op jit(solution)/shard_map/pallas_call | solution.py:76
  72.5 6.2 %collective-permute-start.8 = (f32[8,512]{1,0:T(8,128)S(1)}, f32[8,512]{1,0:T(8,128)}, u32[]{:S(2)}, u32[]{:S(2)}) collective-permute-start(f32[8,512]{1,0:T(8,128)S(1)} %shard_map.83.own_ref), channel_id=1, source_target_pairs={{0,1},{1,0},{2,3},{3,2},{4,5},{5,4},{6,7},{7,6},{8,9},{9,8},{10,11... | collective-permute-start | bytes 49160 | tf_op jit(solution)/shard_map/ppermute | solution.py:32
  78.7 1.2 dynamic_slice.7
  81.9 1.7 %convert_reduce_fusion = f32[12288]{0:T(1024)} fusion(bf16[8,12288]{1,0:T(8,128)(2,1)} %param.12, s32[]{:T(128)S(6)} %select_n.8), kind=kLoop, calls=%fused_computation.3 | loop fusion | flops 12288 | bytes 73732 | tf_op jit(solution)/shard_map/convert_element_type | solution.py:300
  83.6 1.5 %reshape.4.table_ref = f32[64,192]{1,0:T(8,128)} reshape(f32[12288]{0:T(1024)} %convert_reduce_fusion) | data formatting | bytes 98304 | tf_op jit(solution)/shard_map/convert_element_type | solution.py:300
  85.1 0.9 copy-done.6
  86.6 4.6 %shard_map.84.normed_ref = bf16[8,2,512,192]{3,2,1,0:T(8,128)(2,1)S(1)} custom-call(s32[8]{0:T(128)S(1)} %copy-done.12, f32[8,512]{1,0:T(8,128)S(1)} %shard_map.83.own_ref, f32[8,512]{1,0:T(8,128)} %collective-permute-done.8.other_ref, f32[64,192]{1,0:T(8,128)S(1)} %copy-done.6, bf16[384,512]{1,0:T(8,128)(2,1)S(1)} %pad_maximum_fusion.refs_0_, ...), custom_call_target="tpu_custom_call" | custom-call | tf_op jit(solution)/shard_map/pallas_call | solution.py:301
  91.3 3.7 %shard_map.86 = (f32[512,256]{1,0:T(8,128)S(1)}, f32[512,256]{1,0:T(8,128)S(1)}) custom-call(s32[8]{0:T(128)S(1)} %copy-done.13, bf16[8,2,512,192]{3,2,1,0:T(8,128)(2,1)S(1)} %shard_map.84.normed_ref, bf16[4,192,256]{2,1,0:T(8,128)(2,1)S(1)} %pad_maximum_fusion.1.refs_0_, bf16[4,192,256]{2,1,0:T(8,128)(2,1)S(1)} %copy-done.1, ...), custom_call_target="tpu_custom_call" | custom-call | tf_op jit(solution)/shard_map/pallas_call | solution.py:145
  95.0 2.0 %shard_map.87 = (f32[512,256]{1,0:T(8,128)S(1)}, f32[512,256]{1,0:T(8,128)S(1)}) custom-call(s32[8]{0:T(128)S(1)} %copy-done.13, bf16[8,2,512,192]{3,2,1,0:T(8,128)(2,1)S(1)} %shard_map.84.normed_ref, bf16[4,192,256]{2,1,0:T(8,128)(2,1)} %collective-permute-done.14.refs_0_, f32[512,256]{1,0:T(8,128)S(1)} %get-tuple-element.13.refs_1_, ...), custom_call_target="tpu_custom_call" | custom-call | tf_op jit(solution)/shard_map/pallas_call | solution.py:145
  97.0 1.9 %collective-permute-start.18 = (f32[512,256]{1,0:T(8,128)S(1)}, f32[512,256]{1,0:T(8,128)S(1)}, u32[]{:S(2)}, u32[]{:S(2)}) collective-permute-start(f32[512,256]{1,0:T(8,128)S(1)} %get-tuple-element.16), channel_id=1, source_target_pairs={{0,1},{1,0},{2,3},{3,2},{4,5},{5,4},{6,7},{7,6},{8,9},{9,8},{10,11... | collective-permute-start | bytes 1572872 | tf_op jit(solution)/shard_map/ppermute | solution.py:32
  98.9 1.9 %collective-permute-done.18.theirs_ref = f32[512,256]{1,0:T(8,128)S(1)} collective-permute-done((f32[512,256]{1,0:T(8,128)S(1)}, f32[512,256]{1,0:T(8,128)S(1)}, u32[]{:S(2)}, u32[]{:S(2)}) %collective-permute-start.18) | collective-permute-done | bytes 524320 | tf_op jit(solution)/shard_map/ppermute | solution.py:32
  100.9 2.5 %collective-permute-start.19 = (bf16[1024,128]{1,0:T(8,128)(2,1)S(1)}, bf16[1024,128]{1,0:T(8,128)(2,1)S(1)}, u32[]{:S(2)}, u32[]{:S(2)}) collective-permute-start(bf16[1024,128]{1,0:T(8,128)(2,1)S(1)} %shard_map.88.kv0), channel_id=1, source_target_pairs={{0,32},{32,0},{1,33},{33,1},{2,34},{34,2},{3,35},{35,3},{4,36},{36... | collective-permute-start | bytes 786440 | tf_op jit(solution)/shard_map/ppermute | solution.py:32
  103.4 4.9 %collective-permute-start.20 = (bf16[1024,128]{1,0:T(8,128)(2,1)S(1)}, bf16[1024,128]{1,0:T(8,128)(2,1)S(1)}, u32[]{:S(2)}, u32[]{:S(2)}) collective-permute-start(bf16[1024,128]{1,0:T(8,128)(2,1)S(1)} %shard_map.88.kv0), channel_id=1, source_target_pairs={{0,64},{64,0},{1,65},{65,1},{2,66},{66,2},{3,67},{67,3},{4,68},{68... | collective-permute-start | bytes 786440 | tf_op jit(solution)/shard_map/ppermute | solution.py:32
  108.2 2.6 %collective-permute-start.21 = (bf16[1024,128]{1,0:T(8,128)(2,1)S(1)}, bf16[1024,128]{1,0:T(8,128)(2,1)S(1)}, u32[]{:S(2)}, u32[]{:S(2)}) collective-permute-start(bf16[1024,128]{1,0:T(8,128)(2,1)S(1)} %shard_map.88.kv0), channel_id=1, source_target_pairs={{0,96},{32,64},{64,32},{96,0},{1,97},{33,65},{65,33},{97,1},{2,98}... | collective-permute-start | bytes 786440 | tf_op jit(solution)/shard_map/ppermute | solution.py:325
  111.5 2.6 %collective-permute-start.24 = (bf16[512,128]{1,0:T(8,128)(2,1)S(1)}, bf16[512,128]{1,0:T(8,128)(2,1)S(1)}, u32[]{:S(2)}, u32[]{:S(2)}) collective-permute-start(bf16[512,128]{1,0:T(8,128)(2,1)S(1)} %copy-done.8), channel_id=1, source_target_pairs={{256,0},{384,128},{257,1},{385,129},{258,2},{386,130},{259,3},{387... | collective-permute-start | bytes 393224 | tf_op jit(solution)/shard_map/ppermute | solution.py:36
  114.1 1.9 %collective-permute-start.22 = (bf16[512,128]{1,0:T(8,128)(2,1)S(1)}, bf16[512,128]{1,0:T(8,128)(2,1)S(1)}, u32[]{:S(2)}, u32[]{:S(2)}) collective-permute-start(bf16[512,128]{1,0:T(8,128)(2,1)S(1)} %copy-done.8), channel_id=1, source_target_pairs={{128,0},{256,128},{384,256},{129,1},{257,129},{385,257},{130,2},{2... | collective-permute-start | bytes 393224 | tf_op jit(solution)/shard_map/ppermute | solution.py:36
  116.1 5.8 %collective-permute-done.21.kv3 = bf16[1024,128]{1,0:T(8,128)(2,1)S(1)} collective-permute-done((bf16[1024,128]{1,0:T(8,128)(2,1)S(1)}, bf16[1024,128]{1,0:T(8,128)(2,1)S(1)}, u32[]{:S(2)}, u32[]{:S(2)}) %collective-permute-start.21) | collective-permute-done | bytes 262176 | tf_op jit(solution)/shard_map/ppermute | solution.py:325
  123.2 4.3 %collective-permute-done.24.q_ref = bf16[512,128]{1,0:T(8,128)(2,1)S(1)} collective-permute-done((bf16[512,128]{1,0:T(8,128)(2,1)S(1)}, bf16[512,128]{1,0:T(8,128)(2,1)S(1)}, u32[]{:S(2)}, u32[]{:S(2)}) %collective-permute-start.24) | collective-permute-done | bytes 131104 | tf_op jit(solution)/shard_map/ppermute | solution.py:36
  128.2 1.3 collective-permute-start.25
  129.5 0.8 collective-permute-done.22.q_ref
  130.3 3.4 %shard_map.90 = bf16[144,512]{1,0:T(8,128)(2,1)S(1)} custom-call(s32[8]{0:T(128)S(1)} %copy-done.13, s32[16,16]{1,0:T(8,128)S(1)} %copy-done.7, s32[16]{0:T(128)S(1)} %copy-done.14, bf16[512,128]{1,0:T(8,128)(2,1)S(1)} %collective-permute-done.22.q_ref, bf16[1024,128]{1,0:T(8,128)(2,1)S(1)} %shard_map.88.kv0, ...), custom_call_target="tpu_custom_call" | custom-call | tf_op jit(solution)/shard_map/pallas_call | solution.py:222
  133.7 1.9 %collective-permute-start.23 = (bf16[144,512]{1,0:T(8,128)(2,1)S(1)}, bf16[144,512]{1,0:T(8,128)(2,1)S(1)}, u32[]{:S(2)}, u32[]{:S(2)}) collective-permute-start(bf16[144,512]{1,0:T(8,128)(2,1)S(1)} %shard_map.90), channel_id=1, source_target_pairs={{0,128},{128,256},{256,384},{1,129},{129,257},{257,385},{2,130},{1... | collective-permute-start | bytes 442376 | tf_op jit(solution)/shard_map/ppermute | solution.py:36
  135.6 2.7 %shard_map.89.part0 = bf16[144,512]{1,0:T(8,128)(2,1)S(1)} custom-call(s32[8]{0:T(128)S(1)} %copy-done.13, s32[16,16]{1,0:T(8,128)S(1)} %copy-done.7, s32[16]{0:T(128)S(1)} %copy-done.14, bf16[512,128]{1,0:T(8,128)(2,1)S(1)} %copy-done.8, bf16[1024,128]{1,0:T(8,128)(2,1)S(1)} %shard_map.88.kv0, bf16[1024,128]{1,0:T(8,128)(2,1)S(1)} %collective-permute-done.19.kv1, ...), custom_call_target="tpu_custom_call" | custom-call | tf_op jit(solution)/shard_map/pallas_call | solution.py:222
  138.4 1.2 collective-permute-done.25.part2
  139.6 8.7 %collective-permute-done.23.part1 = bf16[144,512]{1,0:T(8,128)(2,1)S(1)} collective-permute-done((bf16[144,512]{1,0:T(8,128)(2,1)S(1)}, bf16[144,512]{1,0:T(8,128)(2,1)S(1)}, u32[]{:S(2)}, u32[]{:S(2)}) %collective-permute-start.23) | collective-permute-done | bytes 147488 | tf_op jit(solution)/shard_map/ppermute | solution.py:36
  148.3 1.4 shard_map.93
  (57 shorter events, 6.8 us)
Async XLA Ops:
  0.1 0.9 copy-start.9
  1.0 0.9 copy-start.10
  1.9 8.2 %copy-start.11 = (s32[8]{0:T(128)}, s32[8]{0:T(128)S(1)}, u32[]{:S(2)}) copy-start(s32[8]{0:T(128)S(1)} %stack.44.ids_ref) | copy-start | bytes 100
  2.5 5.6 %collective-permute-start.9 = (bf16[192,256]{1,0:T(8,128)(2,1)S(1)}, bf16[192,256]{1,0:T(8,128)(2,1)S(1)}, u32[]{:S(2)}, u32[]{:S(2)}) collective-permute-start(bf16[192,256]{1,0:T(8,128)(2,1)S(1)} %get-tuple-element.12), channel_id=1, source_target_pairs={{0,1},{1,0},{2,3},{3,2},{4,5},{5,4},{6,7},{7,6},{8,9},{9,8},{10,11... | collective-permute-start | bytes 294920 | tf_op jit(solution)/shard_map/ppermute | solution.py:32
  5.1 10.1 %collective-permute-start = (bf16[192,512]{1,0:T(8,128)(2,1)}, bf16[192,512]{1,0:T(8,128)(2,1)S(1)}, u32[]{:S(2)}, u32[]{:S(2)}) collective-permute-start(bf16[192,512]{1,0:T(8,128)(2,1)} %bitcast.16), channel_id=1, source_target_pairs={{0,16},{16,0},{1,17},{17,1},{2,18},{18,2},{3,19},{19,3},{4,20},{20... | collective-permute-start | bytes 589832 | tf_op jit(solution)/shard_map/ppermute | solution.py:32
  8.1 12.0 %collective-permute-start.10 = (bf16[2,192,256]{2,1,0:T(8,128)(2,1)S(1)}, bf16[2,192,256]{2,1,0:T(8,128)(2,1)S(1)}, u32[]{:S(2)}, u32[]{:S(2)}) collective-permute-start(bf16[2,192,256]{2,1,0:T(8,128)(2,1)S(1)} %pad_maximum_fusion.2), channel_id=1, source_target_pairs={{0,32},{32,0},{1,33},{33,1},{2,34},{34,2},{3,35},{35,3},{4,36},{36... | collective-permute-start | bytes 589832 | tf_op jit(solution)/shard_map/ppermute | solution.py:32
  16.1 18.9 %collective-permute-start.1 = (bf16[384,512]{1,0:T(8,128)(2,1)S(1)}, bf16[384,512]{1,0:T(8,128)(2,1)S(1)}, u32[]{:S(2)}, u32[]{:S(2)}) collective-permute-start(bf16[384,512]{1,0:T(8,128)(2,1)S(1)} %pad_maximum_fusion.refs_0_), channel_id=1, source_target_pairs={{0,2},{2,4},{4,6},{6,8},{8,10},{10,12},{12,14},{14,0},{1,3},{3,5},... | collective-permute-start | bytes 1179656 | tf_op jit(solution)/shard_map/ppermute | solution.py:32
  20.2 19.1 %collective-permute-start.11 = (bf16[4,192,256]{2,1,0:T(8,128)(2,1)S(1)}, bf16[4,192,256]{2,1,0:T(8,128)(2,1)S(1)}, u32[]{:S(2)}, u32[]{:S(2)}) collective-permute-start(bf16[4,192,256]{2,1,0:T(8,128)(2,1)S(1)} %pad_maximum_fusion.1.refs_0_), channel_id=1, source_target_pairs={{0,448},{64,0},{128,64},{192,128},{256,192},{320,256},{384,320},{4... | collective-permute-start | bytes 1179656 | tf_op jit(solution)/shard_map/ppermute | solution.py:32
  23.2 19.8 %collective-permute-start.5 = (bf16[384,512]{1,0:T(8,128)(2,1)S(1)}, bf16[384,512]{1,0:T(8,128)(2,1)S(1)}, u32[]{:S(2)}, u32[]{:S(2)}) collective-permute-start(bf16[384,512]{1,0:T(8,128)(2,1)S(1)} %pad_maximum_fusion.refs_0_), channel_id=1, source_target_pairs={{0,14},{2,0},{4,2},{6,4},{8,6},{10,8},{12,10},{14,12},{1,15},{3,1}... | collective-permute-start | bytes 1179656 | tf_op jit(solution)/shard_map/ppermute | solution.py:32
  35.1 12.6 %collective-permute-start.2 = (bf16[384,512]{1,0:T(8,128)(2,1)S(1)}, bf16[384,512]{1,0:T(8,128)(2,1)S(1)}, u32[]{:S(2)}, u32[]{:S(2)}) collective-permute-start(bf16[384,512]{1,0:T(8,128)(2,1)S(1)} %collective-permute-done.1.refs_6_.refs_7_), channel_id=1, source_target_pairs={{0,2},{2,4},{4,6},{6,8},{8,10},{10,12},{12,14},{14,0},{1,3},{3,5},... | collective-permute-start | bytes 1179656 | tf_op jit(solution)/shard_map/ppermute | solution.py:32
  37.0 12.6 %collective-permute-start.15 = (bf16[4,192,256]{2,1,0:T(8,128)(2,1)S(1)}, bf16[4,192,256]{2,1,0:T(8,128)(2,1)S(1)}, u32[]{:S(2)}, u32[]{:S(2)}) collective-permute-start(bf16[4,192,256]{2,1,0:T(8,128)(2,1)S(1)} %pad_maximum_fusion.1.refs_0_), channel_id=1, source_target_pairs={{0,64},{64,128},{128,192},{192,256},{256,320},{320,384},{384,448},... | collective-permute-start | bytes 1179656 | tf_op jit(solution)/shard_map/ppermute | solution.py:32
  39.3 13.3 %collective-permute-start.12 = (bf16[4,192,256]{2,1,0:T(8,128)(2,1)S(1)}, bf16[4,192,256]{2,1,0:T(8,128)(2,1)S(1)}, u32[]{:S(2)}, u32[]{:S(2)}) collective-permute-start(bf16[4,192,256]{2,1,0:T(8,128)(2,1)S(1)} %collective-permute-done.11.refs_1_), channel_id=1, source_target_pairs={{0,448},{64,0},{128,64},{192,128},{256,192},{320,256},{384,320},{4... | collective-permute-start | bytes 1179656 | tf_op jit(solution)/shard_map/ppermute | solution.py:32
  42.3 0.8 copy-start
  43.0 14.2 %collective-permute-start.6 = (bf16[384,512]{1,0:T(8,128)(2,1)S(1)}, bf16[384,512]{1,0:T(8,128)(2,1)S(1)}, u32[]{:S(2)}, u32[]{:S(2)}) collective-permute-start(bf16[384,512]{1,0:T(8,128)(2,1)S(1)} %collective-permute-done.5.refs_1_), channel_id=1, source_target_pairs={{0,14},{2,0},{4,2},{6,4},{8,6},{10,8},{12,10},{14,12},{1,15},{3,1}... | collective-permute-start | bytes 1179656 | tf_op jit(solution)/shard_map/ppermute | solution.py:32
  47.6 14.2 %collective-permute-start.3 = (bf16[384,512]{1,0:T(8,128)(2,1)S(1)}, bf16[384,512]{1,0:T(8,128)(2,1)S(1)}, u32[]{:S(2)}, u32[]{:S(2)}) collective-permute-start(bf16[384,512]{1,0:T(8,128)(2,1)S(1)} %collective-permute-done.2.refs_5_.refs_6_), channel_id=1, source_target_pairs={{0,2},{2,4},{4,6},{6,8},{8,10},{10,12},{12,14},{14,0},{1,3},{3,5},... | collective-permute-start | bytes 1179656 | tf_op jit(solution)/shard_map/ppermute | solution.py:32
  49.6 14.2 %collective-permute-start.16 = (bf16[4,192,256]{2,1,0:T(8,128)(2,1)S(1)}, bf16[4,192,256]{2,1,0:T(8,128)(2,1)}, u32[]{:S(2)}, u32[]{:S(2)}) collective-permute-start(bf16[4,192,256]{2,1,0:T(8,128)(2,1)S(1)} %collective-permute-done.15.refs_6_), channel_id=1, source_target_pairs={{0,64},{64,128},{128,192},{192,256},{256,320},{320,384},{384,448},... | collective-permute-start | bytes 1179656 | tf_op jit(solution)/shard_map/ppermute | solution.py:32
  51.9 0.8 copy-start.2
  52.6 13.0 %collective-permute-start.13 = (bf16[4,192,256]{2,1,0:T(8,128)(2,1)S(1)}, bf16[4,192,256]{2,1,0:T(8,128)(2,1)}, u32[]{:S(2)}, u32[]{:S(2)}) collective-permute-start(bf16[4,192,256]{2,1,0:T(8,128)(2,1)S(1)} %collective-permute-done.12.refs_2_), channel_id=1, source_target_pairs={{0,448},{64,0},{128,64},{192,128},{256,192},{320,256},{384,320},{4... | collective-permute-start | bytes 1179656 | tf_op jit(solution)/shard_map/ppermute | solution.py:32
  56.4 0.8 copy-start.4
  57.2 13.0 %collective-permute-start.7 = (bf16[384,512]{1,0:T(8,128)(2,1)S(1)}, bf16[384,512]{1,0:T(8,128)(2,1)S(1)}, u32[]{:S(2)}, u32[]{:S(2)}) collective-permute-start(bf16[384,512]{1,0:T(8,128)(2,1)S(1)} %collective-permute-done.6.refs_2_), channel_id=1, source_target_pairs={{0,14},{2,0},{4,2},{6,4},{8,6},{10,8},{12,10},{14,12},{1,15},{3,1}... | collective-permute-start | bytes 1179656 | tf_op jit(solution)/shard_map/ppermute | solution.py:32
  61.8 10.4 %collective-permute-start.4 = (bf16[384,512]{1,0:T(8,128)(2,1)S(1)}, bf16[384,512]{1,0:T(8,128)(2,1)S(1)}, u32[]{:S(2)}, u32[]{:S(2)}) collective-permute-start(bf16[384,512]{1,0:T(8,128)(2,1)S(1)} %collective-permute-done.3.refs_4_.refs_5_), channel_id=1, source_target_pairs={{0,2},{2,4},{4,6},{6,8},{8,10},{10,12},{12,14},{14,0},{1,3},{3,5},... | collective-permute-start | bytes 1179656 | tf_op jit(solution)/shard_map/ppermute | solution.py:32
  63.7 27.5 %collective-permute-start.17 = (bf16[4,192,256]{2,1,0:T(8,128)(2,1)}, bf16[4,192,256]{2,1,0:T(8,128)(2,1)}, u32[]{:S(2)}, u32[]{:S(2)}) collective-permute-start(bf16[4,192,256]{2,1,0:T(8,128)(2,1)} %collective-permute-done.16.refs_5_), channel_id=1, source_target_pairs={{0,64},{64,128},{128,192},{192,256},{256,320},{320,384},{384,448},... | collective-permute-start | bytes 1179656 | tf_op jit(solution)/shard_map/ppermute | solution.py:32
  65.7 29.4 %collective-permute-start.14 = (bf16[4,192,256]{2,1,0:T(8,128)(2,1)}, bf16[4,192,256]{2,1,0:T(8,128)(2,1)}, u32[]{:S(2)}, u32[]{:S(2)}) collective-permute-start(bf16[4,192,256]{2,1,0:T(8,128)(2,1)} %collective-permute-done.13.refs_3_), channel_id=1, source_target_pairs={{0,448},{64,0},{128,64},{192,128},{256,192},{320,256},{384,320},{4... | collective-permute-start | bytes 1179656 | tf_op jit(solution)/shard_map/ppermute | solution.py:32
  72.5 12.6 %collective-permute-start.8 = (f32[8,512]{1,0:T(8,128)S(1)}, f32[8,512]{1,0:T(8,128)}, u32[]{:S(2)}, u32[]{:S(2)}) collective-permute-start(f32[8,512]{1,0:T(8,128)S(1)} %shard_map.83.own_ref), channel_id=1, source_target_pairs={{0,1},{1,0},{2,3},{3,2},{4,5},{5,4},{6,7},{7,6},{8,9},{9,8},{10,11... | collective-permute-start | bytes 49160 | tf_op jit(solution)/shard_map/ppermute | solution.py:32
  85.1 6.2 %copy-start.1 = (bf16[4,192,256]{2,1,0:T(8,128)(2,1)S(1)}, bf16[4,192,256]{2,1,0:T(8,128)(2,1)}, u32[]{:S(2)}) copy-start(bf16[4,192,256]{2,1,0:T(8,128)(2,1)} %copy-done) | copy-start | bytes 1179652
  85.1 6.2 %copy-start.3 = (bf16[4,192,256]{2,1,0:T(8,128)(2,1)S(1)}, bf16[4,192,256]{2,1,0:T(8,128)(2,1)}, u32[]{:S(2)}) copy-start(bf16[4,192,256]{2,1,0:T(8,128)(2,1)} %copy-done.2) | copy-start | bytes 1179652
  85.1 6.2 %copy-start.5 = (bf16[4,192,256]{2,1,0:T(8,128)(2,1)S(1)}, bf16[4,192,256]{2,1,0:T(8,128)(2,1)}, u32[]{:S(2)}) copy-start(bf16[4,192,256]{2,1,0:T(8,128)(2,1)} %copy-done.4) | copy-start | bytes 1179652
  85.1 0.9 copy-start.6
  86.0 0.6 copy-start.12
  86.6 4.7 %copy-start.13 = (s32[8]{0:T(128)S(1)}, s32[8]{0:T(128)}, u32[]{:S(2)}) copy-start(s32[8]{0:T(128)} %copy-done.11) | copy-start | bytes 100
  95.0 15.8 %copy-start.8 = (bf16[512,128]{1,0:T(8,128)(2,1)S(1)}, bf16[512,128]{1,0:T(8,128)(2,1)}, u32[]{:S(2)}) copy-start(bf16[512,128]{1,0:T(8,128)(2,1)} %q_ref.1) | copy-start | bytes 393220
  95.0 26.9 %copy-start.7 = (s32[16,16]{1,0:T(8,128)S(1)}, s32[16,16]{1,0:T(8,128)}, u32[]{:S(2)}) copy-start(s32[16,16]{1,0:T(8,128)} %visible_ref.7) | copy-start | bytes 3076
  95.0 26.8 %copy-start.14 = (s32[16]{0:T(128)S(1)}, s32[16]{0:T(128)}, u32[]{:S(2)}) copy-start(s32[16]{0:T(128)} %counts_ref.9) | copy-start | bytes 196
  97.0 3.8 %collective-permute-start.18 = (f32[512,256]{1,0:T(8,128)S(1)}, f32[512,256]{1,0:T(8,128)S(1)}, u32[]{:S(2)}, u32[]{:S(2)}) collective-permute-start(f32[512,256]{1,0:T(8,128)S(1)} %get-tuple-element.16), channel_id=1, source_target_pairs={{0,1},{1,0},{2,3},{3,2},{4,5},{5,4},{6,7},{7,6},{8,9},{9,8},{10,11... | collective-permute-start | bytes 1572872 | tf_op jit(solution)/shard_map/ppermute | solution.py:32
  100.9 15.1 %collective-permute-start.19 = (bf16[1024,128]{1,0:T(8,128)(2,1)S(1)}, bf16[1024,128]{1,0:T(8,128)(2,1)S(1)}, u32[]{:S(2)}, u32[]{:S(2)}) collective-permute-start(bf16[1024,128]{1,0:T(8,128)(2,1)S(1)} %shard_map.88.kv0), channel_id=1, source_target_pairs={{0,32},{32,0},{1,33},{33,1},{2,34},{34,2},{3,35},{35,3},{4,36},{36... | collective-permute-start | bytes 786440 | tf_op jit(solution)/shard_map/ppermute | solution.py:32
  103.4 12.7 %collective-permute-start.20 = (bf16[1024,128]{1,0:T(8,128)(2,1)S(1)}, bf16[1024,128]{1,0:T(8,128)(2,1)S(1)}, u32[]{:S(2)}, u32[]{:S(2)}) collective-permute-start(bf16[1024,128]{1,0:T(8,128)(2,1)S(1)} %shard_map.88.kv0), channel_id=1, source_target_pairs={{0,64},{64,0},{1,65},{65,1},{2,66},{66,2},{3,67},{67,3},{4,68},{68... | collective-permute-start | bytes 786440 | tf_op jit(solution)/shard_map/ppermute | solution.py:32
  108.2 13.6 %collective-permute-start.21 = (bf16[1024,128]{1,0:T(8,128)(2,1)S(1)}, bf16[1024,128]{1,0:T(8,128)(2,1)S(1)}, u32[]{:S(2)}, u32[]{:S(2)}) collective-permute-start(bf16[1024,128]{1,0:T(8,128)(2,1)S(1)} %shard_map.88.kv0), channel_id=1, source_target_pairs={{0,96},{32,64},{64,32},{96,0},{1,97},{33,65},{65,33},{97,1},{2,98}... | collective-permute-start | bytes 786440 | tf_op jit(solution)/shard_map/ppermute | solution.py:325
  110.8 3.3 %collective-permute-start.26 = (bf16[512,128]{1,0:T(8,128)(2,1)S(1)}, bf16[512,128]{1,0:T(8,128)(2,1)S(1)}, u32[]{:S(2)}, u32[]{:S(2)}) collective-permute-start(bf16[512,128]{1,0:T(8,128)(2,1)S(1)} %copy-done.8), channel_id=1, source_target_pairs={{384,0},{385,1},{386,2},{387,3},{388,4},{389,5},{390,6},{391,7},{3... | collective-permute-start | bytes 393224 | tf_op jit(solution)/shard_map/ppermute | solution.py:36
  111.5 16.0 %collective-permute-start.24 = (bf16[512,128]{1,0:T(8,128)(2,1)S(1)}, bf16[512,128]{1,0:T(8,128)(2,1)S(1)}, u32[]{:S(2)}, u32[]{:S(2)}) collective-permute-start(bf16[512,128]{1,0:T(8,128)(2,1)S(1)} %copy-done.8), channel_id=1, source_target_pairs={{256,0},{384,128},{257,1},{385,129},{258,2},{386,130},{259,3},{387... | collective-permute-start | bytes 393224 | tf_op jit(solution)/shard_map/ppermute | solution.py:36
  114.1 16.2 %collective-permute-start.22 = (bf16[512,128]{1,0:T(8,128)(2,1)S(1)}, bf16[512,128]{1,0:T(8,128)(2,1)S(1)}, u32[]{:S(2)}, u32[]{:S(2)}) collective-permute-start(bf16[512,128]{1,0:T(8,128)(2,1)S(1)} %copy-done.8), channel_id=1, source_target_pairs={{128,0},{256,128},{384,256},{129,1},{257,129},{385,257},{130,2},{2... | collective-permute-start | bytes 393224 | tf_op jit(solution)/shard_map/ppermute | solution.py:36
  122.6 15.8 %collective-permute-start.27 = (bf16[144,512]{1,0:T(8,128)(2,1)S(1)}, bf16[144,512]{1,0:T(8,128)(2,1)S(1)}, u32[]{:S(2)}, u32[]{:S(2)}) collective-permute-start(bf16[144,512]{1,0:T(8,128)(2,1)S(1)} %shard_map.92), channel_id=1, source_target_pairs={{0,384},{1,385},{2,386},{3,387},{4,388},{5,389},{6,390},{7,391},{8... | collective-permute-start | bytes 442376 | tf_op jit(solution)/shard_map/ppermute | solution.py:36
  128.2 11.3 %collective-permute-start.25 = (bf16[144,512]{1,0:T(8,128)(2,1)S(1)}, bf16[144,512]{1,0:T(8,128)(2,1)S(1)}, u32[]{:S(2)}, u32[]{:S(2)}) collective-permute-start(bf16[144,512]{1,0:T(8,128)(2,1)S(1)} %shard_map.91), channel_id=1, source_target_pairs={{0,256},{128,384},{1,257},{129,385},{2,258},{130,386},{3,259},{131... | collective-permute-start | bytes 442376 | tf_op jit(solution)/shard_map/ppermute | solution.py:36
  133.7 14.6 %collective-permute-start.23 = (bf16[144,512]{1,0:T(8,128)(2,1)S(1)}, bf16[144,512]{1,0:T(8,128)(2,1)S(1)}, u32[]{:S(2)}, u32[]{:S(2)}) collective-permute-start(bf16[144,512]{1,0:T(8,128)(2,1)S(1)} %shard_map.90), channel_id=1, source_target_pairs={{0,128},{128,256},{256,384},{1,129},{129,257},{257,385},{2,130},{1... | collective-permute-start | bytes 442376 | tf_op jit(solution)/shard_map/ppermute | solution.py:36

commit v3 on v2

v3 whole, which is shorter than its diff:
```python
import functools

import jax
import jax.numpy as jnp
from jax import lax
from jax.experimental import pallas as pl
from jax.experimental.pallas import tpu as pltpu
from jax.sharding import Mesh, PartitionSpec as P

HD = 128
EPSILON = 1e-06
NEG_BIG = -1e30
LOG2E = 1.4426950408889634
SPAN_AXES = ("yh", "yl", "xl")
FSDP_AXES = ("xh", "z", "c")
SIZES = (4, 2, 2, 2, 8, 2)
QUAD = 4
RING = 8
STAT_ROWS = 16
SPAN, YH, PLACE, Y, XL, XH, Z, CORE, LEVEL = range(9)

VMEM = pl.BlockSpec(memory_space=pltpu.VMEM)
SMEM = pl.BlockSpec(memory_space=pltpu.SMEM)
HBM = pl.BlockSpec(memory_space=pltpu.HBM)


def params(mib=12):
    return pltpu.CompilerParams(vmem_limit_bytes=mib * 1024 * 1024)


def shifted(value, axis, size, by):
    return lax.ppermute(value, axis, [(i, (i + by) % size) for i in range(size)])


def moved(value, by):
    return lax.ppermute(value, "yh", [(i, i + by) for i in range(QUAD) if 0 <= i + by < QUAD])


def split_kernel(ids_ref, key_ref, value_ref, own_ref, other_ref, sems):
    rows = own_ref.shape[0]
    copies = []
    for part, out in ((1 - ids_ref[CORE], other_ref), (ids_ref[CORE], own_ref)):
        first = pl.multiple_of(part * rows, 16)
        for column, ref in enumerate((key_ref, value_ref)):
            copies.append(
                pltpu.make_async_copy(
                    ref.at[pl.ds(first, rows), :],
                    out.at[:, pl.ds(column * HD, HD)],
                    sems.at[len(copies)],
                )
            )
    for copy in copies:
        copy.start()
    for copy in copies:
        copy.wait()


def table_kernel(levels_ref, ids_ref, modulation_ref, out_ref):
    feats = out_ref.shape[1]
    rows = modulation_ref[...].astype(jnp.float32)
    chosen = lax.broadcasted_iota(jnp.int32, rows.shape, 0) == levels_ref[ids_ref[SPAN]]
    row = jnp.sum(jnp.where(chosen, rows, 0.0), axis=0, keepdims=True)
    for block in range(out_ref.shape[0]):
        out_ref[block : block + 1, :] = row[:, block * feats : (block + 1) * feats]


def sums_kernel(count, has_earlier, *refs):
    out = refs[-1]
    total = jnp.zeros((1, out.shape[1]), jnp.float32)
    square = jnp.zeros((1, out.shape[1]), jnp.float32)
    for ref in refs[:count]:
        block = ref[...].astype(jnp.float32)
        total += jnp.sum(block, axis=0, keepdims=True)
        square += jnp.sum(block * block, axis=0, keepdims=True)
    if has_earlier:
        total += refs[count][0:1, :]
        square += refs[count][1:2, :]
    out[...] = jnp.zeros_like(out)
    out[0:1, :] = total
    out[1:2, :] = square


def row_sums(pieces, earlier=None):
    rest = () if earlier is None else (earlier,)
    return pl.pallas_call(
        functools.partial(sums_kernel, len(pieces), bool(rest)),
        out_shape=jax.ShapeDtypeStruct((8, pieces[0].shape[1]), jnp.float32),
        in_specs=[VMEM] * (len(pieces) + len(rest)),
        out_specs=VMEM,
        compiler_params=params(),
    )(*pieces, *rest)


def norm_kernel(ids_ref, own_ref, other_ref, table_ref, *refs):
    pieces, normed_ref = refs[:RING], refs[RING]
    feats = pieces[0].shape[0] // 2
    model_width = 4.0 * RING * feats
    stats = own_ref[...] + other_ref[...]
    mean = stats[0:1, :] / model_width
    variance = stats[1:2, :] / model_width - mean * mean
    rstd = lax.rsqrt(variance + EPSILON)
    columns = jnp.transpose(jnp.concatenate([mean, rstd, jnp.zeros((6, mean.shape[1]), jnp.float32)], axis=0))
    mean_col, rstd_col = columns[:, 0:1], columns[:, 1:2]
    blocks = table_ref.shape[0] // 2
    for slot, piece in enumerate(pieces):
        for part in range(2):
            x_at = jnp.where(part == 0, ids_ref[XH], 1 - ids_ref[XH])
            z_at = lax.rem(ids_ref[Z] + slot, RING)
            row = x_at * (2 * RING) + z_at * 2 + ids_ref[CORE]
            shift = table_ref[pl.ds(row, 1), :]
            scale = table_ref[pl.ds(blocks + row, 1), :]
            block = jnp.transpose(piece[part * feats : (part + 1) * feats, :]).astype(jnp.float32)
            block = (block - mean_col) * rstd_col * (1.0 + scale) + shift
            normed_ref[slot, part] = block.astype(jnp.bfloat16)


def add_products(ids_ref, normed_ref, weights, slot, parts):
    y_at = lax.rem(ids_ref[Y] + slot, RING)
    half = y_at // (RING // 2)
    part = jnp.where(half == ids_ref[XH], 0, 1)
    for head in range(2):
        for side in range(2):
            xl_at = ids_ref[XL] if side == 0 else 1 - ids_ref[XL]
            z_at = 2 * (y_at - half * (RING // 2)) + xl_at
            place = lax.rem(z_at + RING - ids_ref[Z], RING)
            product = jnp.dot(normed_ref[place, part], weights[2 * side + head], preferred_element_type=jnp.float32)
            parts[head] = product if parts[head] is None else parts[head] + product


def project_kernel(slots, has_earlier, ids_ref, normed_ref, *refs):
    pieces = refs[: len(slots)]
    out_keep, out_send = refs[-2:]
    if has_earlier:
        parts = [refs[len(slots)][...], refs[len(slots) + 1][...]]
    else:
        parts = [None, None]
    for k, slot in enumerate(slots):
        add_products(ids_ref, normed_ref, pieces[k], slot, parts)
    out_keep[...] = parts[0]
    out_send[...] = parts[1]


def project(ids, normed, slots, pieces, earlier=()):
    part = jax.ShapeDtypeStruct((normed.shape[2], 2 * HD), jnp.float32)
    return pl.pallas_call(
        functools.partial(project_kernel, slots, bool(earlier)),
        out_shape=(part, part),
        in_specs=[SMEM, VMEM] + [VMEM] * (len(pieces) + len(earlier)),
        out_specs=(VMEM, VMEM),
        compiler_params=params(),
    )(ids, normed, *pieces, *earlier)


def join_kernel(mine_ref, theirs_ref, out_ref):
    rows = mine_ref.shape[0]
    total = (mine_ref[...] + theirs_ref[...]).astype(jnp.bfloat16)
    out_ref[0:rows, :] = total[:, 0:HD]
    for b in range(rows // HD):
        out_ref[rows + b * HD : rows + (b + 1) * HD, :] = jnp.transpose(
            total[b * HD : (b + 1) * HD, HD : 2 * HD]
        )


def scan_keys(later, flips, ids_ref, visible_ref, counts_ref, q_t, kv_refs, stat, acc):
    factor = LOG2E * HD ** (-0.5)
    quad, place = ids_ref[YH], ids_ref[PLACE]
    q_span = jnp.minimum((quad + later) * QUAD + place, QUAD * QUAD - 1)
    for flip, kv_ref in zip(flips, kv_refs):
        k_span = quad * QUAD + (place ^ flip)
        span_len = kv_ref.shape[0] // 2
        seen = visible_ref[q_span, k_span] == 1
        if later == 0:
            seen = (k_span == q_span) if flip == 0 else jnp.logical_and(seen, k_span < q_span)
        else:
            seen = jnp.logical_and(seen, quad + later < QUAD)

        @pl.when(seen)
        def _():
            scores = jnp.dot(kv_ref[0:span_len, :], q_t[...], preferred_element_type=jnp.float32)
            live = lax.broadcasted_iota(jnp.int32, scores.shape, 0) < counts_ref[k_span]
            scores = jnp.where(live, scores * factor, NEG_BIG)
            best = stat[0:1, :]
            top = jnp.maximum(best, jnp.max(scores, axis=0, keepdims=True))
            weights = jnp.exp2(scores - top)
            fading = jnp.exp2(best - top)
            stat[8:9, :] = stat[8:9, :] * fading + jnp.sum(weights, axis=0, keepdims=True)
            stat[0:1, :] = top
            values = jnp.concatenate(
                [kv_ref[span_len + b * HD : span_len + (b + 1) * HD, :] for b in range(span_len // HD)], axis=1
            )
            acc[...] = acc[...] * fading + jnp.dot(
                values, weights.astype(jnp.bfloat16), preferred_element_type=jnp.float32
            )


def begin_kernel(ids_ref, visible_ref, counts_ref, q0, q1, q2, q3, kv_ref, q_t, stat, acc):
    for later, q_ref in enumerate((q0, q1, q2, q3)):
        q_t[later] = jnp.transpose(q_ref[...])
        stat[later, 0:8, :] = jnp.full((8, stat.shape[2]), NEG_BIG, jnp.float32)
        stat[later, 8:16, :] = jnp.zeros((8, stat.shape[2]), jnp.float32)
        acc[later] = jnp.zeros(acc.shape[1:], jnp.float32)
        scan_keys(
            later, (0,), ids_ref, visible_ref, counts_ref, q_t.at[later], (kv_ref,), stat.at[later], acc.at[later]
        )


def middle_kernel(ids_ref, visible_ref, counts_ref, q_t, stat_in, acc_in, kv_ref, stat, acc):
    for later in range(QUAD):
        scan_keys(
            later, (1,), ids_ref, visible_ref, counts_ref, q_t.at[later], (kv_ref,), stat.at[later], acc.at[later]
        )


def finish_kernel(later, ids_ref, visible_ref, counts_ref, q_t, stat_in, acc_in, kv2, kv3, out_ref, stat, acc):
    span_len = out_ref.shape[1]

    @pl.when(ids_ref[YH] + later < QUAD)
    def _():
        stat[...] = stat_in[later]
        acc[...] = acc_in[later]
        scan_keys(later, (2, 3), ids_ref, visible_ref, counts_ref, q_t.at[later], (kv2, kv3), stat, acc)
        out_ref[0:HD, :] = acc[...].astype(jnp.bfloat16)
        rows = []
        for value in (stat[0:1, :], stat[8:9, :]):
            for _part in range(3):
                part = value.astype(jnp.bfloat16).astype(jnp.float32)
                rows.append(part)
                value = value - part
        rows.append(jnp.zeros((STAT_ROWS - 6, span_len), jnp.float32))
        out_ref[HD : HD + STAT_ROWS, :] = jnp.concatenate(rows, axis=0).astype(jnp.bfloat16)

    @pl.when(ids_ref[YH] + later >= QUAD)
    def _():
        out_ref[...] = jnp.zeros_like(out_ref)


def merge_kernel(ids_ref, counts_ref, part0, part1, part2, part3, out_ref):
    span_len = out_ref.shape[0]
    parts = (part0, part1, part2, part3)
    bests, totals = [], []
    for earlier, part in enumerate(parts):
        stat = part[HD : HD + STAT_ROWS, :].astype(jnp.float32)
        sent = ids_ref[YH] >= earlier
        bests.append(jnp.where(sent, (stat[0:1] + stat[1:2]) + stat[2:3], NEG_BIG))
        totals.append(jnp.where(sent, (stat[3:4] + stat[4:5]) + stat[5:6], 0.0))
    top = functools.reduce(jnp.maximum, bests)
    share = [jnp.exp2(b - top) for b in bests]
    total = sum(s * t for s, t in zip(share, totals))
    result = sum(s * part[0:HD, :].astype(jnp.float32) for s, part in zip(share, parts))
    slot = lax.broadcasted_iota(jnp.int32, total.shape, 1)
    result = jnp.where(slot < counts_ref[ids_ref[SPAN]], result / total, 0.0)
    out_ref[...] = jnp.transpose(result).astype(jnp.bfloat16)


def on_device(tokens, queries, key_weight, value_weight, modulation, levels, visible, counts):
    span_id = lax.axis_index(SPAN_AXES)
    ids = jnp.stack(
        [
            span_id,
            lax.axis_index("yh"),
            lax.axis_index(("yl", "xl")),
            lax.axis_index(("yh", "yl")),
            lax.axis_index("xl"),
            lax.axis_index("xh"),
            lax.axis_index("z"),
            lax.axis_index("c"),
        ]
    ).astype(jnp.int32)
    span_len, feats = tokens.shape
    depth = key_weight.shape[0] // 2

    w_type = jax.ShapeDtypeStruct((depth, 2 * HD), jnp.bfloat16)
    w_own, w_other = pl.pallas_call(
        split_kernel,
        out_shape=(w_type, w_type),
        in_specs=[SMEM, HBM, HBM],
        out_specs=(VMEM, VMEM),
        scratch_shapes=[pltpu.SemaphoreType.DMA((4,))],
        compiler_params=params(),
    )(ids, key_weight, value_weight)
    w_chip = jnp.stack([w_own, shifted(w_other, "c", 2, 1)])
    w0 = jnp.concatenate([w_chip, shifted(w_chip, "xl", 2, 1)], axis=0)

    a0 = jnp.transpose(tokens)
    x0 = jnp.concatenate([a0, shifted(a0, "xh", 2, 1)], axis=0)

    q_later = [moved(queries, -later) for later in (1, 2, 3)]
    w0, *q_later = lax.optimization_barrier((w0, *q_later))

    x_up, x_down, w_up, w_down = [x0], [x0], [w0], [w0]
    y_axes = ("yh", "yl")
    for step in range(4):
        x_up.append(shifted(x_up[-1], "z", RING, 1))
        if step < 3:
            w_up.append(shifted(w_up[-1], y_axes, RING, 1))
            x_down.append(shifted(x_down[-1], "z", RING, -1))
        w_down.append(shifted(w_down[-1], y_axes, RING, -1))
    x_slots = [x0, x_down[1], x_down[2], x_down[3], x_up[4], x_up[3], x_up[2], x_up[1]]
    w_slots = [w0, w_down[1], w_down[2], w_down[3], w_down[4], w_up[3], w_up[2], w_up[1]]

    early = row_sums(x_slots[:4] + x_slots[5:])
    own_sums = row_sums([x_slots[4]], early)
    other_sums = shifted(own_sums, "c", 2, 1)
    table = pl.pallas_call(
        table_kernel,
        out_shape=jax.ShapeDtypeStruct((modulation.shape[1] // feats, feats), jnp.float32),
        in_specs=[SMEM, SMEM, VMEM],
        out_specs=VMEM,
        compiler_params=params(),
    )(levels, ids, modulation)
    normed = pl.pallas_call(
        norm_kernel,
        out_shape=jax.ShapeDtypeStruct((RING, 2, span_len, feats), jnp.bfloat16),
        in_specs=[SMEM] + [VMEM] * (3 + RING),
        out_specs=VMEM,
        compiler_params=params(),
    )(ids, own_sums, other_sums, table, *x_slots)
    first = (0, 1, 2, 3, 5, 6, 7)
    parts = project(ids, normed, first, [w_slots[s] for s in first])
    mine, theirs = project(ids, normed, (4,), [w_slots[4]], parts)
    kv0 = pl.pallas_call(
        join_kernel,
        out_shape=jax.ShapeDtypeStruct((2 * span_len, HD), jnp.bfloat16),
        in_specs=[VMEM, VMEM],
        out_specs=VMEM,
        compiler_params=params(),
    )(mine, shifted(theirs, "c", 2, 1))

    kv1 = shifted(kv0, "xl", 2, 1)
    kv2 = shifted(kv0, "yl", 2, 1)
    kv3 = lax.ppermute(kv0, ("yl", "xl"), [(i, 3 - i) for i in range(4)])
    scalars = (ids, visible, counts)
    q_type = jax.ShapeDtypeStruct((QUAD, HD, span_len), jnp.bfloat16)
    stat_type = jax.ShapeDtypeStruct((QUAD, 16, span_len), jnp.float32)
    acc_type = jax.ShapeDtypeStruct((QUAD, HD, span_len), jnp.float32)
    q_t, stat, acc = pl.pallas_call(
        begin_kernel,
        out_shape=(q_type, stat_type, acc_type),
        in_specs=[SMEM] * 3 + [VMEM] * 5,
        out_specs=(VMEM,) * 3,
        compiler_params=params(),
    )(*scalars, queries, *q_later, kv0)
    stat, acc = pl.pallas_call(
        middle_kernel,
        out_shape=(stat_type, acc_type),
        in_specs=[SMEM] * 3 + [VMEM] * 4,
        out_specs=(VMEM,) * 2,
        input_output_aliases={4: 0, 5: 1},
        compiler_params=params(),
    )(*scalars, q_t, stat, acc, kv1)
    parts = [None] * QUAD
    for later in (3, 2, 1, 0):
        part = pl.pallas_call(
            functools.partial(finish_kernel, later),
            out_shape=jax.ShapeDtypeStruct((HD + STAT_ROWS, span_len), jnp.bfloat16),
            in_specs=[SMEM] * 3 + [VMEM] * 5,
            out_specs=VMEM,
            scratch_shapes=[pltpu.VMEM((16, span_len), jnp.float32), pltpu.VMEM((HD, span_len), jnp.float32)],
            compiler_params=params(),
        )(*scalars, q_t, stat, acc, kv2, kv3)
        parts[later] = moved(part, later) if later else part
    return pl.pallas_call(
        merge_kernel,
        out_shape=jax.ShapeDtypeStruct((span_len, HD), jnp.bfloat16),
        in_specs=[SMEM, SMEM] + [VMEM] * QUAD,
        out_specs=VMEM,
        compiler_params=params(),
    )(ids, counts, *parts)


def solution(mesh):
    fine = Mesh(mesh.devices.reshape(SIZES), SPAN_AXES + FSDP_AXES)
    spread = P(SPAN_AXES, FSDP_AXES)
    return jax.shard_map(
        on_device,
        mesh=fine,
        in_specs=(spread, spread, spread, spread, P(), P(), P(), P()),
        out_specs=spread,
        check_vma=False,
    )
```

time: 151 us -> 138 us (0.914)
  the two profiles are of different devices: /device:TPU:47 before, /device:TPU:41 now
where the time goes in v3:
time: 138 us; the launch traced here: 137 us
  starting transfers between devices  90.9 us (66%)
  waiting for transfers between devices  24.7 us (18%)
  Pallas kernels  17.8 us (13%)
  local copies, waits for them, and re-layouts  1.93 us (1%)
    ppermute x21, starting transfers between devices, shifted(): lax.ppermute(value, axis, [(i, (i + by) % size) for i in range(size)])  78.4 us
    ppermute x6, waiting for transfers between devices, moved(): lax.ppermute(value, 'yh', [(i, i + by) for i in range(QUAD) if 0 <= i + b...  16.7 us
    ppermute x6, starting transfers between devices, moved(): lax.ppermute(value, 'yh', [(i, i + by) for i in range(QUAD) if 0 <= i + b...  10.6 us
    ppermute x1, waiting for transfers between devices, on_device(): kv3 = lax.ppermute(kv0, ('yl', 'xl'), [(i, 3 - i) for i in range(4)])  5.65 us
    pallas_call x4, Pallas kernels, on_device(): pl.pallas_call(functools.partial(finish_kernel, later), out_shape=jax.Sha...  4.44 us
    pallas_call x2, Pallas kernels, project(): pl.pallas_call(functools.partial(project_kernel, slots, bool(earlier)), o...  3.55 us
  transfers between devices with their start and end apart: 28, of which 8 were waited for; matrix products, arithmetic and copies ran while one was open for 1% of the time, Pallas kernels for 10%

profile of v3, /device:TPU:41, one launch (start us, length us, event | category | flops | bytes accessed | tf_op | source)
XLA Modules:
  0.0 137.0 jit_solution(14725227899624732594)
XLA Ops:
  0.1 0.9 copy-done.3
  1.0 0.9 copy-done.4
  1.9 0.6 shard_map.82
  2.5 2.6 %collective-permute-start = (bf16[192,256]{1,0:T(8,128)(2,1)S(1)}, bf16[192,256]{1,0:T(8,128)(2,1)S(1)}, u32[]{:S(2)}, u32[]{:S(2)}) collective-permute-start(bf16[192,256]{1,0:T(8,128)(2,1)S(1)} %get-tuple-element.21), channel_id=1, source_target_pairs={{0,1},{1,0},{2,3},{3,2},{4,5},{5,4},{6,7},{7,6},{8,9},{9,8},{10,11... | collective-permute-start | bytes 294920 | tf_op jit(solution)/shard_map/ppermute | solution.py:32
  5.1 4.7 %collective-permute-start.5 = (bf16[192,512]{1,0:T(8,128)(2,1)}, bf16[192,512]{1,0:T(8,128)(2,1)S(1)}, u32[]{:S(2)}, u32[]{:S(2)}) collective-permute-start(bf16[192,512]{1,0:T(8,128)(2,1)} %bitcast.15), channel_id=1, source_target_pairs={{0,16},{16,0},{1,17},{17,1},{2,18},{18,2},{3,19},{19,3},{4,20},{20... | collective-permute-start | bytes 589832 | tf_op jit(solution)/shard_map/ppermute | solution.py:32
  9.8 2.2 %collective-permute-start.1 = (bf16[2,192,256]{2,1,0:T(8,128)(2,1)S(1)}, bf16[2,192,256]{2,1,0:T(8,128)(2,1)S(1)}, u32[]{:S(2)}, u32[]{:S(2)}) collective-permute-start(bf16[2,192,256]{2,1,0:T(8,128)(2,1)S(1)} %pad_maximum_fusion.2), channel_id=1, source_target_pairs={{0,32},{32,0},{1,33},{33,1},{2,34},{34,2},{3,35},{35,3},{4,36},{36... | collective-permute-start | bytes 589832 | tf_op jit(solution)/shard_map/ppermute | solution.py:32
  12.1 2.9 %collective-permute-start.2 = (bf16[512,128]{1,0:T(8,128)(2,1)}, bf16[512,128]{1,0:T(8,128)(2,1)S(1)}, u32[]{:S(2)}, u32[]{:S(2)}) collective-permute-start(bf16[512,128]{1,0:T(8,128)(2,1)} %q0.1), channel_id=1, source_target_pairs={{128,0},{256,128},{384,256},{129,1},{257,129},{385,257},{130,2},{2... | collective-permute-start | bytes 393224 | tf_op jit(solution)/shard_map/ppermute | solution.py:36
  14.9 1.3 collective-permute-start.3
  16.2 0.7 collective-permute-start.4
  16.9 1.0 pad_maximum_fusion.1.refs_0_
  17.9 4.0 %collective-permute-start.6 = (bf16[384,512]{1,0:T(8,128)(2,1)S(1)}, bf16[384,512]{1,0:T(8,128)(2,1)S(1)}, u32[]{:S(2)}, u32[]{:S(2)}) collective-permute-start(bf16[384,512]{1,0:T(8,128)(2,1)S(1)} %pad_maximum_fusion.1.refs_0_), channel_id=1, source_target_pairs={{0,2},{2,4},{4,6},{6,8},{8,10},{10,12},{12,14},{14,0},{1,3},{3,5},... | collective-permute-start | bytes 1179656 | tf_op jit(solution)/shard_map/ppermute | solution.py:32
  22.0 3.9 %collective-permute-done.3.q2 = bf16[512,128]{1,0:T(8,128)(2,1)S(1)} collective-permute-done((bf16[512,128]{1,0:T(8,128)(2,1)}, bf16[512,128]{1,0:T(8,128)(2,1)S(1)}, u32[]{:S(2)}, u32[]{:S(2)}) %collective-permute-start.3) | collective-permute-done | bytes 131104 | tf_op jit(solution)/shard_map/ppermute | solution.py:36
  25.9 3.1 %collective-permute-start.14 = (bf16[4,192,256]{2,1,0:T(8,128)(2,1)S(1)}, bf16[4,192,256]{2,1,0:T(8,128)(2,1)S(1)}, u32[]{:S(2)}, u32[]{:S(2)}) collective-permute-start(bf16[4,192,256]{2,1,0:T(8,128)(2,1)S(1)} %pad_maximum_fusion.refs_0_), channel_id=1, source_target_pairs={{0,448},{64,0},{128,64},{192,128},{256,192},{320,256},{384,320},{4... | collective-permute-start | bytes 1179656 | tf_op jit(solution)/shard_map/ppermute | solution.py:32
  29.0 10.7 %collective-permute-start.10 = (bf16[384,512]{1,0:T(8,128)(2,1)S(1)}, bf16[384,512]{1,0:T(8,128)(2,1)S(1)}, u32[]{:S(2)}, u32[]{:S(2)}) collective-permute-start(bf16[384,512]{1,0:T(8,128)(2,1)S(1)} %pad_maximum_fusion.1.refs_0_), channel_id=1, source_target_pairs={{0,14},{2,0},{4,2},{6,4},{8,6},{10,8},{12,10},{14,12},{1,15},{3,1}... | collective-permute-start | bytes 1179656 | tf_op jit(solution)/shard_map/ppermute | solution.py:32
  39.7 1.9 %collective-permute-start.7 = (bf16[384,512]{1,0:T(8,128)(2,1)S(1)}, bf16[384,512]{1,0:T(8,128)(2,1)S(1)}, u32[]{:S(2)}, u32[]{:S(2)}) collective-permute-start(bf16[384,512]{1,0:T(8,128)(2,1)S(1)} %collective-permute-done.6.refs_6_.refs_7_), channel_id=1, source_target_pairs={{0,2},{2,4},{4,6},{6,8},{8,10},{10,12},{12,14},{14,0},{1,3},{3,5},... | collective-permute-start | bytes 1179656 | tf_op jit(solution)/shard_map/ppermute | solution.py:32
  41.6 2.2 %collective-permute-start.18 = (bf16[4,192,256]{2,1,0:T(8,128)(2,1)S(1)}, bf16[4,192,256]{2,1,0:T(8,128)(2,1)S(1)}, u32[]{:S(2)}, u32[]{:S(2)}) collective-permute-start(bf16[4,192,256]{2,1,0:T(8,128)(2,1)S(1)} %pad_maximum_fusion.refs_0_), channel_id=1, source_target_pairs={{0,64},{64,128},{128,192},{192,256},{256,320},{320,384},{384,448},... | collective-permute-start | bytes 1179656 | tf_op jit(solution)/shard_map/ppermute | solution.py:32
  43.8 3.1 %collective-permute-start.15 = (bf16[4,192,256]{2,1,0:T(8,128)(2,1)S(1)}, bf16[4,192,256]{2,1,0:T(8,128)(2,1)S(1)}, u32[]{:S(2)}, u32[]{:S(2)}) collective-permute-start(bf16[4,192,256]{2,1,0:T(8,128)(2,1)S(1)} %collective-permute-done.14.refs_1_), channel_id=1, source_target_pairs={{0,448},{64,0},{128,64},{192,128},{256,192},{320,256},{384,320},{4... | collective-permute-start | bytes 1179656 | tf_op jit(solution)/shard_map/ppermute | solution.py:32
  47.1 5.3 %collective-permute-start.11 = (bf16[384,512]{1,0:T(8,128)(2,1)S(1)}, bf16[384,512]{1,0:T(8,128)(2,1)S(1)}, u32[]{:S(2)}, u32[]{:S(2)}) collective-permute-start(bf16[384,512]{1,0:T(8,128)(2,1)S(1)} %collective-permute-done.10.refs_1_), channel_id=1, source_target_pairs={{0,14},{2,0},{4,2},{6,4},{8,6},{10,8},{12,10},{14,12},{1,15},{3,1}... | collective-permute-start | bytes 1179656 | tf_op jit(solution)/shard_map/ppermute | solution.py:32
  52.5 1.9 %collective-permute-start.8 = (bf16[384,512]{1,0:T(8,128)(2,1)S(1)}, bf16[384,512]{1,0:T(8,128)(2,1)S(1)}, u32[]{:S(2)}, u32[]{:S(2)}) collective-permute-start(bf16[384,512]{1,0:T(8,128)(2,1)S(1)} %collective-permute-done.7.refs_5_.refs_6_), channel_id=1, source_target_pairs={{0,2},{2,4},{4,6},{6,8},{8,10},{10,12},{12,14},{14,0},{1,3},{3,5},... | collective-permute-start | bytes 1179656 | tf_op jit(solution)/shard_map/ppermute | solution.py:32
  54.4 3.4 %collective-permute-start.19 = (bf16[4,192,256]{2,1,0:T(8,128)(2,1)S(1)}, bf16[4,192,256]{2,1,0:T(8,128)(2,1)S(1)}, u32[]{:S(2)}, u32[]{:S(2)}) collective-permute-start(bf16[4,192,256]{2,1,0:T(8,128)(2,1)S(1)} %collective-permute-done.18.refs_6_), channel_id=1, source_target_pairs={{0,64},{64,128},{128,192},{192,256},{256,320},{320,384},{384,448},... | collective-permute-start | bytes 1179656 | tf_op jit(solution)/shard_map/ppermute | solution.py:32
  57.9 1.9 %collective-permute-start.16 = (bf16[4,192,256]{2,1,0:T(8,128)(2,1)S(1)}, bf16[4,192,256]{2,1,0:T(8,128)(2,1)S(1)}, u32[]{:S(2)}, u32[]{:S(2)}) collective-permute-start(bf16[4,192,256]{2,1,0:T(8,128)(2,1)S(1)} %collective-permute-done.15.refs_2_), channel_id=1, source_target_pairs={{0,448},{64,0},{128,64},{192,128},{256,192},{320,256},{384,320},{4... | collective-permute-start | bytes 1179656 | tf_op jit(solution)/shard_map/ppermute | solution.py:32
  59.8 4.6 %collective-permute-start.12 = (bf16[384,512]{1,0:T(8,128)(2,1)S(1)}, bf16[384,512]{1,0:T(8,128)(2,1)S(1)}, u32[]{:S(2)}, u32[]{:S(2)}) collective-permute-start(bf16[384,512]{1,0:T(8,128)(2,1)S(1)} %collective-permute-done.11.refs_2_), channel_id=1, source_target_pairs={{0,14},{2,0},{4,2},{6,4},{8,6},{10,8},{12,10},{14,12},{1,15},{3,1}... | collective-permute-start | bytes 1179656 | tf_op jit(solution)/shard_map/ppermute | solution.py:32
  64.4 1.9 %collective-permute-start.9 = (bf16[384,512]{1,0:T(8,128)(2,1)S(1)}, bf16[384,512]{1,0:T(8,128)(2,1)S(1)}, u32[]{:S(2)}, u32[]{:S(2)}) collective-permute-start(bf16[384,512]{1,0:T(8,128)(2,1)S(1)} %collective-permute-done.8.refs_4_.refs_5_), channel_id=1, source_target_pairs={{0,2},{2,4},{4,6},{6,8},{8,10},{10,12},{12,14},{14,0},{1,3},{3,5},... | collective-permute-start | bytes 1179656 | tf_op jit(solution)/shard_map/ppermute | solution.py:32
  66.3 4.3 %collective-permute-start.20 = (bf16[4,192,256]{2,1,0:T(8,128)(2,1)S(1)}, bf16[4,192,256]{2,1,0:T(8,128)(2,1)S(1)}, u32[]{:S(2)}, u32[]{:S(2)}) collective-permute-start(bf16[4,192,256]{2,1,0:T(8,128)(2,1)S(1)} %collective-permute-done.19.refs_5_), channel_id=1, source_target_pairs={{0,64},{64,128},{128,192},{192,256},{256,320},{320,384},{384,448},... | collective-permute-start | bytes 1179656 | tf_op jit(solution)/shard_map/ppermute | solution.py:32
  70.6 3.5 %collective-permute-start.17 = (bf16[4,192,256]{2,1,0:T(8,128)(2,1)S(1)}, bf16[4,192,256]{2,1,0:T(8,128)(2,1)S(1)}, u32[]{:S(2)}, u32[]{:S(2)}) collective-permute-start(bf16[4,192,256]{2,1,0:T(8,128)(2,1)S(1)} %collective-permute-done.16.refs_3_), channel_id=1, source_target_pairs={{0,448},{64,0},{128,64},{192,128},{256,192},{320,256},{384,320},{4... | collective-permute-start | bytes 1179656 | tf_op jit(solution)/shard_map/ppermute | solution.py:32
  75.0 6.0 %collective-permute-start.13 = (f32[8,512]{1,0:T(8,128)S(1)}, f32[8,512]{1,0:T(8,128)S(1)}, u32[]{:S(2)}, u32[]{:S(2)}) collective-permute-start(f32[8,512]{1,0:T(8,128)S(1)} %shard_map.84.own_ref), channel_id=1, source_target_pairs={{0,1},{1,0},{2,3},{3,2},{4,5},{5,4},{6,7},{7,6},{8,9},{9,8},{10,11... | collective-permute-start | bytes 49160 | tf_op jit(solution)/shard_map/ppermute | solution.py:32
  81.0 0.7 shard_map.85.table_ref
  81.8 2.6 %shard_map.86.normed_ref = bf16[8,2,512,192]{3,2,1,0:T(8,128)(2,1)S(1)} custom-call(s32[8]{0:T(128)S(1)} %stack.44.ids_ref, f32[8,512]{1,0:T(8,128)S(1)} %shard_map.84.own_ref, f32[8,512]{1,0:T(8,128)S(1)} %collective-permute-done.13.other_ref, f32[64,192]{1,0:T(8,128)S(1)} %shard_map.85.table_ref, bf16[384,512]{1,0:T(8,128)(2,1)S(1)} %pad_maximum_fusion.1.refs_0_, ...), custom_call_target="tpu_custom_call" | custom-call | tf_op jit(solution)/shard_map/pallas_call | solution.py:311
  84.4 2.6 %shard_map.87 = (f32[512,256]{1,0:T(8,128)S(1)}, f32[512,256]{1,0:T(8,128)S(1)}) custom-call(s32[8]{0:T(128)S(1)} %stack.44.ids_ref, bf16[8,2,512,192]{3,2,1,0:T(8,128)(2,1)S(1)} %shard_map.86.normed_ref, bf16[4,192,256]{2,1,0:T(8,128)(2,1)S(1)} %pad_maximum_fusion.refs_0_, bf16[4,192,256]{2,1,0:T(8,128)(2,1)S(1)} %collective-permute-done.14.refs_1_, ...), custom_call_target="tpu_custom_call" | custom-call | tf_op jit(solution)/shard_map/pallas_call | solution.py:145
  87.1 1.0 shard_map.88
  88.0 2.3 %collective-permute-start.21 = (f32[512,256]{1,0:T(8,128)S(1)}, f32[512,256]{1,0:T(8,128)S(1)}, u32[]{:S(2)}, u32[]{:S(2)}) collective-permute-start(f32[512,256]{1,0:T(8,128)S(1)} %get-tuple-element.29), channel_id=1, source_target_pairs={{0,1},{1,0},{2,3},{3,2},{4,5},{5,4},{6,7},{7,6},{8,9},{9,8},{10,11... | collective-permute-start | bytes 1572872 | tf_op jit(solution)/shard_map/ppermute | solution.py:32
  90.3 1.5 %collective-permute-done.21.theirs_ref = f32[512,256]{1,0:T(8,128)S(1)} collective-permute-done((f32[512,256]{1,0:T(8,128)S(1)}, f32[512,256]{1,0:T(8,128)S(1)}, u32[]{:S(2)}, u32[]{:S(2)}) %collective-permute-start.21) | collective-permute-done | bytes 524320 | tf_op jit(solution)/shard_map/ppermute | solution.py:32
  91.9 3.1 %collective-permute-start.22 = (bf16[1024,128]{1,0:T(8,128)(2,1)S(1)}, bf16[1024,128]{1,0:T(8,128)(2,1)S(1)}, u32[]{:S(2)}, u32[]{:S(2)}) collective-permute-start(bf16[1024,128]{1,0:T(8,128)(2,1)S(1)} %shard_map.89.kv_ref), channel_id=1, source_target_pairs={{0,32},{32,0},{1,33},{33,1},{2,34},{34,2},{3,35},{35,3},{4,36},{36... | collective-permute-start | bytes 786440 | tf_op jit(solution)/shard_map/ppermute | solution.py:32
  95.0 5.8 %collective-permute-start.23 = (bf16[1024,128]{1,0:T(8,128)(2,1)S(1)}, bf16[1024,128]{1,0:T(8,128)(2,1)S(1)}, u32[]{:S(2)}, u32[]{:S(2)}) collective-permute-start(bf16[1024,128]{1,0:T(8,128)(2,1)S(1)} %shard_map.89.kv_ref), channel_id=1, source_target_pairs={{0,64},{64,0},{1,65},{65,1},{2,66},{66,2},{3,67},{67,3},{4,68},{68... | collective-permute-start | bytes 786440 | tf_op jit(solution)/shard_map/ppermute | solution.py:32
  100.8 2.0 %collective-permute-start.24 = (bf16[1024,128]{1,0:T(8,128)(2,1)S(1)}, bf16[1024,128]{1,0:T(8,128)(2,1)S(1)}, u32[]{:S(2)}, u32[]{:S(2)}) collective-permute-start(bf16[1024,128]{1,0:T(8,128)(2,1)S(1)} %shard_map.89.kv_ref), channel_id=1, source_target_pairs={{0,96},{32,64},{64,32},{96,0},{1,97},{33,65},{65,33},{97,1},{2,98}... | collective-permute-start | bytes 786440 | tf_op jit(solution)/shard_map/ppermute | solution.py:331
  102.8 2.4 %shard_map.90 = (bf16[4,128,512]{2,1,0:T(8,128)(2,1)S(1)}, f32[4,16,512]{2,1,0:T(8,128)S(1)}, f32[4,128,512]{2,1,0:T(8,128)S(1)}) custom-call(s32[8]{0:T(128)S(1)} %stack.44.ids_ref, s32[16,16]{1,0:T(8,128)S(1)} %copy-done, s32[16]{0:T(128)S(1)} %copy-done.5, bf16[512,128]{1,0:T(8,128)(2,1)S(1)} %copy-done.2, ...), custom_call_target="tpu_custom_call" | custom-call | tf_op jit(solution)/shard_map/pallas_call | solution.py:336
  105.2 1.4 %shard_map.91 = (f32[4,16,512]{2,1,0:T(8,128)S(1)}, f32[4,128,512]{2,1,0:T(8,128)S(1)}) custom-call(s32[8]{0:T(128)S(1)} %stack.44.ids_ref, s32[16,16]{1,0:T(8,128)S(1)} %copy-done, s32[16]{0:T(128)S(1)} %copy-done.5, bf16[4,128,512]{2,1,0:T(8,128)(2,1)S(1)} %get-tuple-element.30.q_t, ...), custom_call_target="tpu_custom_call", output_to_operand_aliasing={{0}: (4, {}), {1}: (5, {})} | custom-call | tf_op jit(solution)/shard_map/pallas_call | solution.py:343
  106.9 5.6 %collective-permute-done.24.kv3 = bf16[1024,128]{1,0:T(8,128)(2,1)S(1)} collective-permute-done((bf16[1024,128]{1,0:T(8,128)(2,1)S(1)}, bf16[1024,128]{1,0:T(8,128)(2,1)S(1)}, u32[]{:S(2)}, u32[]{:S(2)}) %collective-permute-start.24) | collective-permute-done | bytes 262176 | tf_op jit(solution)/shard_map/ppermute | solution.py:331
  112.6 0.9 shard_map.95
  113.4 0.7 collective-permute-start.27
  114.1 0.7 shard_map.94
  114.8 1.3 collective-permute-start.26
  116.1 1.4 %shard_map.93 = bf16[144,512]{1,0:T(8,128)(2,1)S(1)} custom-call(s32[8]{0:T(128)S(1)} %stack.44.ids_ref, s32[16,16]{1,0:T(8,128)S(1)} %copy-done, s32[16]{0:T(128)S(1)} %copy-done.5, bf16[4,128,512]{2,1,0:T(8,128)(2,1)S(1)} %get-tuple-element.30.q_t, f32[4,16,512]{2,1,0:T(8,128)S(1)} %get-tuple-element.33.stat_in, ...), custom_call_target="tpu_custom_call" | custom-call | tf_op jit(solution)/shard_map/pallas_call | solution.py:353
  117.6 3.8 %collective-permute-start.25 = (bf16[144,512]{1,0:T(8,128)(2,1)S(1)}, bf16[144,512]{1,0:T(8,128)(2,1)S(1)}, u32[]{:S(2)}, u32[]{:S(2)}) collective-permute-start(bf16[144,512]{1,0:T(8,128)(2,1)S(1)} %shard_map.93), channel_id=1, source_target_pairs={{0,128},{128,256},{256,384},{1,129},{129,257},{257,385},{2,130},{1... | collective-permute-start | bytes 442376 | tf_op jit(solution)/shard_map/ppermute | solution.py:36
  121.3 1.4 %shard_map.92.part0 = bf16[144,512]{1,0:T(8,128)(2,1)S(1)} custom-call(s32[8]{0:T(128)S(1)} %stack.44.ids_ref, s32[16,16]{1,0:T(8,128)S(1)} %copy-done, s32[16]{0:T(128)S(1)} %copy-done.5, bf16[4,128,512]{2,1,0:T(8,128)(2,1)S(1)} %get-tuple-element.30.q_t, f32[4,16,512]{2,1,0:T(8,128)S(1)} %get-tuple-element.33.stat_in, ...), custom_call_target="tpu_custom_call" | custom-call | tf_op jit(solution)/shard_map/pallas_call | solution.py:353
  122.8 8.4 %collective-permute-done.26.part2 = bf16[144,512]{1,0:T(8,128)(2,1)S(1)} collective-permute-done((bf16[144,512]{1,0:T(8,128)(2,1)S(1)}, bf16[144,512]{1,0:T(8,128)(2,1)S(1)}, u32[]{:S(2)}, u32[]{:S(2)}) %collective-permute-start.26) | collective-permute-done | bytes 147488 | tf_op jit(solution)/shard_map/ppermute | solution.py:36
  131.2 4.3 %collective-permute-done.25.part1 = bf16[144,512]{1,0:T(8,128)(2,1)S(1)} collective-permute-done((bf16[144,512]{1,0:T(8,128)(2,1)S(1)}, bf16[144,512]{1,0:T(8,128)(2,1)S(1)}, u32[]{:S(2)}, u32[]{:S(2)}) %collective-permute-start.25) | collective-permute-done | bytes 147488 | tf_op jit(solution)/shard_map/ppermute | solution.py:36
  135.5 1.4 %shard_map.96 = bf16[512,128]{1,0:T(8,128)(2,1)} custom-call(s32[8]{0:T(128)S(1)} %stack.44.ids_ref, s32[16]{0:T(128)S(1)} %copy-done.5, bf16[144,512]{1,0:T(8,128)(2,1)S(1)} %shard_map.92.part0, bf16[144,512]{1,0:T(8,128)(2,1)S(1)} %collective-permute-done.25.part1, bf16[144,512]{1,0:T(8,128)(2,1)S(1)} %collective-permute-done.26.part2, ...), custom_call_target="tpu_custom_call" | custom-call | tf_op jit(solution)/shard_map/pallas_call | solution.py:362
  (41 shorter events, 1.7 us)
Async XLA Ops:
  0.0 81.0 %copy-start.1 = (bf16[8,12288]{1,0:T(8,128)(2,1)S(1)}, bf16[8,12288]{1,0:T(8,128)(2,1)}, u32[]{:S(2)}) copy-start(bf16[8,12288]{1,0:T(8,128)(2,1)} %modulation_ref.1) | copy-start | bytes 589828
  0.1 0.9 copy-start.3
  1.0 0.9 copy-start.4
  1.9 79.1 %copy-start.6 = (s32[16]{0:T(128)S(1)}, s32[16]{0:T(128)}, u32[]{:S(2)}) copy-start(s32[16]{0:T(128)} %levels_ref.1) | copy-start | bytes 196
  2.5 7.3 %collective-permute-start = (bf16[192,256]{1,0:T(8,128)(2,1)S(1)}, bf16[192,256]{1,0:T(8,128)(2,1)S(1)}, u32[]{:S(2)}, u32[]{:S(2)}) collective-permute-start(bf16[192,256]{1,0:T(8,128)(2,1)S(1)} %get-tuple-element.21), channel_id=1, source_target_pairs={{0,1},{1,0},{2,3},{3,2},{4,5},{5,4},{6,7},{7,6},{8,9},{9,8},{10,11... | collective-permute-start | bytes 294920 | tf_op jit(solution)/shard_map/ppermute | solution.py:32
  5.1 11.8 %collective-permute-start.5 = (bf16[192,512]{1,0:T(8,128)(2,1)}, bf16[192,512]{1,0:T(8,128)(2,1)S(1)}, u32[]{:S(2)}, u32[]{:S(2)}) collective-permute-start(bf16[192,512]{1,0:T(8,128)(2,1)} %bitcast.15), channel_id=1, source_target_pairs={{0,16},{16,0},{1,17},{17,1},{2,18},{18,2},{3,19},{19,3},{4,20},{20... | collective-permute-start | bytes 589832 | tf_op jit(solution)/shard_map/ppermute | solution.py:32
  9.8 12.1 %collective-permute-start.1 = (bf16[2,192,256]{2,1,0:T(8,128)(2,1)S(1)}, bf16[2,192,256]{2,1,0:T(8,128)(2,1)S(1)}, u32[]{:S(2)}, u32[]{:S(2)}) collective-permute-start(bf16[2,192,256]{2,1,0:T(8,128)(2,1)S(1)} %pad_maximum_fusion.2), channel_id=1, source_target_pairs={{0,32},{32,0},{1,33},{33,1},{2,34},{34,2},{3,35},{35,3},{4,36},{36... | collective-permute-start | bytes 589832 | tf_op jit(solution)/shard_map/ppermute | solution.py:32
  12.1 9.9 %collective-permute-start.2 = (bf16[512,128]{1,0:T(8,128)(2,1)}, bf16[512,128]{1,0:T(8,128)(2,1)S(1)}, u32[]{:S(2)}, u32[]{:S(2)}) collective-permute-start(bf16[512,128]{1,0:T(8,128)(2,1)} %q0.1), channel_id=1, source_target_pairs={{128,0},{256,128},{384,256},{129,1},{257,129},{385,257},{130,2},{2... | collective-permute-start | bytes 393224 | tf_op jit(solution)/shard_map/ppermute | solution.py:36
  14.9 11.0 %collective-permute-start.3 = (bf16[512,128]{1,0:T(8,128)(2,1)}, bf16[512,128]{1,0:T(8,128)(2,1)S(1)}, u32[]{:S(2)}, u32[]{:S(2)}) collective-permute-start(bf16[512,128]{1,0:T(8,128)(2,1)} %q0.1), channel_id=1, source_target_pairs={{256,0},{384,128},{257,1},{385,129},{258,2},{386,130},{259,3},{387... | collective-permute-start | bytes 393224 | tf_op jit(solution)/shard_map/ppermute | solution.py:36
  16.2 9.7 %collective-permute-start.4 = (bf16[512,128]{1,0:T(8,128)(2,1)}, bf16[512,128]{1,0:T(8,128)(2,1)S(1)}, u32[]{:S(2)}, u32[]{:S(2)}) collective-permute-start(bf16[512,128]{1,0:T(8,128)(2,1)} %q0.1), channel_id=1, source_target_pairs={{384,0},{385,1},{386,2},{387,3},{388,4},{389,5},{390,6},{391,7},{3... | collective-permute-start | bytes 393224 | tf_op jit(solution)/shard_map/ppermute | solution.py:36
  17.9 21.8 %collective-permute-start.6 = (bf16[384,512]{1,0:T(8,128)(2,1)S(1)}, bf16[384,512]{1,0:T(8,128)(2,1)S(1)}, u32[]{:S(2)}, u32[]{:S(2)}) collective-permute-start(bf16[384,512]{1,0:T(8,128)(2,1)S(1)} %pad_maximum_fusion.1.refs_0_), channel_id=1, source_target_pairs={{0,2},{2,4},{4,6},{6,8},{8,10},{10,12},{12,14},{14,0},{1,3},{3,5},... | collective-permute-start | bytes 1179656 | tf_op jit(solution)/shard_map/ppermute | solution.py:32
  25.9 17.9 %collective-permute-start.14 = (bf16[4,192,256]{2,1,0:T(8,128)(2,1)S(1)}, bf16[4,192,256]{2,1,0:T(8,128)(2,1)S(1)}, u32[]{:S(2)}, u32[]{:S(2)}) collective-permute-start(bf16[4,192,256]{2,1,0:T(8,128)(2,1)S(1)} %pad_maximum_fusion.refs_0_), channel_id=1, source_target_pairs={{0,448},{64,0},{128,64},{192,128},{256,192},{320,256},{384,320},{4... | collective-permute-start | bytes 1179656 | tf_op jit(solution)/shard_map/ppermute | solution.py:32
  29.0 18.1 %collective-permute-start.10 = (bf16[384,512]{1,0:T(8,128)(2,1)S(1)}, bf16[384,512]{1,0:T(8,128)(2,1)S(1)}, u32[]{:S(2)}, u32[]{:S(2)}) collective-permute-start(bf16[384,512]{1,0:T(8,128)(2,1)S(1)} %pad_maximum_fusion.1.refs_0_), channel_id=1, source_target_pairs={{0,14},{2,0},{4,2},{6,4},{8,6},{10,8},{12,10},{14,12},{1,15},{3,1}... | collective-permute-start | bytes 1179656 | tf_op jit(solution)/shard_map/ppermute | solution.py:32
  39.7 12.8 %collective-permute-start.7 = (bf16[384,512]{1,0:T(8,128)(2,1)S(1)}, bf16[384,512]{1,0:T(8,128)(2,1)S(1)}, u32[]{:S(2)}, u32[]{:S(2)}) collective-permute-start(bf16[384,512]{1,0:T(8,128)(2,1)S(1)} %collective-permute-done.6.refs_6_.refs_7_), channel_id=1, source_target_pairs={{0,2},{2,4},{4,6},{6,8},{8,10},{10,12},{12,14},{14,0},{1,3},{3,5},... | collective-permute-start | bytes 1179656 | tf_op jit(solution)/shard_map/ppermute | solution.py:32
  41.6 12.8 %collective-permute-start.18 = (bf16[4,192,256]{2,1,0:T(8,128)(2,1)S(1)}, bf16[4,192,256]{2,1,0:T(8,128)(2,1)S(1)}, u32[]{:S(2)}, u32[]{:S(2)}) collective-permute-start(bf16[4,192,256]{2,1,0:T(8,128)(2,1)S(1)} %pad_maximum_fusion.refs_0_), channel_id=1, source_target_pairs={{0,64},{64,128},{128,192},{192,256},{256,320},{320,384},{384,448},... | collective-permute-start | bytes 1179656 | tf_op jit(solution)/shard_map/ppermute | solution.py:32
  43.8 14.0 %collective-permute-start.15 = (bf16[4,192,256]{2,1,0:T(8,128)(2,1)S(1)}, bf16[4,192,256]{2,1,0:T(8,128)(2,1)S(1)}, u32[]{:S(2)}, u32[]{:S(2)}) collective-permute-start(bf16[4,192,256]{2,1,0:T(8,128)(2,1)S(1)} %collective-permute-done.14.refs_1_), channel_id=1, source_target_pairs={{0,448},{64,0},{128,64},{192,128},{256,192},{320,256},{384,320},{4... | collective-permute-start | bytes 1179656 | tf_op jit(solution)/shard_map/ppermute | solution.py:32
  47.1 12.6 %collective-permute-start.11 = (bf16[384,512]{1,0:T(8,128)(2,1)S(1)}, bf16[384,512]{1,0:T(8,128)(2,1)S(1)}, u32[]{:S(2)}, u32[]{:S(2)}) collective-permute-start(bf16[384,512]{1,0:T(8,128)(2,1)S(1)} %collective-permute-done.10.refs_1_), channel_id=1, source_target_pairs={{0,14},{2,0},{4,2},{6,4},{8,6},{10,8},{12,10},{14,12},{1,15},{3,1}... | collective-permute-start | bytes 1179656 | tf_op jit(solution)/shard_map/ppermute | solution.py:32
  52.5 11.9 %collective-permute-start.8 = (bf16[384,512]{1,0:T(8,128)(2,1)S(1)}, bf16[384,512]{1,0:T(8,128)(2,1)S(1)}, u32[]{:S(2)}, u32[]{:S(2)}) collective-permute-start(bf16[384,512]{1,0:T(8,128)(2,1)S(1)} %collective-permute-done.7.refs_5_.refs_6_), channel_id=1, source_target_pairs={{0,2},{2,4},{4,6},{6,8},{8,10},{10,12},{12,14},{14,0},{1,3},{3,5},... | collective-permute-start | bytes 1179656 | tf_op jit(solution)/shard_map/ppermute | solution.py:32
  54.4 11.9 %collective-permute-start.19 = (bf16[4,192,256]{2,1,0:T(8,128)(2,1)S(1)}, bf16[4,192,256]{2,1,0:T(8,128)(2,1)S(1)}, u32[]{:S(2)}, u32[]{:S(2)}) collective-permute-start(bf16[4,192,256]{2,1,0:T(8,128)(2,1)S(1)} %collective-permute-done.18.refs_6_), channel_id=1, source_target_pairs={{0,64},{64,128},{128,192},{192,256},{256,320},{320,384},{384,448},... | collective-permute-start | bytes 1179656 | tf_op jit(solution)/shard_map/ppermute | solution.py:32
  57.9 12.7 %collective-permute-start.16 = (bf16[4,192,256]{2,1,0:T(8,128)(2,1)S(1)}, bf16[4,192,256]{2,1,0:T(8,128)(2,1)S(1)}, u32[]{:S(2)}, u32[]{:S(2)}) collective-permute-start(bf16[4,192,256]{2,1,0:T(8,128)(2,1)S(1)} %collective-permute-done.15.refs_2_), channel_id=1, source_target_pairs={{0,448},{64,0},{128,64},{192,128},{256,192},{320,256},{384,320},{4... | collective-permute-start | bytes 1179656 | tf_op jit(solution)/shard_map/ppermute | solution.py:32
  59.8 14.3 %collective-permute-start.12 = (bf16[384,512]{1,0:T(8,128)(2,1)S(1)}, bf16[384,512]{1,0:T(8,128)(2,1)S(1)}, u32[]{:S(2)}, u32[]{:S(2)}) collective-permute-start(bf16[384,512]{1,0:T(8,128)(2,1)S(1)} %collective-permute-done.11.refs_2_), channel_id=1, source_target_pairs={{0,14},{2,0},{4,2},{6,4},{8,6},{10,8},{12,10},{14,12},{1,15},{3,1}... | collective-permute-start | bytes 1179656 | tf_op jit(solution)/shard_map/ppermute | solution.py:32
  64.4 10.5 %collective-permute-start.9 = (bf16[384,512]{1,0:T(8,128)(2,1)S(1)}, bf16[384,512]{1,0:T(8,128)(2,1)S(1)}, u32[]{:S(2)}, u32[]{:S(2)}) collective-permute-start(bf16[384,512]{1,0:T(8,128)(2,1)S(1)} %collective-permute-done.8.refs_4_.refs_5_), channel_id=1, source_target_pairs={{0,2},{2,4},{4,6},{6,8},{8,10},{10,12},{12,14},{14,0},{1,3},{3,5},... | collective-permute-start | bytes 1179656 | tf_op jit(solution)/shard_map/ppermute | solution.py:32
  66.3 18.1 %collective-permute-start.20 = (bf16[4,192,256]{2,1,0:T(8,128)(2,1)S(1)}, bf16[4,192,256]{2,1,0:T(8,128)(2,1)S(1)}, u32[]{:S(2)}, u32[]{:S(2)}) collective-permute-start(bf16[4,192,256]{2,1,0:T(8,128)(2,1)S(1)} %collective-permute-done.19.refs_5_), channel_id=1, source_target_pairs={{0,64},{64,128},{128,192},{192,256},{256,320},{320,384},{384,448},... | collective-permute-start | bytes 1179656 | tf_op jit(solution)/shard_map/ppermute | solution.py:32
  70.6 16.5 %collective-permute-start.17 = (bf16[4,192,256]{2,1,0:T(8,128)(2,1)S(1)}, bf16[4,192,256]{2,1,0:T(8,128)(2,1)S(1)}, u32[]{:S(2)}, u32[]{:S(2)}) collective-permute-start(bf16[4,192,256]{2,1,0:T(8,128)(2,1)S(1)} %collective-permute-done.16.refs_3_), channel_id=1, source_target_pairs={{0,448},{64,0},{128,64},{192,128},{256,192},{320,256},{384,320},{4... | collective-permute-start | bytes 1179656 | tf_op jit(solution)/shard_map/ppermute | solution.py:32
  75.0 6.9 %collective-permute-start.13 = (f32[8,512]{1,0:T(8,128)S(1)}, f32[8,512]{1,0:T(8,128)S(1)}, u32[]{:S(2)}, u32[]{:S(2)}) collective-permute-start(f32[8,512]{1,0:T(8,128)S(1)} %shard_map.84.own_ref), channel_id=1, source_target_pairs={{0,1},{1,0},{2,3},{3,2},{4,5},{5,4},{6,7},{7,6},{8,9},{9,8},{10,11... | collective-permute-start | bytes 49160 | tf_op jit(solution)/shard_map/ppermute | solution.py:32
  87.0 15.8 %copy-start = (s32[16,16]{1,0:T(8,128)S(1)}, s32[16,16]{1,0:T(8,128)}, u32[]{:S(2)}) copy-start(s32[16,16]{1,0:T(8,128)} %visible_ref.11) | copy-start | bytes 3076
  87.0 15.8 %copy-start.2 = (bf16[512,128]{1,0:T(8,128)(2,1)S(1)}, bf16[512,128]{1,0:T(8,128)(2,1)}, u32[]{:S(2)}) copy-start(bf16[512,128]{1,0:T(8,128)(2,1)} %q0.1) | copy-start | bytes 393220
  87.0 15.8 %copy-start.5 = (s32[16]{0:T(128)S(1)}, s32[16]{0:T(128)}, u32[]{:S(2)}) copy-start(s32[16]{0:T(128)} %counts_ref.13) | copy-start | bytes 196
  88.0 3.8 %collective-permute-start.21 = (f32[512,256]{1,0:T(8,128)S(1)}, f32[512,256]{1,0:T(8,128)S(1)}, u32[]{:S(2)}, u32[]{:S(2)}) collective-permute-start(f32[512,256]{1,0:T(8,128)S(1)} %get-tuple-element.29), channel_id=1, source_target_pairs={{0,1},{1,0},{2,3},{3,2},{4,5},{5,4},{6,7},{7,6},{8,9},{9,8},{10,11... | collective-permute-start | bytes 1572872 | tf_op jit(solution)/shard_map/ppermute | solution.py:32
  91.9 13.3 %collective-permute-start.22 = (bf16[1024,128]{1,0:T(8,128)(2,1)S(1)}, bf16[1024,128]{1,0:T(8,128)(2,1)S(1)}, u32[]{:S(2)}, u32[]{:S(2)}) collective-permute-start(bf16[1024,128]{1,0:T(8,128)(2,1)S(1)} %shard_map.89.kv_ref), channel_id=1, source_target_pairs={{0,32},{32,0},{1,33},{33,1},{2,34},{34,2},{3,35},{35,3},{4,36},{36... | collective-permute-start | bytes 786440 | tf_op jit(solution)/shard_map/ppermute | solution.py:32
  95.0 11.9 %collective-permute-start.23 = (bf16[1024,128]{1,0:T(8,128)(2,1)S(1)}, bf16[1024,128]{1,0:T(8,128)(2,1)S(1)}, u32[]{:S(2)}, u32[]{:S(2)}) collective-permute-start(bf16[1024,128]{1,0:T(8,128)(2,1)S(1)} %shard_map.89.kv_ref), channel_id=1, source_target_pairs={{0,64},{64,0},{1,65},{65,1},{2,66},{66,2},{3,67},{67,3},{4,68},{68... | collective-permute-start | bytes 786440 | tf_op jit(solution)/shard_map/ppermute | solution.py:32
  100.8 11.7 %collective-permute-start.24 = (bf16[1024,128]{1,0:T(8,128)(2,1)S(1)}, bf16[1024,128]{1,0:T(8,128)(2,1)S(1)}, u32[]{:S(2)}, u32[]{:S(2)}) collective-permute-start(bf16[1024,128]{1,0:T(8,128)(2,1)S(1)} %shard_map.89.kv_ref), channel_id=1, source_target_pairs={{0,96},{32,64},{64,32},{96,0},{1,97},{33,65},{65,33},{97,1},{2,98}... | collective-permute-start | bytes 786440 | tf_op jit(solution)/shard_map/ppermute | solution.py:331
  113.4 9.3 %collective-permute-start.27 = (bf16[144,512]{1,0:T(8,128)(2,1)S(1)}, bf16[144,512]{1,0:T(8,128)(2,1)S(1)}, u32[]{:S(2)}, u32[]{:S(2)}) collective-permute-start(bf16[144,512]{1,0:T(8,128)(2,1)S(1)} %shard_map.95), channel_id=1, source_target_pairs={{0,384},{1,385},{2,386},{3,387},{4,388},{5,389},{6,390},{7,391},{8... | collective-permute-start | bytes 442376 | tf_op jit(solution)/shard_map/ppermute | solution.py:36
  114.8 16.4 %collective-permute-start.26 = (bf16[144,512]{1,0:T(8,128)(2,1)S(1)}, bf16[144,512]{1,0:T(8,128)(2,1)S(1)}, u32[]{:S(2)}, u32[]{:S(2)}) collective-permute-start(bf16[144,512]{1,0:T(8,128)(2,1)S(1)} %shard_map.94), channel_id=1, source_target_pairs={{0,256},{128,384},{1,257},{129,385},{2,258},{130,386},{3,259},{131... | collective-permute-start | bytes 442376 | tf_op jit(solution)/shard_map/ppermute | solution.py:36
  117.6 18.0 %collective-permute-start.25 = (bf16[144,512]{1,0:T(8,128)(2,1)S(1)}, bf16[144,512]{1,0:T(8,128)(2,1)S(1)}, u32[]{:S(2)}, u32[]{:S(2)}) collective-permute-start(bf16[144,512]{1,0:T(8,128)(2,1)S(1)} %shard_map.93), channel_id=1, source_target_pairs={{0,128},{128,256},{256,384},{1,129},{129,257},{257,385},{2,130},{1... | collective-permute-start | bytes 442376 | tf_op jit(solution)/shard_map/ppermute | solution.py:36

commit v4 on v3

--- a/solution.py
+++ b/solution.py
@@ -21,7 +21,6 @@
 
 VMEM = pl.BlockSpec(memory_space=pltpu.VMEM)
 SMEM = pl.BlockSpec(memory_space=pltpu.SMEM)
-HBM = pl.BlockSpec(memory_space=pltpu.HBM)
 
 
 def params(mib=12):
@@ -32,27 +31,25 @@
     return lax.ppermute(value, axis, [(i, (i + by) % size) for i in range(size)])
 
 
+def turned(place, later):
+    return place ^ 2 if later == 2 else place
+
+
 def moved(value, by):
-    return lax.ppermute(value, "yh", [(i, i + by) for i in range(QUAD) if 0 <= i + by < QUAD])
-
-
-def split_kernel(ids_ref, key_ref, value_ref, own_ref, other_ref, sems):
+    pairs = []
+    for yh in range(QUAD):
+        for yl in range(2):
+            if 0 <= yh + by < QUAD:
+                pairs.append((2 * yh + yl, 2 * (yh + by) + turned(2 * yl, abs(by)) // 2))
+    return lax.ppermute(value, ("yh", "yl"), pairs)
+
+
+def split_kernel(ids_ref, key_ref, value_ref, own_ref, other_ref):
     rows = own_ref.shape[0]
-    copies = []
-    for part, out in ((1 - ids_ref[CORE], other_ref), (ids_ref[CORE], own_ref)):
+    for part, out in ((ids_ref[CORE], own_ref), (1 - ids_ref[CORE], other_ref)):
         first = pl.multiple_of(part * rows, 16)
-        for column, ref in enumerate((key_ref, value_ref)):
-            copies.append(
-                pltpu.make_async_copy(
-                    ref.at[pl.ds(first, rows), :],
-                    out.at[:, pl.ds(column * HD, HD)],
-                    sems.at[len(copies)],
-                )
-            )
-    for copy in copies:
-        copy.start()
-    for copy in copies:
-        copy.wait()
+        out[:, 0:HD] = key_ref[pl.ds(first, rows), :]
+        out[:, HD : 2 * HD] = value_ref[pl.ds(first, rows), :]
 
 
 def table_kernel(levels_ref, ids_ref, modulation_ref, out_ref):
@@ -114,41 +111,33 @@
             normed_ref[slot, part] = block.astype(jnp.bfloat16)
 
 
-def add_products(ids_ref, normed_ref, weights, slot, parts):
-    y_at = lax.rem(ids_ref[Y] + slot, RING)
-    half = y_at // (RING // 2)
-    part = jnp.where(half == ids_ref[XH], 0, 1)
-    for head in range(2):
+def project_kernel(head, ids_ref, normed_ref, *refs):
+    pieces, out_ref = refs[:RING], refs[RING]
+    for slot, weights in enumerate(pieces):
+        y_at = lax.rem(ids_ref[Y] + slot, RING)
+        half = y_at // (RING // 2)
+        part = jnp.where(half == ids_ref[XH], 0, 1)
+        product = None
         for side in range(2):
             xl_at = ids_ref[XL] if side == 0 else 1 - ids_ref[XL]
             z_at = 2 * (y_at - half * (RING // 2)) + xl_at
             place = lax.rem(z_at + RING - ids_ref[Z], RING)
-            product = jnp.dot(normed_ref[place, part], weights[2 * side + head], preferred_element_type=jnp.float32)
-            parts[head] = product if parts[head] is None else parts[head] + product
-
-
-def project_kernel(slots, has_earlier, ids_ref, normed_ref, *refs):
-    pieces = refs[: len(slots)]
-    out_keep, out_send = refs[-2:]
-    if has_earlier:
-        parts = [refs[len(slots)][...], refs[len(slots) + 1][...]]
-    else:
-        parts = [None, None]
-    for k, slot in enumerate(slots):
-        add_products(ids_ref, normed_ref, pieces[k], slot, parts)
-    out_keep[...] = parts[0]
-    out_send[...] = parts[1]
-
-
-def project(ids, normed, slots, pieces, earlier=()):
-    part = jax.ShapeDtypeStruct((normed.shape[2], 2 * HD), jnp.float32)
+            term = jnp.dot(normed_ref[place, part], weights[2 * side + head], preferred_element_type=jnp.float32)
+            product = term if product is None else product + term
+        if slot == 0:
+            out_ref[...] = product
+        else:
+            out_ref[...] += product
+
+
+def project(head, ids, normed, pieces):
     return pl.pallas_call(
-        functools.partial(project_kernel, slots, bool(earlier)),
-        out_shape=(part, part),
-        in_specs=[SMEM, VMEM] + [VMEM] * (len(pieces) + len(earlier)),
-        out_specs=(VMEM, VMEM),
-        compiler_params=params(),
-    )(ids, normed, *pieces, *earlier)
+        functools.partial(project_kernel, head),
+        out_shape=jax.ShapeDtypeStruct((normed.shape[2], 2 * HD), jnp.float32),
+        in_specs=[SMEM] + [VMEM] * (1 + RING),
+        out_specs=VMEM,
+        compiler_params=params(),
+    )(ids, normed, *pieces)
 
 
 def join_kernel(mine_ref, theirs_ref, out_ref):
@@ -164,7 +153,7 @@
 def scan_keys(later, flips, ids_ref, visible_ref, counts_ref, q_t, kv_refs, stat, acc):
     factor = LOG2E * HD ** (-0.5)
     quad, place = ids_ref[YH], ids_ref[PLACE]
-    q_span = jnp.minimum((quad + later) * QUAD + place, QUAD * QUAD - 1)
+    q_span = jnp.minimum((quad + later) * QUAD + turned(place, later), QUAD * QUAD - 1)
     for flip, kv_ref in zip(flips, kv_refs):
         k_span = quad * QUAD + (place ^ flip)
         span_len = kv_ref.shape[0] // 2
@@ -207,18 +196,18 @@
 def middle_kernel(ids_ref, visible_ref, counts_ref, q_t, stat_in, acc_in, kv_ref, stat, acc):
     for later in range(QUAD):
         scan_keys(
-            later, (1,), ids_ref, visible_ref, counts_ref, q_t.at[later], (kv_ref,), stat.at[later], acc.at[later]
+            later, (2,), ids_ref, visible_ref, counts_ref, q_t.at[later], (kv_ref,), stat.at[later], acc.at[later]
         )
 
 
-def finish_kernel(later, ids_ref, visible_ref, counts_ref, q_t, stat_in, acc_in, kv2, kv3, out_ref, stat, acc):
+def finish_kernel(later, ids_ref, visible_ref, counts_ref, q_t, stat_in, acc_in, kv1, kv3, out_ref, stat, acc):
     span_len = out_ref.shape[1]
 
     @pl.when(ids_ref[YH] + later < QUAD)
     def _():
         stat[...] = stat_in[later]
         acc[...] = acc_in[later]
-        scan_keys(later, (2, 3), ids_ref, visible_ref, counts_ref, q_t.at[later], (kv2, kv3), stat, acc)
+        scan_keys(later, (1, 3), ids_ref, visible_ref, counts_ref, q_t.at[later], (kv1, kv3), stat, acc)
         out_ref[0:HD, :] = acc[...].astype(jnp.bfloat16)
         rows = []
         for value in (stat[0:1, :], stat[8:9, :]):
@@ -273,9 +262,8 @@
     w_own, w_other = pl.pallas_call(
         split_kernel,
         out_shape=(w_type, w_type),
-        in_specs=[SMEM, HBM, HBM],
+        in_specs=[SMEM, VMEM, VMEM],
         out_specs=(VMEM, VMEM),
-        scratch_shapes=[pltpu.SemaphoreType.DMA((4,))],
         compiler_params=params(),
     )(ids, key_weight, value_weight)
     w_chip = jnp.stack([w_own, shifted(w_other, "c", 2, 1)])
@@ -315,16 +303,15 @@
         out_specs=VMEM,
         compiler_params=params(),
     )(ids, own_sums, other_sums, table, *x_slots)
-    first = (0, 1, 2, 3, 5, 6, 7)
-    parts = project(ids, normed, first, [w_slots[s] for s in first])
-    mine, theirs = project(ids, normed, (4,), [w_slots[4]], parts)
+    theirs = shifted(project(1, ids, normed, w_slots), "c", 2, 1)
+    mine = project(0, ids, normed, w_slots)
     kv0 = pl.pallas_call(
         join_kernel,
         out_shape=jax.ShapeDtypeStruct((2 * span_len, HD), jnp.bfloat16),
         in_specs=[VMEM, VMEM],
         out_specs=VMEM,
         compiler_params=params(),
-    )(mine, shifted(theirs, "c", 2, 1))
+    )(mine, theirs)
 
     kv1 = shifted(kv0, "xl", 2, 1)
     kv2 = shifted(kv0, "yl", 2, 1)
@@ -347,9 +334,9 @@
         out_specs=(VMEM,) * 2,
         input_output_aliases={4: 0, 5: 1},
         compiler_params=params(),
-    )(*scalars, q_t, stat, acc, kv1)
+    )(*scalars, q_t, stat, acc, kv2)
     parts = [None] * QUAD
-    for later in (3, 2, 1, 0):
+    for later in (2, 3, 1, 0):
         part = pl.pallas_call(
             functools.partial(finish_kernel, later),
             out_shape=jax.ShapeDtypeStruct((HD + STAT_ROWS, span_len), jnp.bfloat16),
@@ -357,7 +344,7 @@
             out_specs=VMEM,
             scratch_shapes=[pltpu.VMEM((16, span_len), jnp.float32), pltpu.VMEM((HD, span_len), jnp.float32)],
             compiler_params=params(),
-        )(*scalars, q_t, stat, acc, kv2, kv3)
+        )(*scalars, q_t, stat, acc, kv1, kv3)
         parts[later] = moved(part, later) if later else part
     return pl.pallas_call(
         merge_kernel,

time: 138 us -> 139 us (level)
  the two profiles are of different devices: /device:TPU:41 before, /device:TPU:1 now
where the time goes in v4:
time: 139 us; the launch traced here: 138 us
  starting transfers between devices  91.5 us (66%)
  Pallas kernels  22.6 us (16%)
  waiting for transfers between devices  20.6 us (15%)
  local copies, waits for them, and re-layouts  1.93 us (1%)
    ppermute x21, starting transfers between devices, shifted(): lax.ppermute(value, axis, [(i, (i + by) % size) for i in range(size)])  79.3 us
    ppermute x6, waiting for transfers between devices, moved(): return lax.ppermute(value, ('yh', 'yl'), pairs)  14.3 us
    ppermute x6, starting transfers between devices, moved(): return lax.ppermute(value, ('yh', 'yl'), pairs)  9.28 us
    pallas_call x4, Pallas kernels, on_device(): pl.pallas_call(functools.partial(finish_kernel, later), out_shape=jax.Sha...  7.2 us
    ppermute x21, waiting for transfers between devices, shifted(): lax.ppermute(value, axis, [(i, (i + by) % size) for i in range(size)])  6.27 us
    pallas_call x2, Pallas kernels, project(): pl.pallas_call(functools.partial(project_kernel, head), out_shape=jax.Sha...  3.57 us
    pallas_call x1, Pallas kernels, on_device(): pl.pallas_call(begin_kernel, out_shape=(q_type, stat_type, acc_type), in_...  3.05 us
    ppermute x1, starting transfers between devices, on_device(): kv3 = lax.ppermute(kv0, ('yl', 'xl'), [(i, 3 - i) for i in range(4)])  2.93 us
  transfers between devices with their start and end apart: 28, of which 8 were waited for; matrix products, arithmetic and copies ran while one was open for 1% of the time, Pallas kernels for 12%

profile of v4, /device:TPU:1, one launch (start us, length us, event | category | flops | bytes accessed | tf_op | source)
XLA Modules:
  0.0 138.1 jit_solution(8941507832387663557)
XLA Ops:
  0.1 0.9 copy-done.3
  1.0 0.9 copy-done.4
  2.5 8.8 %collective-permute-start = (bf16[192,256]{1,0:T(8,128)(2,1)S(1)}, bf16[192,256]{1,0:T(8,128)(2,1)S(1)}, u32[]{:S(2)}, u32[]{:S(2)}) collective-permute-start(bf16[192,256]{1,0:T(8,128)(2,1)S(1)} %get-tuple-element.17), channel_id=1, source_target_pairs={{0,1},{1,0},{2,3},{3,2},{4,5},{5,4},{6,7},{7,6},{8,9},{9,8},{10,11... | collective-permute-start | bytes 294920 | tf_op jit(solution)/shard_map/ppermute | solution.py:31
  11.3 1.9 %collective-permute-start.5 = (bf16[192,512]{1,0:T(8,128)(2,1)}, bf16[192,512]{1,0:T(8,128)(2,1)S(1)}, u32[]{:S(2)}, u32[]{:S(2)}) collective-permute-start(bf16[192,512]{1,0:T(8,128)(2,1)} %bitcast.15), channel_id=1, source_target_pairs={{0,16},{16,0},{1,17},{17,1},{2,18},{18,2},{3,19},{19,3},{4,20},{20... | collective-permute-start | bytes 589832 | tf_op jit(solution)/shard_map/ppermute | solution.py:31
  13.3 1.9 %collective-permute-start.1 = (bf16[2,192,256]{2,1,0:T(8,128)(2,1)S(1)}, bf16[2,192,256]{2,1,0:T(8,128)(2,1)S(1)}, u32[]{:S(2)}, u32[]{:S(2)}) collective-permute-start(bf16[2,192,256]{2,1,0:T(8,128)(2,1)S(1)} %pad_maximum_fusion.2), channel_id=1, source_target_pairs={{0,32},{32,0},{1,33},{33,1},{2,34},{34,2},{3,35},{35,3},{4,36},{36... | collective-permute-start | bytes 589832 | tf_op jit(solution)/shard_map/ppermute | solution.py:31
  15.2 1.3 collective-permute-start.2
  16.5 1.3 collective-permute-start.3
  17.8 1.3 collective-permute-start.4
  19.1 2.3 %collective-permute-done.5 = bf16[192,512]{1,0:T(8,128)(2,1)S(1)} collective-permute-done((bf16[192,512]{1,0:T(8,128)(2,1)}, bf16[192,512]{1,0:T(8,128)(2,1)S(1)}, u32[]{:S(2)}, u32[]{:S(2)}) %collective-permute-start.5) | collective-permute-done | bytes 196640 | tf_op jit(solution)/shard_map/ppermute | solution.py:31
  21.4 1.0 pad_maximum_fusion.1.refs_0_
  22.4 1.9 %collective-permute-start.6 = (bf16[384,512]{1,0:T(8,128)(2,1)S(1)}, bf16[384,512]{1,0:T(8,128)(2,1)S(1)}, u32[]{:S(2)}, u32[]{:S(2)}) collective-permute-start(bf16[384,512]{1,0:T(8,128)(2,1)S(1)} %pad_maximum_fusion.1.refs_0_), channel_id=1, source_target_pairs={{0,2},{2,4},{4,6},{6,8},{8,10},{10,12},{12,14},{14,0},{1,3},{3,5},... | collective-permute-start | bytes 1179656 | tf_op jit(solution)/shard_map/ppermute | solution.py:31
  24.4 0.8 collective-permute-done.2.q1
  25.1 1.6 %collective-permute-done.3.q2 = bf16[512,128]{1,0:T(8,128)(2,1)S(1)} collective-permute-done((bf16[512,128]{1,0:T(8,128)(2,1)}, bf16[512,128]{1,0:T(8,128)(2,1)S(1)}, u32[]{:S(2)}, u32[]{:S(2)}) %collective-permute-start.3) | collective-permute-done | bytes 131104 | tf_op jit(solution)/shard_map/ppermute | solution.py:44
  26.7 3.1 %collective-permute-done.4.q3 = bf16[512,128]{1,0:T(8,128)(2,1)S(1)} collective-permute-done((bf16[512,128]{1,0:T(8,128)(2,1)}, bf16[512,128]{1,0:T(8,128)(2,1)S(1)}, u32[]{:S(2)}, u32[]{:S(2)}) %collective-permute-start.4) | collective-permute-done | bytes 131104 | tf_op jit(solution)/shard_map/ppermute | solution.py:44
  29.9 6.9 %collective-permute-start.14 = (bf16[4,192,256]{2,1,0:T(8,128)(2,1)S(1)}, bf16[4,192,256]{2,1,0:T(8,128)(2,1)S(1)}, u32[]{:S(2)}, u32[]{:S(2)}) collective-permute-start(bf16[4,192,256]{2,1,0:T(8,128)(2,1)S(1)} %pad_maximum_fusion.refs_0_), channel_id=1, source_target_pairs={{0,448},{64,0},{128,64},{192,128},{256,192},{320,256},{384,320},{4... | collective-permute-start | bytes 1179656 | tf_op jit(solution)/shard_map/ppermute | solution.py:31
  36.8 8.8 %collective-permute-start.10 = (bf16[384,512]{1,0:T(8,128)(2,1)S(1)}, bf16[384,512]{1,0:T(8,128)(2,1)S(1)}, u32[]{:S(2)}, u32[]{:S(2)}) collective-permute-start(bf16[384,512]{1,0:T(8,128)(2,1)S(1)} %pad_maximum_fusion.1.refs_0_), channel_id=1, source_target_pairs={{0,14},{2,0},{4,2},{6,4},{8,6},{10,8},{12,10},{14,12},{1,15},{3,1}... | collective-permute-start | bytes 1179656 | tf_op jit(solution)/shard_map/ppermute | solution.py:31
  45.6 1.9 %collective-permute-start.7 = (bf16[384,512]{1,0:T(8,128)(2,1)S(1)}, bf16[384,512]{1,0:T(8,128)(2,1)S(1)}, u32[]{:S(2)}, u32[]{:S(2)}) collective-permute-start(bf16[384,512]{1,0:T(8,128)(2,1)S(1)} %collective-permute-done.6.refs_6_.refs_7_), channel_id=1, source_target_pairs={{0,2},{2,4},{4,6},{6,8},{8,10},{10,12},{12,14},{14,0},{1,3},{3,5},... | collective-permute-start | bytes 1179656 | tf_op jit(solution)/shard_map/ppermute | solution.py:31
  47.5 3.7 %collective-permute-start.18 = (bf16[4,192,256]{2,1,0:T(8,128)(2,1)S(1)}, bf16[4,192,256]{2,1,0:T(8,128)(2,1)S(1)}, u32[]{:S(2)}, u32[]{:S(2)}) collective-permute-start(bf16[4,192,256]{2,1,0:T(8,128)(2,1)S(1)} %pad_maximum_fusion.refs_0_), channel_id=1, source_target_pairs={{0,64},{64,128},{128,192},{192,256},{256,320},{320,384},{384,448},... | collective-permute-start | bytes 1179656 | tf_op jit(solution)/shard_map/ppermute | solution.py:31
  51.3 2.8 %collective-permute-start.15 = (bf16[4,192,256]{2,1,0:T(8,128)(2,1)S(1)}, bf16[4,192,256]{2,1,0:T(8,128)(2,1)S(1)}, u32[]{:S(2)}, u32[]{:S(2)}) collective-permute-start(bf16[4,192,256]{2,1,0:T(8,128)(2,1)S(1)} %collective-permute-done.14.refs_1_), channel_id=1, source_target_pairs={{0,448},{64,0},{128,64},{192,128},{256,192},{320,256},{384,320},{4... | collective-permute-start | bytes 1179656 | tf_op jit(solution)/shard_map/ppermute | solution.py:31
  54.0 4.6 %collective-permute-start.11 = (bf16[384,512]{1,0:T(8,128)(2,1)S(1)}, bf16[384,512]{1,0:T(8,128)(2,1)S(1)}, u32[]{:S(2)}, u32[]{:S(2)}) collective-permute-start(bf16[384,512]{1,0:T(8,128)(2,1)S(1)} %collective-permute-done.10.refs_1_), channel_id=1, source_target_pairs={{0,14},{2,0},{4,2},{6,4},{8,6},{10,8},{12,10},{14,12},{1,15},{3,1}... | collective-permute-start | bytes 1179656 | tf_op jit(solution)/shard_map/ppermute | solution.py:31
  58.6 1.9 %collective-permute-start.8 = (bf16[384,512]{1,0:T(8,128)(2,1)S(1)}, bf16[384,512]{1,0:T(8,128)(2,1)S(1)}, u32[]{:S(2)}, u32[]{:S(2)}) collective-permute-start(bf16[384,512]{1,0:T(8,128)(2,1)S(1)} %collective-permute-done.7.refs_5_.refs_6_), channel_id=1, source_target_pairs={{0,2},{2,4},{4,6},{6,8},{8,10},{10,12},{12,14},{14,0},{1,3},{3,5},... | collective-permute-start | bytes 1179656 | tf_op jit(solution)/shard_map/ppermute | solution.py:31
  60.6 3.5 %collective-permute-start.19 = (bf16[4,192,256]{2,1,0:T(8,128)(2,1)S(1)}, bf16[4,192,256]{2,1,0:T(8,128)(2,1)S(1)}, u32[]{:S(2)}, u32[]{:S(2)}) collective-permute-start(bf16[4,192,256]{2,1,0:T(8,128)(2,1)S(1)} %collective-permute-done.18.refs_7_), channel_id=1, source_target_pairs={{0,64},{64,128},{128,192},{192,256},{256,320},{320,384},{384,448},... | collective-permute-start | bytes 1179656 | tf_op jit(solution)/shard_map/ppermute | solution.py:31
  64.1 3.0 %collective-permute-start.16 = (bf16[4,192,256]{2,1,0:T(8,128)(2,1)S(1)}, bf16[4,192,256]{2,1,0:T(8,128)(2,1)S(1)}, u32[]{:S(2)}, u32[]{:S(2)}) collective-permute-start(bf16[4,192,256]{2,1,0:T(8,128)(2,1)S(1)} %collective-permute-done.15.refs_2_), channel_id=1, source_target_pairs={{0,448},{64,0},{128,64},{192,128},{256,192},{320,256},{384,320},{4... | collective-permute-start | bytes 1179656 | tf_op jit(solution)/shard_map/ppermute | solution.py:31
  67.1 4.6 %collective-permute-start.12 = (bf16[384,512]{1,0:T(8,128)(2,1)S(1)}, bf16[384,512]{1,0:T(8,128)(2,1)S(1)}, u32[]{:S(2)}, u32[]{:S(2)}) collective-permute-start(bf16[384,512]{1,0:T(8,128)(2,1)S(1)} %collective-permute-done.11.refs_2_), channel_id=1, source_target_pairs={{0,14},{2,0},{4,2},{6,4},{8,6},{10,8},{12,10},{14,12},{1,15},{3,1}... | collective-permute-start | bytes 1179656 | tf_op jit(solution)/shard_map/ppermute | solution.py:31
  71.7 1.9 %collective-permute-start.9 = (bf16[384,512]{1,0:T(8,128)(2,1)S(1)}, bf16[384,512]{1,0:T(8,128)(2,1)S(1)}, u32[]{:S(2)}, u32[]{:S(2)}) collective-permute-start(bf16[384,512]{1,0:T(8,128)(2,1)S(1)} %collective-permute-done.8.refs_4_.refs_5_), channel_id=1, source_target_pairs={{0,2},{2,4},{4,6},{6,8},{8,10},{10,12},{12,14},{14,0},{1,3},{3,5},... | collective-permute-start | bytes 1179656 | tf_op jit(solution)/shard_map/ppermute | solution.py:31
  73.6 2.4 %collective-permute-start.20 = (bf16[4,192,256]{2,1,0:T(8,128)(2,1)S(1)}, bf16[4,192,256]{2,1,0:T(8,128)(2,1)S(1)}, u32[]{:S(2)}, u32[]{:S(2)}) collective-permute-start(bf16[4,192,256]{2,1,0:T(8,128)(2,1)S(1)} %collective-permute-done.19.refs_6_), channel_id=1, source_target_pairs={{0,64},{64,128},{128,192},{192,256},{256,320},{320,384},{384,448},... | collective-permute-start | bytes 1179656 | tf_op jit(solution)/shard_map/ppermute | solution.py:31
  76.0 4.1 %collective-permute-start.17 = (bf16[4,192,256]{2,1,0:T(8,128)(2,1)S(1)}, bf16[4,192,256]{2,1,0:T(8,128)(2,1)S(1)}, u32[]{:S(2)}, u32[]{:S(2)}) collective-permute-start(bf16[4,192,256]{2,1,0:T(8,128)(2,1)S(1)} %collective-permute-done.16.refs_3_), channel_id=1, source_target_pairs={{0,448},{64,0},{128,64},{192,128},{256,192},{320,256},{384,320},{4... | collective-permute-start | bytes 1179656 | tf_op jit(solution)/shard_map/ppermute | solution.py:31
  81.5 6.8 %collective-permute-start.13 = (f32[8,512]{1,0:T(8,128)S(1)}, f32[8,512]{1,0:T(8,128)S(1)}, u32[]{:S(2)}, u32[]{:S(2)}) collective-permute-start(f32[8,512]{1,0:T(8,128)S(1)} %shard_map.84.own_ref), channel_id=1, source_target_pairs={{0,1},{1,0},{2,3},{3,2},{4,5},{5,4},{6,7},{7,6},{8,9},{9,8},{10,11... | collective-permute-start | bytes 49160 | tf_op jit(solution)/shard_map/ppermute | solution.py:31
  89.1 2.6 %shard_map.86.normed_ref = bf16[8,2,512,192]{3,2,1,0:T(8,128)(2,1)S(1)} custom-call(s32[8]{0:T(128)S(1)} %stack.44.ids_ref, f32[8,512]{1,0:T(8,128)S(1)} %shard_map.84.own_ref, f32[8,512]{1,0:T(8,128)S(1)} %collective-permute-done.13.other_ref, f32[64,192]{1,0:T(8,128)S(1)} %shard_map.85.table_ref, bf16[384,512]{1,0:T(8,128)(2,1)S(1)} %pad_maximum_fusion.1.refs_0_, ...), custom_call_target="tpu_custom_call" | custom-call | tf_op jit(solution)/shard_map/pallas_call | solution.py:299
  91.7 1.8 %shard_map.88 = f32[512,256]{1,0:T(8,128)S(1)} custom-call(s32[8]{0:T(128)S(1)} %stack.44.ids_ref, bf16[8,2,512,192]{3,2,1,0:T(8,128)(2,1)S(1)} %shard_map.86.normed_ref, bf16[4,192,256]{2,1,0:T(8,128)(2,1)S(1)} %pad_maximum_fusion.refs_0_, bf16[4,192,256]{2,1,0:T(8,128)(2,1)S(1)} %collective-permute-done.14.refs_1_, ...), custom_call_target="tpu_custom_call" | custom-call | tf_op jit(solution)/shard_map/pallas_call | solution.py:134
  93.6 2.4 %collective-permute-start.21 = (f32[512,256]{1,0:T(8,128)S(1)}, f32[512,256]{1,0:T(8,128)S(1)}, u32[]{:S(2)}, u32[]{:S(2)}) collective-permute-start(f32[512,256]{1,0:T(8,128)S(1)} %shard_map.88), channel_id=1, source_target_pairs={{0,1},{1,0},{2,3},{3,2},{4,5},{5,4},{6,7},{7,6},{8,9},{9,8},{10,11... | collective-permute-start | bytes 1572872 | tf_op jit(solution)/shard_map/ppermute | solution.py:31
  96.0 1.8 %shard_map.87.mine_ref = f32[512,256]{1,0:T(8,128)S(1)} custom-call(s32[8]{0:T(128)S(1)} %stack.44.ids_ref, bf16[8,2,512,192]{3,2,1,0:T(8,128)(2,1)S(1)} %shard_map.86.normed_ref, bf16[4,192,256]{2,1,0:T(8,128)(2,1)S(1)} %pad_maximum_fusion.refs_0_, bf16[4,192,256]{2,1,0:T(8,128)(2,1)S(1)} %collective-permute-done.14.refs_1_, ...), custom_call_target="tpu_custom_call" | custom-call | tf_op jit(solution)/shard_map/pallas_call | solution.py:134
  97.9 2.4 %collective-permute-start.22 = (bf16[1024,128]{1,0:T(8,128)(2,1)S(1)}, bf16[1024,128]{1,0:T(8,128)(2,1)S(1)}, u32[]{:S(2)}, u32[]{:S(2)}) collective-permute-start(bf16[1024,128]{1,0:T(8,128)(2,1)S(1)} %shard_map.89.kv_ref), channel_id=1, source_target_pairs={{0,64},{64,0},{1,65},{65,1},{2,66},{66,2},{3,67},{67,3},{4,68},{68... | collective-permute-start | bytes 786440 | tf_op jit(solution)/shard_map/ppermute | solution.py:31
  100.3 3.1 %collective-permute-start.23 = (bf16[1024,128]{1,0:T(8,128)(2,1)S(1)}, bf16[1024,128]{1,0:T(8,128)(2,1)S(1)}, u32[]{:S(2)}, u32[]{:S(2)}) collective-permute-start(bf16[1024,128]{1,0:T(8,128)(2,1)S(1)} %shard_map.89.kv_ref), channel_id=1, source_target_pairs={{0,32},{32,0},{1,33},{33,1},{2,34},{34,2},{3,35},{35,3},{4,36},{36... | collective-permute-start | bytes 786440 | tf_op jit(solution)/shard_map/ppermute | solution.py:31
  103.3 2.9 %collective-permute-start.24 = (bf16[1024,128]{1,0:T(8,128)(2,1)S(1)}, bf16[1024,128]{1,0:T(8,128)(2,1)S(1)}, u32[]{:S(2)}, u32[]{:S(2)}) collective-permute-start(bf16[1024,128]{1,0:T(8,128)(2,1)S(1)} %shard_map.89.kv_ref), channel_id=1, source_target_pairs={{0,96},{32,64},{64,32},{96,0},{1,97},{33,65},{65,33},{97,1},{2,98}... | collective-permute-start | bytes 786440 | tf_op jit(solution)/shard_map/ppermute | solution.py:318
  106.3 3.0 %shard_map.90 = (bf16[4,128,512]{2,1,0:T(8,128)(2,1)S(1)}, f32[4,16,512]{2,1,0:T(8,128)S(1)}, f32[4,128,512]{2,1,0:T(8,128)S(1)}) custom-call(s32[8]{0:T(128)S(1)} %stack.44.ids_ref, s32[16,16]{1,0:T(8,128)S(1)} %copy-done, s32[16]{0:T(128)S(1)} %copy-done.5, bf16[512,128]{1,0:T(8,128)(2,1)S(1)} %copy-done.2, ...), custom_call_target="tpu_custom_call" | custom-call | tf_op jit(solution)/shard_map/pallas_call | solution.py:323
  109.4 2.7 %shard_map.91 = (f32[4,16,512]{2,1,0:T(8,128)S(1)}, f32[4,128,512]{2,1,0:T(8,128)S(1)}) custom-call(s32[8]{0:T(128)S(1)} %stack.44.ids_ref, s32[16,16]{1,0:T(8,128)S(1)} %copy-done, s32[16]{0:T(128)S(1)} %copy-done.5, bf16[4,128,512]{2,1,0:T(8,128)(2,1)S(1)} %get-tuple-element.22.q_t, ...), custom_call_target="tpu_custom_call", output_to_operand_aliasing={{0}: (4, {}), {1}: (5, {})} | custom-call | tf_op jit(solution)/shard_map/pallas_call | solution.py:330
  112.1 3.1 %collective-permute-done.23.kv1 = bf16[1024,128]{1,0:T(8,128)(2,1)S(1)} collective-permute-done((bf16[1024,128]{1,0:T(8,128)(2,1)S(1)}, bf16[1024,128]{1,0:T(8,128)(2,1)S(1)}, u32[]{:S(2)}, u32[]{:S(2)}) %collective-permute-start.23) | collective-permute-done | bytes 262176 | tf_op jit(solution)/shard_map/ppermute | solution.py:31
  115.2 2.3 %shard_map.93 = bf16[144,512]{1,0:T(8,128)(2,1)S(1)} custom-call(s32[8]{0:T(128)S(1)} %stack.44.ids_ref, s32[16,16]{1,0:T(8,128)S(1)} %copy-done, s32[16]{0:T(128)S(1)} %copy-done.5, bf16[4,128,512]{2,1,0:T(8,128)(2,1)S(1)} %get-tuple-element.22.q_t, f32[4,16,512]{2,1,0:T(8,128)S(1)} %get-tuple-element.25.stat_in, ...), custom_call_target="tpu_custom_call" | custom-call | tf_op jit(solution)/shard_map/pallas_call | solution.py:340
  117.5 2.7 %collective-permute-start.25 = (bf16[144,512]{1,0:T(8,128)(2,1)S(1)}, bf16[144,512]{1,0:T(8,128)(2,1)S(1)}, u32[]{:S(2)}, u32[]{:S(2)}) collective-permute-start(bf16[144,512]{1,0:T(8,128)(2,1)S(1)} %shard_map.93), channel_id=1, source_target_pairs={{0,128},{64,192},{128,256},{192,320},{256,384},{320,448},{1,129},{... | collective-permute-start | bytes 442376 | tf_op jit(solution)/shard_map/ppermute | solution.py:44
  120.2 2.1 %shard_map.94 = bf16[144,512]{1,0:T(8,128)(2,1)S(1)} custom-call(s32[8]{0:T(128)S(1)} %stack.44.ids_ref, s32[16,16]{1,0:T(8,128)S(1)} %copy-done, s32[16]{0:T(128)S(1)} %copy-done.5, bf16[4,128,512]{2,1,0:T(8,128)(2,1)S(1)} %get-tuple-element.22.q_t, f32[4,16,512]{2,1,0:T(8,128)S(1)} %get-tuple-element.25.stat_in, ...), custom_call_target="tpu_custom_call" | custom-call | tf_op jit(solution)/shard_map/pallas_call | solution.py:340
  122.3 1.4 collective-permute-start.26
  123.7 2.1 %shard_map.95 = bf16[144,512]{1,0:T(8,128)(2,1)S(1)} custom-call(s32[8]{0:T(128)S(1)} %stack.44.ids_ref, s32[16,16]{1,0:T(8,128)S(1)} %copy-done, s32[16]{0:T(128)S(1)} %copy-done.5, bf16[4,128,512]{2,1,0:T(8,128)(2,1)S(1)} %get-tuple-element.22.q_t, f32[4,16,512]{2,1,0:T(8,128)S(1)} %get-tuple-element.25.stat_in, ...), custom_call_target="tpu_custom_call" | custom-call | tf_op jit(solution)/shard_map/pallas_call | solution.py:340
  125.8 1.3 collective-permute-start.27
  127.1 0.8 shard_map.92.part0
  127.9 5.6 %collective-permute-done.26.part2 = bf16[144,512]{1,0:T(8,128)(2,1)S(1)} collective-permute-done((bf16[144,512]{1,0:T(8,128)(2,1)S(1)}, bf16[144,512]{1,0:T(8,128)(2,1)S(1)}, u32[]{:S(2)}, u32[]{:S(2)}) %collective-permute-start.26) | collective-permute-done | bytes 147488 | tf_op jit(solution)/shard_map/ppermute | solution.py:44
  133.5 3.2 %collective-permute-done.27.part3 = bf16[144,512]{1,0:T(8,128)(2,1)S(1)} collective-permute-done((bf16[144,512]{1,0:T(8,128)(2,1)S(1)}, bf16[144,512]{1,0:T(8,128)(2,1)S(1)}, u32[]{:S(2)}, u32[]{:S(2)}) %collective-permute-start.27) | collective-permute-done | bytes 147488 | tf_op jit(solution)/shard_map/ppermute | solution.py:44
  136.7 1.4 %shard_map.96 = bf16[512,128]{1,0:T(8,128)(2,1)} custom-call(s32[8]{0:T(128)S(1)} %stack.44.ids_ref, s32[16]{0:T(128)S(1)} %copy-done.5, bf16[144,512]{1,0:T(8,128)(2,1)S(1)} %shard_map.92.part0, bf16[144,512]{1,0:T(8,128)(2,1)S(1)} %collective-permute-done.25.part1, bf16[144,512]{1,0:T(8,128)(2,1)S(1)} %collective-permute-done.26.part2, ...), custom_call_target="tpu_custom_call" | custom-call | tf_op jit(solution)/shard_map/pallas_call | solution.py:349
  (41 shorter events, 3.0 us)
Async XLA Ops:
  0.0 88.3 %copy-start.1 = (bf16[8,12288]{1,0:T(8,128)(2,1)S(1)}, bf16[8,12288]{1,0:T(8,128)(2,1)}, u32[]{:S(2)}) copy-start(bf16[8,12288]{1,0:T(8,128)(2,1)} %modulation_ref.1) | copy-start | bytes 589828
  0.1 0.9 copy-start.3
  1.0 0.9 copy-start.4
  1.9 86.4 %copy-start.6 = (s32[16]{0:T(128)S(1)}, s32[16]{0:T(128)}, u32[]{:S(2)}) copy-start(s32[16]{0:T(128)} %levels_ref.1) | copy-start | bytes 196
  2.5 10.7 %collective-permute-start = (bf16[192,256]{1,0:T(8,128)(2,1)S(1)}, bf16[192,256]{1,0:T(8,128)(2,1)S(1)}, u32[]{:S(2)}, u32[]{:S(2)}) collective-permute-start(bf16[192,256]{1,0:T(8,128)(2,1)S(1)} %get-tuple-element.17), channel_id=1, source_target_pairs={{0,1},{1,0},{2,3},{3,2},{4,5},{5,4},{6,7},{7,6},{8,9},{9,8},{10,11... | collective-permute-start | bytes 294920 | tf_op jit(solution)/shard_map/ppermute | solution.py:31
  11.3 10.1 %collective-permute-start.5 = (bf16[192,512]{1,0:T(8,128)(2,1)}, bf16[192,512]{1,0:T(8,128)(2,1)S(1)}, u32[]{:S(2)}, u32[]{:S(2)}) collective-permute-start(bf16[192,512]{1,0:T(8,128)(2,1)} %bitcast.15), channel_id=1, source_target_pairs={{0,16},{16,0},{1,17},{17,1},{2,18},{18,2},{3,19},{19,3},{4,20},{20... | collective-permute-start | bytes 589832 | tf_op jit(solution)/shard_map/ppermute | solution.py:31
  13.3 11.0 %collective-permute-start.1 = (bf16[2,192,256]{2,1,0:T(8,128)(2,1)S(1)}, bf16[2,192,256]{2,1,0:T(8,128)(2,1)S(1)}, u32[]{:S(2)}, u32[]{:S(2)}) collective-permute-start(bf16[2,192,256]{2,1,0:T(8,128)(2,1)S(1)} %pad_maximum_fusion.2), channel_id=1, source_target_pairs={{0,32},{32,0},{1,33},{33,1},{2,34},{34,2},{3,35},{35,3},{4,36},{36... | collective-permute-start | bytes 589832 | tf_op jit(solution)/shard_map/ppermute | solution.py:31
  15.2 10.0 %collective-permute-start.2 = (bf16[512,128]{1,0:T(8,128)(2,1)}, bf16[512,128]{1,0:T(8,128)(2,1)S(1)}, u32[]{:S(2)}, u32[]{:S(2)}) collective-permute-start(bf16[512,128]{1,0:T(8,128)(2,1)} %q0.1), channel_id=1, source_target_pairs={{128,0},{192,64},{256,128},{320,192},{384,256},{448,320},{129,1},{... | collective-permute-start | bytes 393224 | tf_op jit(solution)/shard_map/ppermute | solution.py:44
  16.5 10.2 %collective-permute-start.3 = (bf16[512,128]{1,0:T(8,128)(2,1)}, bf16[512,128]{1,0:T(8,128)(2,1)S(1)}, u32[]{:S(2)}, u32[]{:S(2)}) collective-permute-start(bf16[512,128]{1,0:T(8,128)(2,1)} %q0.1), channel_id=1, source_target_pairs={{256,64},{320,0},{384,192},{448,128},{257,65},{321,1},{385,193},{4... | collective-permute-start | bytes 393224 | tf_op jit(solution)/shard_map/ppermute | solution.py:44
  17.8 12.1 %collective-permute-start.4 = (bf16[512,128]{1,0:T(8,128)(2,1)}, bf16[512,128]{1,0:T(8,128)(2,1)S(1)}, u32[]{:S(2)}, u32[]{:S(2)}) collective-permute-start(bf16[512,128]{1,0:T(8,128)(2,1)} %q0.1), channel_id=1, source_target_pairs={{384,0},{448,64},{385,1},{449,65},{386,2},{450,66},{387,3},{451,67... | collective-permute-start | bytes 393224 | tf_op jit(solution)/shard_map/ppermute | solution.py:44
  22.4 23.2 %collective-permute-start.6 = (bf16[384,512]{1,0:T(8,128)(2,1)S(1)}, bf16[384,512]{1,0:T(8,128)(2,1)S(1)}, u32[]{:S(2)}, u32[]{:S(2)}) collective-permute-start(bf16[384,512]{1,0:T(8,128)(2,1)S(1)} %pad_maximum_fusion.1.refs_0_), channel_id=1, source_target_pairs={{0,2},{2,4},{4,6},{6,8},{8,10},{10,12},{12,14},{14,0},{1,3},{3,5},... | collective-permute-start | bytes 1179656 | tf_op jit(solution)/shard_map/ppermute | solution.py:31
  29.9 21.4 %collective-permute-start.14 = (bf16[4,192,256]{2,1,0:T(8,128)(2,1)S(1)}, bf16[4,192,256]{2,1,0:T(8,128)(2,1)S(1)}, u32[]{:S(2)}, u32[]{:S(2)}) collective-permute-start(bf16[4,192,256]{2,1,0:T(8,128)(2,1)S(1)} %pad_maximum_fusion.refs_0_), channel_id=1, source_target_pairs={{0,448},{64,0},{128,64},{192,128},{256,192},{320,256},{384,320},{4... | collective-permute-start | bytes 1179656 | tf_op jit(solution)/shard_map/ppermute | solution.py:31
  36.8 17.3 %collective-permute-start.10 = (bf16[384,512]{1,0:T(8,128)(2,1)S(1)}, bf16[384,512]{1,0:T(8,128)(2,1)S(1)}, u32[]{:S(2)}, u32[]{:S(2)}) collective-permute-start(bf16[384,512]{1,0:T(8,128)(2,1)S(1)} %pad_maximum_fusion.1.refs_0_), channel_id=1, source_target_pairs={{0,14},{2,0},{4,2},{6,4},{8,6},{10,8},{12,10},{14,12},{1,15},{3,1}... | collective-permute-start | bytes 1179656 | tf_op jit(solution)/shard_map/ppermute | solution.py:31
  45.6 13.0 %collective-permute-start.7 = (bf16[384,512]{1,0:T(8,128)(2,1)S(1)}, bf16[384,512]{1,0:T(8,128)(2,1)S(1)}, u32[]{:S(2)}, u32[]{:S(2)}) collective-permute-start(bf16[384,512]{1,0:T(8,128)(2,1)S(1)} %collective-permute-done.6.refs_6_.refs_7_), channel_id=1, source_target_pairs={{0,2},{2,4},{4,6},{6,8},{8,10},{10,12},{12,14},{14,0},{1,3},{3,5},... | collective-permute-start | bytes 1179656 | tf_op jit(solution)/shard_map/ppermute | solution.py:31
  47.5 13.1 %collective-permute-start.18 = (bf16[4,192,256]{2,1,0:T(8,128)(2,1)S(1)}, bf16[4,192,256]{2,1,0:T(8,128)(2,1)S(1)}, u32[]{:S(2)}, u32[]{:S(2)}) collective-permute-start(bf16[4,192,256]{2,1,0:T(8,128)(2,1)S(1)} %pad_maximum_fusion.refs_0_), channel_id=1, source_target_pairs={{0,64},{64,128},{128,192},{192,256},{256,320},{320,384},{384,448},... | collective-permute-start | bytes 1179656 | tf_op jit(solution)/shard_map/ppermute | solution.py:31
  51.3 12.8 %collective-permute-start.15 = (bf16[4,192,256]{2,1,0:T(8,128)(2,1)S(1)}, bf16[4,192,256]{2,1,0:T(8,128)(2,1)S(1)}, u32[]{:S(2)}, u32[]{:S(2)}) collective-permute-start(bf16[4,192,256]{2,1,0:T(8,128)(2,1)S(1)} %collective-permute-done.14.refs_1_), channel_id=1, source_target_pairs={{0,448},{64,0},{128,64},{192,128},{256,192},{320,256},{384,320},{4... | collective-permute-start | bytes 1179656 | tf_op jit(solution)/shard_map/ppermute | solution.py:31
  54.0 13.1 %collective-permute-start.11 = (bf16[384,512]{1,0:T(8,128)(2,1)S(1)}, bf16[384,512]{1,0:T(8,128)(2,1)S(1)}, u32[]{:S(2)}, u32[]{:S(2)}) collective-permute-start(bf16[384,512]{1,0:T(8,128)(2,1)S(1)} %collective-permute-done.10.refs_1_), channel_id=1, source_target_pairs={{0,14},{2,0},{4,2},{6,4},{8,6},{10,8},{12,10},{14,12},{1,15},{3,1}... | collective-permute-start | bytes 1179656 | tf_op jit(solution)/shard_map/ppermute | solution.py:31
  58.6 13.1 %collective-permute-start.8 = (bf16[384,512]{1,0:T(8,128)(2,1)S(1)}, bf16[384,512]{1,0:T(8,128)(2,1)S(1)}, u32[]{:S(2)}, u32[]{:S(2)}) collective-permute-start(bf16[384,512]{1,0:T(8,128)(2,1)S(1)} %collective-permute-done.7.refs_5_.refs_6_), channel_id=1, source_target_pairs={{0,2},{2,4},{4,6},{6,8},{8,10},{10,12},{12,14},{14,0},{1,3},{3,5},... | collective-permute-start | bytes 1179656 | tf_op jit(solution)/shard_map/ppermute | solution.py:31
  60.6 13.1 %collective-permute-start.19 = (bf16[4,192,256]{2,1,0:T(8,128)(2,1)S(1)}, bf16[4,192,256]{2,1,0:T(8,128)(2,1)S(1)}, u32[]{:S(2)}, u32[]{:S(2)}) collective-permute-start(bf16[4,192,256]{2,1,0:T(8,128)(2,1)S(1)} %collective-permute-done.18.refs_7_), channel_id=1, source_target_pairs={{0,64},{64,128},{128,192},{192,256},{256,320},{320,384},{384,448},... | collective-permute-start | bytes 1179656 | tf_op jit(solution)/shard_map/ppermute | solution.py:31
  64.1 11.9 %collective-permute-start.16 = (bf16[4,192,256]{2,1,0:T(8,128)(2,1)S(1)}, bf16[4,192,256]{2,1,0:T(8,128)(2,1)S(1)}, u32[]{:S(2)}, u32[]{:S(2)}) collective-permute-start(bf16[4,192,256]{2,1,0:T(8,128)(2,1)S(1)} %collective-permute-done.15.refs_2_), channel_id=1, source_target_pairs={{0,448},{64,0},{128,64},{192,128},{256,192},{320,256},{384,320},{4... | collective-permute-start | bytes 1179656 | tf_op jit(solution)/shard_map/ppermute | solution.py:31
  67.1 13.1 %collective-permute-start.12 = (bf16[384,512]{1,0:T(8,128)(2,1)S(1)}, bf16[384,512]{1,0:T(8,128)(2,1)S(1)}, u32[]{:S(2)}, u32[]{:S(2)}) collective-permute-start(bf16[384,512]{1,0:T(8,128)(2,1)S(1)} %collective-permute-done.11.refs_2_), channel_id=1, source_target_pairs={{0,14},{2,0},{4,2},{6,4},{8,6},{10,8},{12,10},{14,12},{1,15},{3,1}... | collective-permute-start | bytes 1179656 | tf_op jit(solution)/shard_map/ppermute | solution.py:31
  71.7 9.7 %collective-permute-start.9 = (bf16[384,512]{1,0:T(8,128)(2,1)S(1)}, bf16[384,512]{1,0:T(8,128)(2,1)S(1)}, u32[]{:S(2)}, u32[]{:S(2)}) collective-permute-start(bf16[384,512]{1,0:T(8,128)(2,1)S(1)} %collective-permute-done.8.refs_4_.refs_5_), channel_id=1, source_target_pairs={{0,2},{2,4},{4,6},{6,8},{8,10},{10,12},{12,14},{14,0},{1,3},{3,5},... | collective-permute-start | bytes 1179656 | tf_op jit(solution)/shard_map/ppermute | solution.py:31
  73.6 18.1 %collective-permute-start.20 = (bf16[4,192,256]{2,1,0:T(8,128)(2,1)S(1)}, bf16[4,192,256]{2,1,0:T(8,128)(2,1)S(1)}, u32[]{:S(2)}, u32[]{:S(2)}) collective-permute-start(bf16[4,192,256]{2,1,0:T(8,128)(2,1)S(1)} %collective-permute-done.19.refs_6_), channel_id=1, source_target_pairs={{0,64},{64,128},{128,192},{192,256},{256,320},{320,384},{384,448},... | collective-permute-start | bytes 1179656 | tf_op jit(solution)/shard_map/ppermute | solution.py:31
  76.0 15.7 %collective-permute-start.17 = (bf16[4,192,256]{2,1,0:T(8,128)(2,1)S(1)}, bf16[4,192,256]{2,1,0:T(8,128)(2,1)S(1)}, u32[]{:S(2)}, u32[]{:S(2)}) collective-permute-start(bf16[4,192,256]{2,1,0:T(8,128)(2,1)S(1)} %collective-permute-done.16.refs_3_), channel_id=1, source_target_pairs={{0,448},{64,0},{128,64},{192,128},{256,192},{320,256},{384,320},{4... | collective-permute-start | bytes 1179656 | tf_op jit(solution)/shard_map/ppermute | solution.py:31
  81.5 7.6 %collective-permute-start.13 = (f32[8,512]{1,0:T(8,128)S(1)}, f32[8,512]{1,0:T(8,128)S(1)}, u32[]{:S(2)}, u32[]{:S(2)}) collective-permute-start(f32[8,512]{1,0:T(8,128)S(1)} %shard_map.84.own_ref), channel_id=1, source_target_pairs={{0,1},{1,0},{2,3},{3,2},{4,5},{5,4},{6,7},{7,6},{8,9},{9,8},{10,11... | collective-permute-start | bytes 49160 | tf_op jit(solution)/shard_map/ppermute | solution.py:31
  93.5 12.7 %copy-start = (s32[16,16]{1,0:T(8,128)S(1)}, s32[16,16]{1,0:T(8,128)}, u32[]{:S(2)}) copy-start(s32[16,16]{1,0:T(8,128)} %visible_ref.11) | copy-start | bytes 3076
  93.5 12.7 %copy-start.2 = (bf16[512,128]{1,0:T(8,128)(2,1)S(1)}, bf16[512,128]{1,0:T(8,128)(2,1)}, u32[]{:S(2)}) copy-start(bf16[512,128]{1,0:T(8,128)(2,1)} %q0.1) | copy-start | bytes 393220
  93.6 12.7 %copy-start.5 = (s32[16]{0:T(128)S(1)}, s32[16]{0:T(128)}, u32[]{:S(2)}) copy-start(s32[16]{0:T(128)} %counts_ref.13) | copy-start | bytes 196
  93.6 4.2 %collective-permute-start.21 = (f32[512,256]{1,0:T(8,128)S(1)}, f32[512,256]{1,0:T(8,128)S(1)}, u32[]{:S(2)}, u32[]{:S(2)}) collective-permute-start(f32[512,256]{1,0:T(8,128)S(1)} %shard_map.88), channel_id=1, source_target_pairs={{0,1},{1,0},{2,3},{3,2},{4,5},{5,4},{6,7},{7,6},{8,9},{9,8},{10,11... | collective-permute-start | bytes 1572872 | tf_op jit(solution)/shard_map/ppermute | solution.py:31
  97.9 11.5 %collective-permute-start.22 = (bf16[1024,128]{1,0:T(8,128)(2,1)S(1)}, bf16[1024,128]{1,0:T(8,128)(2,1)S(1)}, u32[]{:S(2)}, u32[]{:S(2)}) collective-permute-start(bf16[1024,128]{1,0:T(8,128)(2,1)S(1)} %shard_map.89.kv_ref), channel_id=1, source_target_pairs={{0,64},{64,0},{1,65},{65,1},{2,66},{66,2},{3,67},{67,3},{4,68},{68... | collective-permute-start | bytes 786440 | tf_op jit(solution)/shard_map/ppermute | solution.py:31
  100.3 14.9 %collective-permute-start.23 = (bf16[1024,128]{1,0:T(8,128)(2,1)S(1)}, bf16[1024,128]{1,0:T(8,128)(2,1)S(1)}, u32[]{:S(2)}, u32[]{:S(2)}) collective-permute-start(bf16[1024,128]{1,0:T(8,128)(2,1)S(1)} %shard_map.89.kv_ref), channel_id=1, source_target_pairs={{0,32},{32,0},{1,33},{33,1},{2,34},{34,2},{3,35},{35,3},{4,36},{36... | collective-permute-start | bytes 786440 | tf_op jit(solution)/shard_map/ppermute | solution.py:31
  103.3 11.9 %collective-permute-start.24 = (bf16[1024,128]{1,0:T(8,128)(2,1)S(1)}, bf16[1024,128]{1,0:T(8,128)(2,1)S(1)}, u32[]{:S(2)}, u32[]{:S(2)}) collective-permute-start(bf16[1024,128]{1,0:T(8,128)(2,1)S(1)} %shard_map.89.kv_ref), channel_id=1, source_target_pairs={{0,96},{32,64},{64,32},{96,0},{1,97},{33,65},{65,33},{97,1},{2,98}... | collective-permute-start | bytes 786440 | tf_op jit(solution)/shard_map/ppermute | solution.py:318
  117.5 10.4 %collective-permute-start.25 = (bf16[144,512]{1,0:T(8,128)(2,1)S(1)}, bf16[144,512]{1,0:T(8,128)(2,1)S(1)}, u32[]{:S(2)}, u32[]{:S(2)}) collective-permute-start(bf16[144,512]{1,0:T(8,128)(2,1)S(1)} %shard_map.93), channel_id=1, source_target_pairs={{0,128},{64,192},{128,256},{192,320},{256,384},{320,448},{1,129},{... | collective-permute-start | bytes 442376 | tf_op jit(solution)/shard_map/ppermute | solution.py:44
  122.3 11.2 %collective-permute-start.26 = (bf16[144,512]{1,0:T(8,128)(2,1)S(1)}, bf16[144,512]{1,0:T(8,128)(2,1)S(1)}, u32[]{:S(2)}, u32[]{:S(2)}) collective-permute-start(bf16[144,512]{1,0:T(8,128)(2,1)S(1)} %shard_map.94), channel_id=1, source_target_pairs={{0,320},{64,256},{128,448},{192,384},{1,321},{65,257},{129,449},{1... | collective-permute-start | bytes 442376 | tf_op jit(solution)/shard_map/ppermute | solution.py:44
  125.8 10.9 %collective-permute-start.27 = (bf16[144,512]{1,0:T(8,128)(2,1)S(1)}, bf16[144,512]{1,0:T(8,128)(2,1)S(1)}, u32[]{:S(2)}, u32[]{:S(2)}) collective-permute-start(bf16[144,512]{1,0:T(8,128)(2,1)S(1)} %shard_map.95), channel_id=1, source_target_pairs={{0,384},{64,448},{1,385},{65,449},{2,386},{66,450},{3,387},{67,451... | collective-permute-start | bytes 442376 | tf_op jit(solution)/shard_map/ppermute | solution.py:44

commit v5 on v4

--- a/solution.py
+++ b/solution.py
@@ -201,22 +201,25 @@
 
 
 def finish_kernel(later, ids_ref, visible_ref, counts_ref, q_t, stat_in, acc_in, kv1, kv3, out_ref, stat, acc):
-    span_len = out_ref.shape[1]
+    span_len = out_ref.shape[0] - STAT_ROWS
 
     @pl.when(ids_ref[YH] + later < QUAD)
     def _():
         stat[...] = stat_in[later]
         acc[...] = acc_in[later]
         scan_keys(later, (1, 3), ids_ref, visible_ref, counts_ref, q_t.at[later], (kv1, kv3), stat, acc)
-        out_ref[0:HD, :] = acc[...].astype(jnp.bfloat16)
-        rows = []
-        for value in (stat[0:1, :], stat[8:9, :]):
-            for _part in range(3):
-                part = value.astype(jnp.bfloat16).astype(jnp.float32)
-                rows.append(part)
-                value = value - part
-        rows.append(jnp.zeros((STAT_ROWS - 6, span_len), jnp.float32))
-        out_ref[HD : HD + STAT_ROWS, :] = jnp.concatenate(rows, axis=0).astype(jnp.bfloat16)
+        best = stat[0:1, :]
+        high = best.astype(jnp.bfloat16).astype(jnp.float32)
+        low = (best - high).astype(jnp.bfloat16).astype(jnp.float32)
+        scale = jnp.where(best > 0.5 * NEG_BIG, jnp.exp2((best - high) - low), 0.0)
+        total = stat[8:9, :] * scale
+        total_high = total.astype(jnp.bfloat16).astype(jnp.float32)
+        stats = jnp.concatenate([high, low, total_high, total - total_high], axis=0)
+        result = (acc[...] * scale).astype(jnp.bfloat16)
+        for b in range(span_len // HD):
+            out_ref[b * HD : (b + 1) * HD, :] = result[:, b * HD : (b + 1) * HD]
+        stats = jnp.concatenate([stats[:, b * HD : (b + 1) * HD] for b in range(span_len // HD)], axis=0)
+        out_ref[span_len:, :] = stats.astype(jnp.bfloat16)
 
     @pl.when(ids_ref[YH] + later >= QUAD)
     def _():
@@ -226,19 +229,22 @@
 def merge_kernel(ids_ref, counts_ref, part0, part1, part2, part3, out_ref):
     span_len = out_ref.shape[0]
     parts = (part0, part1, part2, part3)
-    bests, totals = [], []
-    for earlier, part in enumerate(parts):
-        stat = part[HD : HD + STAT_ROWS, :].astype(jnp.float32)
-        sent = ids_ref[YH] >= earlier
-        bests.append(jnp.where(sent, (stat[0:1] + stat[1:2]) + stat[2:3], NEG_BIG))
-        totals.append(jnp.where(sent, (stat[3:4] + stat[4:5]) + stat[5:6], 0.0))
-    top = functools.reduce(jnp.maximum, bests)
-    share = [jnp.exp2(b - top) for b in bests]
-    total = sum(s * t for s, t in zip(share, totals))
-    result = sum(s * part[0:HD, :].astype(jnp.float32) for s, part in zip(share, parts))
-    slot = lax.broadcasted_iota(jnp.int32, total.shape, 1)
-    result = jnp.where(slot < counts_ref[ids_ref[SPAN]], result / total, 0.0)
-    out_ref[...] = jnp.transpose(result).astype(jnp.bfloat16)
+    blocks = span_len // HD
+    for block in range(blocks):
+        bests, totals = [], []
+        for earlier, part in enumerate(parts):
+            stat = part[span_len:, :].astype(jnp.float32)[block * 4 : (block + 1) * 4, :]
+            sent = ids_ref[YH] >= earlier
+            bests.append(jnp.where(sent, stat[0:1] + stat[1:2], NEG_BIG))
+            totals.append(jnp.where(sent, stat[2:3] + stat[3:4], 0.0))
+        top = functools.reduce(jnp.maximum, bests)
+        share = [jnp.exp2(b - top) for b in bests]
+        total = sum(s * t for s, t in zip(share, totals))
+        rows = slice(block * HD, (block + 1) * HD)
+        result = sum(s * part[rows, :].astype(jnp.float32) for s, part in zip(share, parts))
+        slot = lax.broadcasted_iota(jnp.int32, total.shape, 1) + block * HD
+        result = jnp.where(slot < counts_ref[ids_ref[SPAN]], result / total, 0.0)
+        out_ref[rows, :] = jnp.transpose(result).astype(jnp.bfloat16)
 
 
 def on_device(tokens, queries, key_weight, value_weight, modulation, levels, visible, counts):
@@ -272,8 +278,8 @@
     a0 = jnp.transpose(tokens)
     x0 = jnp.concatenate([a0, shifted(a0, "xh", 2, 1)], axis=0)
 
-    q_later = [moved(queries, -later) for later in (1, 2, 3)]
-    w0, *q_later = lax.optimization_barrier((w0, *q_later))
+    q1, q2, q3 = (moved(queries, -later) for later in (1, 2, 3))
+    w0, q1, q3 = lax.optimization_barrier((w0, q1, q3))
 
     x_up, x_down, w_up, w_down = [x0], [x0], [w0], [w0]
     y_axes = ("yh", "yl")
@@ -303,6 +309,7 @@
         out_specs=VMEM,
         compiler_params=params(),
     )(ids, own_sums, other_sums, table, *x_slots)
+    normed, q2 = lax.optimization_barrier((normed, q2))
     theirs = shifted(project(1, ids, normed, w_slots), "c", 2, 1)
     mine = project(0, ids, normed, w_slots)
     kv0 = pl.pallas_call(
@@ -326,7 +333,7 @@
         in_specs=[SMEM] * 3 + [VMEM] * 5,
         out_specs=(VMEM,) * 3,
         compiler_params=params(),
-    )(*scalars, queries, *q_later, kv0)
+    )(*scalars, queries, q1, q2, q3, kv0)
     stat, acc = pl.pallas_call(
         middle_kernel,
         out_shape=(stat_type, acc_type),
@@ -339,7 +346,7 @@
     for later in (2, 3, 1, 0):
         part = pl.pallas_call(
             functools.partial(finish_kernel, later),
-            out_shape=jax.ShapeDtypeStruct((HD + STAT_ROWS, span_len), jnp.bfloat16),
+            out_shape=jax.ShapeDtypeStruct((span_len + STAT_ROWS, HD), jnp.bfloat16),
             in_specs=[SMEM] * 3 + [VMEM] * 5,
             out_specs=VMEM,
             scratch_shapes=[pltpu.VMEM((16, span_len), jnp.float32), pltpu.VMEM((HD, span_len), jnp.float32)],

time: 139 us -> 136 us (0.978)
  Pallas kernels: 22.6 us -> 19.3 us
  starting transfers between devices: 91.5 us -> 93.5 us
    ppermute x6, waiting for transfers between devices: 14.3 us -> 9.34 us  [moved(): return lax.ppermute(value, ('yh', 'yl'), pairs)]
    ppermute x21, starting transfers between devices: 79.3 us -> 83.7 us  [shifted(): lax.ppermute(value, axis, [(i, (i + by) % size) for i in range(size)])]
    ppermute x21, waiting for transfers between devices: 6.27 us -> 9.92 us  [shifted(): lax.ppermute(value, axis, [(i, (i + by) % size) for i in range(size)])]
    ppermute x6, starting transfers between devices: 9.28 us -> 7.77 us  [moved(): return lax.ppermute(value, ('yh', 'yl'), pairs)]
  transfers between devices with their start and end apart: 28 -> 28, of which waited for: 8 -> 6; matrix products, arithmetic and copies ran while one was open for 1% -> 1% of each run, Pallas kernels for 12% -> 10%
where the time goes in v5:
time: 136 us; the launch traced here: 135 us
  starting transfers between devices  93.5 us (69%)
  Pallas kernels  19.3 us (14%)
  waiting for transfers between devices  19.3 us (14%)
  local copies, waits for them, and re-layouts  1.93 us (1%)
    ppermute x21, starting transfers between devices, shifted(): lax.ppermute(value, axis, [(i, (i + by) % size) for i in range(size)])  83.7 us
    ppermute x21, waiting for transfers between devices, shifted(): lax.ppermute(value, axis, [(i, (i + by) % size) for i in range(size)])  9.92 us
    ppermute x6, waiting for transfers between devices, moved(): return lax.ppermute(value, ('yh', 'yl'), pairs)  9.34 us
    ppermute x6, starting transfers between devices, moved(): return lax.ppermute(value, ('yh', 'yl'), pairs)  7.77 us
    pallas_call x4, Pallas kernels, on_device(): pl.pallas_call(functools.partial(finish_kernel, later), out_shape=jax.Sha...  5.92 us
    pallas_call x2, Pallas kernels, project(): pl.pallas_call(functools.partial(project_kernel, head), out_shape=jax.Sha...  3.57 us
  transfers between devices with their start and end apart: 28, of which 6 were waited for; matrix products, arithmetic and copies ran while one was open for 1% of the time, Pallas kernels for 10%

profile of v5, /device:TPU:1, one launch (start us, length us, event | category | flops | bytes accessed | tf_op | source)
XLA Modules:
  0.0 135.5 jit_solution(9981485808024757070)
XLA Ops:
  0.1 0.9 copy-done.3
  1.0 0.9 copy-done.4
  1.9 0.6 shard_map.82
  2.5 8.8 %collective-permute-start = (bf16[192,256]{1,0:T(8,128)(2,1)S(1)}, bf16[192,256]{1,0:T(8,128)(2,1)S(1)}, u32[]{:S(2)}, u32[]{:S(2)}) collective-permute-start(bf16[192,256]{1,0:T(8,128)(2,1)S(1)} %get-tuple-element.18), channel_id=1, source_target_pairs={{0,1},{1,0},{2,3},{3,2},{4,5},{5,4},{6,7},{7,6},{8,9},{9,8},{10,11... | collective-permute-start | bytes 294920 | tf_op jit(solution)/shard_map/ppermute | solution.py:31
  11.3 1.9 %collective-permute-start.4 = (bf16[192,512]{1,0:T(8,128)(2,1)}, bf16[192,512]{1,0:T(8,128)(2,1)S(1)}, u32[]{:S(2)}, u32[]{:S(2)}) collective-permute-start(bf16[192,512]{1,0:T(8,128)(2,1)} %bitcast.15), channel_id=1, source_target_pairs={{0,16},{16,0},{1,17},{17,1},{2,18},{18,2},{3,19},{19,3},{4,20},{20... | collective-permute-start | bytes 589832 | tf_op jit(solution)/shard_map/ppermute | solution.py:31
  13.3 1.9 %collective-permute-start.1 = (bf16[2,192,256]{2,1,0:T(8,128)(2,1)S(1)}, bf16[2,192,256]{2,1,0:T(8,128)(2,1)S(1)}, u32[]{:S(2)}, u32[]{:S(2)}) collective-permute-start(bf16[2,192,256]{2,1,0:T(8,128)(2,1)S(1)} %pad_maximum_fusion.2), channel_id=1, source_target_pairs={{0,32},{32,0},{1,33},{33,1},{2,34},{34,2},{3,35},{35,3},{4,36},{36... | collective-permute-start | bytes 589832 | tf_op jit(solution)/shard_map/ppermute | solution.py:31
  15.2 1.3 collective-permute-start.2
  16.5 1.3 collective-permute-start.3
  17.8 3.6 %collective-permute-done.4 = bf16[192,512]{1,0:T(8,128)(2,1)S(1)} collective-permute-done((bf16[192,512]{1,0:T(8,128)(2,1)}, bf16[192,512]{1,0:T(8,128)(2,1)S(1)}, u32[]{:S(2)}, u32[]{:S(2)}) %collective-permute-start.4) | collective-permute-done | bytes 196640 | tf_op jit(solution)/shard_map/ppermute | solution.py:31
  21.4 1.0 pad_maximum_fusion.1.refs_0_
  22.4 1.9 %collective-permute-start.5 = (bf16[384,512]{1,0:T(8,128)(2,1)S(1)}, bf16[384,512]{1,0:T(8,128)(2,1)S(1)}, u32[]{:S(2)}, u32[]{:S(2)}) collective-permute-start(bf16[384,512]{1,0:T(8,128)(2,1)S(1)} %pad_maximum_fusion.1.refs_0_), channel_id=1, source_target_pairs={{0,2},{2,4},{4,6},{6,8},{8,10},{10,12},{12,14},{14,0},{1,3},{3,5},... | collective-permute-start | bytes 1179656 | tf_op jit(solution)/shard_map/ppermute | solution.py:31
  24.4 0.8 collective-permute-done.2.q1
  25.3 3.0 %collective-permute-start.14 = (bf16[4,192,256]{2,1,0:T(8,128)(2,1)S(1)}, bf16[4,192,256]{2,1,0:T(8,128)(2,1)S(1)}, u32[]{:S(2)}, u32[]{:S(2)}) collective-permute-start(bf16[4,192,256]{2,1,0:T(8,128)(2,1)S(1)} %pad_maximum_fusion.refs_0_), channel_id=1, source_target_pairs={{0,448},{64,0},{128,64},{192,128},{256,192},{320,256},{384,320},{4... | collective-permute-start | bytes 1179656 | tf_op jit(solution)/shard_map/ppermute | solution.py:31
  28.3 10.8 %collective-permute-start.9 = (bf16[384,512]{1,0:T(8,128)(2,1)S(1)}, bf16[384,512]{1,0:T(8,128)(2,1)S(1)}, u32[]{:S(2)}, u32[]{:S(2)}) collective-permute-start(bf16[384,512]{1,0:T(8,128)(2,1)S(1)} %pad_maximum_fusion.1.refs_0_), channel_id=1, source_target_pairs={{0,14},{2,0},{4,2},{6,4},{8,6},{10,8},{12,10},{14,12},{1,15},{3,1}... | collective-permute-start | bytes 1179656 | tf_op jit(solution)/shard_map/ppermute | solution.py:31
  39.1 1.9 %collective-permute-start.6 = (bf16[384,512]{1,0:T(8,128)(2,1)S(1)}, bf16[384,512]{1,0:T(8,128)(2,1)S(1)}, u32[]{:S(2)}, u32[]{:S(2)}) collective-permute-start(bf16[384,512]{1,0:T(8,128)(2,1)S(1)} %collective-permute-done.5.refs_6_.refs_7_), channel_id=1, source_target_pairs={{0,2},{2,4},{4,6},{6,8},{8,10},{10,12},{12,14},{14,0},{1,3},{3,5},... | collective-permute-start | bytes 1179656 | tf_op jit(solution)/shard_map/ppermute | solution.py:31
  41.0 3.9 %collective-permute-start.18 = (bf16[4,192,256]{2,1,0:T(8,128)(2,1)S(1)}, bf16[4,192,256]{2,1,0:T(8,128)(2,1)S(1)}, u32[]{:S(2)}, u32[]{:S(2)}) collective-permute-start(bf16[4,192,256]{2,1,0:T(8,128)(2,1)S(1)} %pad_maximum_fusion.refs_0_), channel_id=1, source_target_pairs={{0,64},{64,128},{128,192},{192,256},{256,320},{320,384},{384,448},... | collective-permute-start | bytes 1179656 | tf_op jit(solution)/shard_map/ppermute | solution.py:31
  44.9 2.6 %collective-permute-start.15 = (bf16[4,192,256]{2,1,0:T(8,128)(2,1)S(1)}, bf16[4,192,256]{2,1,0:T(8,128)(2,1)S(1)}, u32[]{:S(2)}, u32[]{:S(2)}) collective-permute-start(bf16[4,192,256]{2,1,0:T(8,128)(2,1)S(1)} %collective-permute-done.14.refs_1_), channel_id=1, source_target_pairs={{0,448},{64,0},{128,64},{192,128},{256,192},{320,256},{384,320},{4... | collective-permute-start | bytes 1179656 | tf_op jit(solution)/shard_map/ppermute | solution.py:31
  47.6 4.6 %collective-permute-start.10 = (bf16[384,512]{1,0:T(8,128)(2,1)S(1)}, bf16[384,512]{1,0:T(8,128)(2,1)S(1)}, u32[]{:S(2)}, u32[]{:S(2)}) collective-permute-start(bf16[384,512]{1,0:T(8,128)(2,1)S(1)} %collective-permute-done.9.refs_1_), channel_id=1, source_target_pairs={{0,14},{2,0},{4,2},{6,4},{8,6},{10,8},{12,10},{14,12},{1,15},{3,1}... | collective-permute-start | bytes 1179656 | tf_op jit(solution)/shard_map/ppermute | solution.py:31
  52.1 1.9 %collective-permute-start.7 = (bf16[384,512]{1,0:T(8,128)(2,1)S(1)}, bf16[384,512]{1,0:T(8,128)(2,1)S(1)}, u32[]{:S(2)}, u32[]{:S(2)}) collective-permute-start(bf16[384,512]{1,0:T(8,128)(2,1)S(1)} %collective-permute-done.6.refs_5_.refs_6_), channel_id=1, source_target_pairs={{0,2},{2,4},{4,6},{6,8},{8,10},{10,12},{12,14},{14,0},{1,3},{3,5},... | collective-permute-start | bytes 1179656 | tf_op jit(solution)/shard_map/ppermute | solution.py:31
  54.1 3.2 %collective-permute-start.19 = (bf16[4,192,256]{2,1,0:T(8,128)(2,1)S(1)}, bf16[4,192,256]{2,1,0:T(8,128)(2,1)S(1)}, u32[]{:S(2)}, u32[]{:S(2)}) collective-permute-start(bf16[4,192,256]{2,1,0:T(8,128)(2,1)S(1)} %collective-permute-done.18.refs_7_), channel_id=1, source_target_pairs={{0,64},{64,128},{128,192},{192,256},{256,320},{320,384},{384,448},... | collective-permute-start | bytes 1179656 | tf_op jit(solution)/shard_map/ppermute | solution.py:31
  57.3 3.2 %collective-permute-start.16 = (bf16[4,192,256]{2,1,0:T(8,128)(2,1)S(1)}, bf16[4,192,256]{2,1,0:T(8,128)(2,1)S(1)}, u32[]{:S(2)}, u32[]{:S(2)}) collective-permute-start(bf16[4,192,256]{2,1,0:T(8,128)(2,1)S(1)} %collective-permute-done.15.refs_2_), channel_id=1, source_target_pairs={{0,448},{64,0},{128,64},{192,128},{256,192},{320,256},{384,320},{4... | collective-permute-start | bytes 1179656 | tf_op jit(solution)/shard_map/ppermute | solution.py:31
  60.6 4.6 %collective-permute-start.11 = (bf16[384,512]{1,0:T(8,128)(2,1)S(1)}, bf16[384,512]{1,0:T(8,128)(2,1)S(1)}, u32[]{:S(2)}, u32[]{:S(2)}) collective-permute-start(bf16[384,512]{1,0:T(8,128)(2,1)S(1)} %collective-permute-done.10.refs_2_), channel_id=1, source_target_pairs={{0,14},{2,0},{4,2},{6,4},{8,6},{10,8},{12,10},{14,12},{1,15},{3,1}... | collective-permute-start | bytes 1179656 | tf_op jit(solution)/shard_map/ppermute | solution.py:31
  65.2 1.9 %collective-permute-start.8 = (bf16[384,512]{1,0:T(8,128)(2,1)S(1)}, bf16[384,512]{1,0:T(8,128)(2,1)S(1)}, u32[]{:S(2)}, u32[]{:S(2)}) collective-permute-start(bf16[384,512]{1,0:T(8,128)(2,1)S(1)} %collective-permute-done.7.refs_4_.refs_5_), channel_id=1, source_target_pairs={{0,2},{2,4},{4,6},{6,8},{8,10},{10,12},{12,14},{14,0},{1,3},{3,5},... | collective-permute-start | bytes 1179656 | tf_op jit(solution)/shard_map/ppermute | solution.py:31
  67.1 2.0 %collective-permute-start.20 = (bf16[4,192,256]{2,1,0:T(8,128)(2,1)S(1)}, bf16[4,192,256]{2,1,0:T(8,128)(2,1)S(1)}, u32[]{:S(2)}, u32[]{:S(2)}) collective-permute-start(bf16[4,192,256]{2,1,0:T(8,128)(2,1)S(1)} %collective-permute-done.19.refs_6_), channel_id=1, source_target_pairs={{0,64},{64,128},{128,192},{192,256},{256,320},{320,384},{384,448},... | collective-permute-start | bytes 1179656 | tf_op jit(solution)/shard_map/ppermute | solution.py:31
  69.2 4.5 %collective-permute-start.17 = (bf16[4,192,256]{2,1,0:T(8,128)(2,1)S(1)}, bf16[4,192,256]{2,1,0:T(8,128)(2,1)S(1)}, u32[]{:S(2)}, u32[]{:S(2)}) collective-permute-start(bf16[4,192,256]{2,1,0:T(8,128)(2,1)S(1)} %collective-permute-done.16.refs_3_), channel_id=1, source_target_pairs={{0,448},{64,0},{128,64},{192,128},{256,192},{320,256},{384,320},{4... | collective-permute-start | bytes 1179656 | tf_op jit(solution)/shard_map/ppermute | solution.py:31
  73.7 1.3 collective-permute-start.13
  75.6 6.7 %collective-permute-start.12 = (f32[8,512]{1,0:T(8,128)S(1)}, f32[8,512]{1,0:T(8,128)S(1)}, u32[]{:S(2)}, u32[]{:S(2)}) collective-permute-start(f32[8,512]{1,0:T(8,128)S(1)} %shard_map.84.own_ref), channel_id=1, source_target_pairs={{0,1},{1,0},{2,3},{3,2},{4,5},{5,4},{6,7},{7,6},{8,9},{9,8},{10,11... | collective-permute-start | bytes 49160 | tf_op jit(solution)/shard_map/ppermute | solution.py:31
  82.3 0.7 shard_map.85.table_ref
  83.1 2.6 %shard_map.86.normed_ref = bf16[8,2,512,192]{3,2,1,0:T(8,128)(2,1)S(1)} custom-call(s32[8]{0:T(128)S(1)} %stack.44.ids_ref, f32[8,512]{1,0:T(8,128)S(1)} %shard_map.84.own_ref, f32[8,512]{1,0:T(8,128)S(1)} %collective-permute-done.12.other_ref, f32[64,192]{1,0:T(8,128)S(1)} %shard_map.85.table_ref, bf16[384,512]{1,0:T(8,128)(2,1)S(1)} %pad_maximum_fusion.1.refs_0_, ...), custom_call_target="tpu_custom_call" | custom-call | tf_op jit(solution)/shard_map/pallas_call | solution.py:305
  85.7 1.8 %shard_map.88 = f32[512,256]{1,0:T(8,128)S(1)} custom-call(s32[8]{0:T(128)S(1)} %stack.44.ids_ref, bf16[8,2,512,192]{3,2,1,0:T(8,128)(2,1)S(1)} %shard_map.86.normed_ref, bf16[4,192,256]{2,1,0:T(8,128)(2,1)S(1)} %pad_maximum_fusion.refs_0_, bf16[4,192,256]{2,1,0:T(8,128)(2,1)S(1)} %collective-permute-done.14.refs_1_, ...), custom_call_target="tpu_custom_call" | custom-call | tf_op jit(solution)/shard_map/pallas_call | solution.py:134
  87.6 4.8 %collective-permute-start.21 = (f32[512,256]{1,0:T(8,128)S(1)}, f32[512,256]{1,0:T(8,128)S(1)}, u32[]{:S(2)}, u32[]{:S(2)}) collective-permute-start(f32[512,256]{1,0:T(8,128)S(1)} %shard_map.88), channel_id=1, source_target_pairs={{0,1},{1,0},{2,3},{3,2},{4,5},{5,4},{6,7},{7,6},{8,9},{9,8},{10,11... | collective-permute-start | bytes 1572872 | tf_op jit(solution)/shard_map/ppermute | solution.py:31
  92.4 1.8 %shard_map.87.mine_ref = f32[512,256]{1,0:T(8,128)S(1)} custom-call(s32[8]{0:T(128)S(1)} %stack.44.ids_ref, bf16[8,2,512,192]{3,2,1,0:T(8,128)(2,1)S(1)} %shard_map.86.normed_ref, bf16[4,192,256]{2,1,0:T(8,128)(2,1)S(1)} %pad_maximum_fusion.refs_0_, bf16[4,192,256]{2,1,0:T(8,128)(2,1)S(1)} %collective-permute-done.14.refs_1_, ...), custom_call_target="tpu_custom_call" | custom-call | tf_op jit(solution)/shard_map/pallas_call | solution.py:134
  94.3 6.5 %collective-permute-start.22 = (bf16[1024,128]{1,0:T(8,128)(2,1)S(1)}, bf16[1024,128]{1,0:T(8,128)(2,1)S(1)}, u32[]{:S(2)}, u32[]{:S(2)}) collective-permute-start(bf16[1024,128]{1,0:T(8,128)(2,1)S(1)} %shard_map.89.kv_ref), channel_id=1, source_target_pairs={{0,64},{64,0},{1,65},{65,1},{2,66},{66,2},{3,67},{67,3},{4,68},{68... | collective-permute-start | bytes 786440 | tf_op jit(solution)/shard_map/ppermute | solution.py:31
  100.8 3.1 %collective-permute-start.23 = (bf16[1024,128]{1,0:T(8,128)(2,1)S(1)}, bf16[1024,128]{1,0:T(8,128)(2,1)S(1)}, u32[]{:S(2)}, u32[]{:S(2)}) collective-permute-start(bf16[1024,128]{1,0:T(8,128)(2,1)S(1)} %shard_map.89.kv_ref), channel_id=1, source_target_pairs={{0,32},{32,0},{1,33},{33,1},{2,34},{34,2},{3,35},{35,3},{4,36},{36... | collective-permute-start | bytes 786440 | tf_op jit(solution)/shard_map/ppermute | solution.py:31
  103.8 1.9 %collective-permute-start.24 = (bf16[1024,128]{1,0:T(8,128)(2,1)S(1)}, bf16[1024,128]{1,0:T(8,128)(2,1)S(1)}, u32[]{:S(2)}, u32[]{:S(2)}) collective-permute-start(bf16[1024,128]{1,0:T(8,128)(2,1)S(1)} %shard_map.89.kv_ref), channel_id=1, source_target_pairs={{0,96},{32,64},{64,32},{96,0},{1,97},{33,65},{65,33},{97,1},{2,98}... | collective-permute-start | bytes 786440 | tf_op jit(solution)/shard_map/ppermute | solution.py:325
  105.8 2.4 %shard_map.90 = (bf16[4,128,512]{2,1,0:T(8,128)(2,1)S(1)}, f32[4,16,512]{2,1,0:T(8,128)S(1)}, f32[4,128,512]{2,1,0:T(8,128)S(1)}) custom-call(s32[8]{0:T(128)S(1)} %stack.44.ids_ref, s32[16,16]{1,0:T(8,128)S(1)} %copy-done, s32[16]{0:T(128)S(1)} %copy-done.5, bf16[512,128]{1,0:T(8,128)(2,1)S(1)} %copy-done.2, ...), custom_call_target="tpu_custom_call" | custom-call | tf_op jit(solution)/shard_map/pallas_call | solution.py:330
  108.2 1.4 %shard_map.91 = (f32[4,16,512]{2,1,0:T(8,128)S(1)}, f32[4,128,512]{2,1,0:T(8,128)S(1)}) custom-call(s32[8]{0:T(128)S(1)} %stack.44.ids_ref, s32[16,16]{1,0:T(8,128)S(1)} %copy-done, s32[16]{0:T(128)S(1)} %copy-done.5, bf16[4,128,512]{2,1,0:T(8,128)(2,1)S(1)} %get-tuple-element.24.q_t, ...), custom_call_target="tpu_custom_call", output_to_operand_aliasing={{0}: (4, {}), {1}: (5, {})} | custom-call | tf_op jit(solution)/shard_map/pallas_call | solution.py:337
  109.6 6.2 %collective-permute-done.23.kv1 = bf16[1024,128]{1,0:T(8,128)(2,1)S(1)} collective-permute-done((bf16[1024,128]{1,0:T(8,128)(2,1)S(1)}, bf16[1024,128]{1,0:T(8,128)(2,1)S(1)}, u32[]{:S(2)}, u32[]{:S(2)}) %collective-permute-start.23) | collective-permute-done | bytes 262176 | tf_op jit(solution)/shard_map/ppermute | solution.py:31
  115.8 2.3 %shard_map.93 = bf16[528,128]{1,0:T(8,128)(2,1)S(1)} custom-call(s32[8]{0:T(128)S(1)} %stack.44.ids_ref, s32[16,16]{1,0:T(8,128)S(1)} %copy-done, s32[16]{0:T(128)S(1)} %copy-done.5, bf16[4,128,512]{2,1,0:T(8,128)(2,1)S(1)} %get-tuple-element.24.q_t, f32[4,16,512]{2,1,0:T(8,128)S(1)} %get-tuple-element.27.stat_in, ...), custom_call_target="tpu_custom_call" | custom-call | tf_op jit(solution)/shard_map/pallas_call | solution.py:347
  118.1 1.3 collective-permute-start.25
  119.4 1.4 %shard_map.94 = bf16[528,128]{1,0:T(8,128)(2,1)S(1)} custom-call(s32[8]{0:T(128)S(1)} %stack.44.ids_ref, s32[16,16]{1,0:T(8,128)S(1)} %copy-done, s32[16]{0:T(128)S(1)} %copy-done.5, bf16[4,128,512]{2,1,0:T(8,128)(2,1)S(1)} %get-tuple-element.24.q_t, f32[4,16,512]{2,1,0:T(8,128)S(1)} %get-tuple-element.27.stat_in, ...), custom_call_target="tpu_custom_call" | custom-call | tf_op jit(solution)/shard_map/pallas_call | solution.py:347
  120.9 1.3 collective-permute-start.26
  122.2 1.4 %shard_map.95 = bf16[528,128]{1,0:T(8,128)(2,1)S(1)} custom-call(s32[8]{0:T(128)S(1)} %stack.44.ids_ref, s32[16,16]{1,0:T(8,128)S(1)} %copy-done, s32[16]{0:T(128)S(1)} %copy-done.5, bf16[4,128,512]{2,1,0:T(8,128)(2,1)S(1)} %get-tuple-element.24.q_t, f32[4,16,512]{2,1,0:T(8,128)S(1)} %get-tuple-element.27.stat_in, ...), custom_call_target="tpu_custom_call" | custom-call | tf_op jit(solution)/shard_map/pallas_call | solution.py:347
  123.6 1.3 collective-permute-start.27
  124.9 0.8 shard_map.92.part0
  125.7 5.5 %collective-permute-done.26.part2 = bf16[528,128]{1,0:T(8,128)(2,1)S(1)} collective-permute-done((bf16[528,128]{1,0:T(8,128)(2,1)S(1)}, bf16[528,128]{1,0:T(8,128)(2,1)S(1)}, u32[]{:S(2)}, u32[]{:S(2)}) %collective-permute-start.26) | collective-permute-done | bytes 135200 | tf_op jit(solution)/shard_map/ppermute | solution.py:44
  131.2 2.9 %collective-permute-done.27.part3 = bf16[528,128]{1,0:T(8,128)(2,1)S(1)} collective-permute-done((bf16[528,128]{1,0:T(8,128)(2,1)S(1)}, bf16[528,128]{1,0:T(8,128)(2,1)S(1)}, u32[]{:S(2)}, u32[]{:S(2)}) %collective-permute-start.27) | collective-permute-done | bytes 135200 | tf_op jit(solution)/shard_map/ppermute | solution.py:44
  134.1 1.4 %shard_map.96 = bf16[512,128]{1,0:T(8,128)(2,1)} custom-call(s32[8]{0:T(128)S(1)} %stack.44.ids_ref, s32[16]{0:T(128)S(1)} %copy-done.5, bf16[528,128]{1,0:T(8,128)(2,1)S(1)} %shard_map.92.part0, bf16[528,128]{1,0:T(8,128)(2,1)S(1)} %collective-permute-done.25.part1, bf16[528,128]{1,0:T(8,128)(2,1)S(1)} %collective-permute-done.26.part2, ...), custom_call_target="tpu_custom_call" | custom-call | tf_op jit(solution)/shard_map/pallas_call | solution.py:356
  (41 shorter events, 1.2 us)
Async XLA Ops:
  0.0 82.3 %copy-start.1 = (bf16[8,12288]{1,0:T(8,128)(2,1)S(1)}, bf16[8,12288]{1,0:T(8,128)(2,1)}, u32[]{:S(2)}) copy-start(bf16[8,12288]{1,0:T(8,128)(2,1)} %modulation_ref.1) | copy-start | bytes 589828
  0.1 0.9 copy-start.3
  1.0 0.9 copy-start.4
  1.9 80.4 %copy-start.6 = (s32[16]{0:T(128)S(1)}, s32[16]{0:T(128)}, u32[]{:S(2)}) copy-start(s32[16]{0:T(128)} %levels_ref.1) | copy-start | bytes 196
  2.5 10.7 %collective-permute-start = (bf16[192,256]{1,0:T(8,128)(2,1)S(1)}, bf16[192,256]{1,0:T(8,128)(2,1)S(1)}, u32[]{:S(2)}, u32[]{:S(2)}) collective-permute-start(bf16[192,256]{1,0:T(8,128)(2,1)S(1)} %get-tuple-element.18), channel_id=1, source_target_pairs={{0,1},{1,0},{2,3},{3,2},{4,5},{5,4},{6,7},{7,6},{8,9},{9,8},{10,11... | collective-permute-start | bytes 294920 | tf_op jit(solution)/shard_map/ppermute | solution.py:31
  11.3 10.1 %collective-permute-start.4 = (bf16[192,512]{1,0:T(8,128)(2,1)}, bf16[192,512]{1,0:T(8,128)(2,1)S(1)}, u32[]{:S(2)}, u32[]{:S(2)}) collective-permute-start(bf16[192,512]{1,0:T(8,128)(2,1)} %bitcast.15), channel_id=1, source_target_pairs={{0,16},{16,0},{1,17},{17,1},{2,18},{18,2},{3,19},{19,3},{4,20},{20... | collective-permute-start | bytes 589832 | tf_op jit(solution)/shard_map/ppermute | solution.py:31
  13.3 11.0 %collective-permute-start.1 = (bf16[2,192,256]{2,1,0:T(8,128)(2,1)S(1)}, bf16[2,192,256]{2,1,0:T(8,128)(2,1)S(1)}, u32[]{:S(2)}, u32[]{:S(2)}) collective-permute-start(bf16[2,192,256]{2,1,0:T(8,128)(2,1)S(1)} %pad_maximum_fusion.2), channel_id=1, source_target_pairs={{0,32},{32,0},{1,33},{33,1},{2,34},{34,2},{3,35},{35,3},{4,36},{36... | collective-permute-start | bytes 589832 | tf_op jit(solution)/shard_map/ppermute | solution.py:31
  15.2 10.0 %collective-permute-start.2 = (bf16[512,128]{1,0:T(8,128)(2,1)}, bf16[512,128]{1,0:T(8,128)(2,1)S(1)}, u32[]{:S(2)}, u32[]{:S(2)}) collective-permute-start(bf16[512,128]{1,0:T(8,128)(2,1)} %q0.1), channel_id=1, source_target_pairs={{128,0},{192,64},{256,128},{320,192},{384,256},{448,320},{129,1},{... | collective-permute-start | bytes 393224 | tf_op jit(solution)/shard_map/ppermute | solution.py:44
  16.5 8.8 %collective-permute-start.3 = (bf16[512,128]{1,0:T(8,128)(2,1)}, bf16[512,128]{1,0:T(8,128)(2,1)S(1)}, u32[]{:S(2)}, u32[]{:S(2)}) collective-permute-start(bf16[512,128]{1,0:T(8,128)(2,1)} %q0.1), channel_id=1, source_target_pairs={{384,0},{448,64},{385,1},{449,65},{386,2},{450,66},{387,3},{451,67... | collective-permute-start | bytes 393224 | tf_op jit(solution)/shard_map/ppermute | solution.py:44
  22.4 16.7 %collective-permute-start.5 = (bf16[384,512]{1,0:T(8,128)(2,1)S(1)}, bf16[384,512]{1,0:T(8,128)(2,1)S(1)}, u32[]{:S(2)}, u32[]{:S(2)}) collective-permute-start(bf16[384,512]{1,0:T(8,128)(2,1)S(1)} %pad_maximum_fusion.1.refs_0_), channel_id=1, source_target_pairs={{0,2},{2,4},{4,6},{6,8},{8,10},{10,12},{12,14},{14,0},{1,3},{3,5},... | collective-permute-start | bytes 1179656 | tf_op jit(solution)/shard_map/ppermute | solution.py:31
  25.3 19.6 %collective-permute-start.14 = (bf16[4,192,256]{2,1,0:T(8,128)(2,1)S(1)}, bf16[4,192,256]{2,1,0:T(8,128)(2,1)S(1)}, u32[]{:S(2)}, u32[]{:S(2)}) collective-permute-start(bf16[4,192,256]{2,1,0:T(8,128)(2,1)S(1)} %pad_maximum_fusion.refs_0_), channel_id=1, source_target_pairs={{0,448},{64,0},{128,64},{192,128},{256,192},{320,256},{384,320},{4... | collective-permute-start | bytes 1179656 | tf_op jit(solution)/shard_map/ppermute | solution.py:31
  28.3 19.2 %collective-permute-start.9 = (bf16[384,512]{1,0:T(8,128)(2,1)S(1)}, bf16[384,512]{1,0:T(8,128)(2,1)S(1)}, u32[]{:S(2)}, u32[]{:S(2)}) collective-permute-start(bf16[384,512]{1,0:T(8,128)(2,1)S(1)} %pad_maximum_fusion.1.refs_0_), channel_id=1, source_target_pairs={{0,14},{2,0},{4,2},{6,4},{8,6},{10,8},{12,10},{14,12},{1,15},{3,1}... | collective-permute-start | bytes 1179656 | tf_op jit(solution)/shard_map/ppermute | solution.py:31
  39.1 13.0 %collective-permute-start.6 = (bf16[384,512]{1,0:T(8,128)(2,1)S(1)}, bf16[384,512]{1,0:T(8,128)(2,1)S(1)}, u32[]{:S(2)}, u32[]{:S(2)}) collective-permute-start(bf16[384,512]{1,0:T(8,128)(2,1)S(1)} %collective-permute-done.5.refs_6_.refs_7_), channel_id=1, source_target_pairs={{0,2},{2,4},{4,6},{6,8},{8,10},{10,12},{12,14},{14,0},{1,3},{3,5},... | collective-permute-start | bytes 1179656 | tf_op jit(solution)/shard_map/ppermute | solution.py:31
  41.0 13.1 %collective-permute-start.18 = (bf16[4,192,256]{2,1,0:T(8,128)(2,1)S(1)}, bf16[4,192,256]{2,1,0:T(8,128)(2,1)S(1)}, u32[]{:S(2)}, u32[]{:S(2)}) collective-permute-start(bf16[4,192,256]{2,1,0:T(8,128)(2,1)S(1)} %pad_maximum_fusion.refs_0_), channel_id=1, source_target_pairs={{0,64},{64,128},{128,192},{192,256},{256,320},{320,384},{384,448},... | collective-permute-start | bytes 1179656 | tf_op jit(solution)/shard_map/ppermute | solution.py:31
  44.9 12.4 %collective-permute-start.15 = (bf16[4,192,256]{2,1,0:T(8,128)(2,1)S(1)}, bf16[4,192,256]{2,1,0:T(8,128)(2,1)S(1)}, u32[]{:S(2)}, u32[]{:S(2)}) collective-permute-start(bf16[4,192,256]{2,1,0:T(8,128)(2,1)S(1)} %collective-permute-done.14.refs_1_), channel_id=1, source_target_pairs={{0,448},{64,0},{128,64},{192,128},{256,192},{320,256},{384,320},{4... | collective-permute-start | bytes 1179656 | tf_op jit(solution)/shard_map/ppermute | solution.py:31
  47.6 13.1 %collective-permute-start.10 = (bf16[384,512]{1,0:T(8,128)(2,1)S(1)}, bf16[384,512]{1,0:T(8,128)(2,1)S(1)}, u32[]{:S(2)}, u32[]{:S(2)}) collective-permute-start(bf16[384,512]{1,0:T(8,128)(2,1)S(1)} %collective-permute-done.9.refs_1_), channel_id=1, source_target_pairs={{0,14},{2,0},{4,2},{6,4},{8,6},{10,8},{12,10},{14,12},{1,15},{3,1}... | collective-permute-start | bytes 1179656 | tf_op jit(solution)/shard_map/ppermute | solution.py:31
  52.1 13.1 %collective-permute-start.7 = (bf16[384,512]{1,0:T(8,128)(2,1)S(1)}, bf16[384,512]{1,0:T(8,128)(2,1)S(1)}, u32[]{:S(2)}, u32[]{:S(2)}) collective-permute-start(bf16[384,512]{1,0:T(8,128)(2,1)S(1)} %collective-permute-done.6.refs_5_.refs_6_), channel_id=1, source_target_pairs={{0,2},{2,4},{4,6},{6,8},{8,10},{10,12},{12,14},{14,0},{1,3},{3,5},... | collective-permute-start | bytes 1179656 | tf_op jit(solution)/shard_map/ppermute | solution.py:31
  54.1 13.1 %collective-permute-start.19 = (bf16[4,192,256]{2,1,0:T(8,128)(2,1)S(1)}, bf16[4,192,256]{2,1,0:T(8,128)(2,1)S(1)}, u32[]{:S(2)}, u32[]{:S(2)}) collective-permute-start(bf16[4,192,256]{2,1,0:T(8,128)(2,1)S(1)} %collective-permute-done.18.refs_7_), channel_id=1, source_target_pairs={{0,64},{64,128},{128,192},{192,256},{256,320},{320,384},{384,448},... | collective-permute-start | bytes 1179656 | tf_op jit(solution)/shard_map/ppermute | solution.py:31
  57.3 11.8 %collective-permute-start.16 = (bf16[4,192,256]{2,1,0:T(8,128)(2,1)S(1)}, bf16[4,192,256]{2,1,0:T(8,128)(2,1)S(1)}, u32[]{:S(2)}, u32[]{:S(2)}) collective-permute-start(bf16[4,192,256]{2,1,0:T(8,128)(2,1)S(1)} %collective-permute-done.15.refs_2_), channel_id=1, source_target_pairs={{0,448},{64,0},{128,64},{192,128},{256,192},{320,256},{384,320},{4... | collective-permute-start | bytes 1179656 | tf_op jit(solution)/shard_map/ppermute | solution.py:31
  60.6 14.4 %collective-permute-start.11 = (bf16[384,512]{1,0:T(8,128)(2,1)S(1)}, bf16[384,512]{1,0:T(8,128)(2,1)S(1)}, u32[]{:S(2)}, u32[]{:S(2)}) collective-permute-start(bf16[384,512]{1,0:T(8,128)(2,1)S(1)} %collective-permute-done.10.refs_2_), channel_id=1, source_target_pairs={{0,14},{2,0},{4,2},{6,4},{8,6},{10,8},{12,10},{14,12},{1,15},{3,1}... | collective-permute-start | bytes 1179656 | tf_op jit(solution)/shard_map/ppermute | solution.py:31
  65.2 10.3 %collective-permute-start.8 = (bf16[384,512]{1,0:T(8,128)(2,1)S(1)}, bf16[384,512]{1,0:T(8,128)(2,1)S(1)}, u32[]{:S(2)}, u32[]{:S(2)}) collective-permute-start(bf16[384,512]{1,0:T(8,128)(2,1)S(1)} %collective-permute-done.7.refs_4_.refs_5_), channel_id=1, source_target_pairs={{0,2},{2,4},{4,6},{6,8},{8,10},{10,12},{12,14},{14,0},{1,3},{3,5},... | collective-permute-start | bytes 1179656 | tf_op jit(solution)/shard_map/ppermute | solution.py:31
  67.1 18.6 %collective-permute-start.20 = (bf16[4,192,256]{2,1,0:T(8,128)(2,1)S(1)}, bf16[4,192,256]{2,1,0:T(8,128)(2,1)S(1)}, u32[]{:S(2)}, u32[]{:S(2)}) collective-permute-start(bf16[4,192,256]{2,1,0:T(8,128)(2,1)S(1)} %collective-permute-done.19.refs_6_), channel_id=1, source_target_pairs={{0,64},{64,128},{128,192},{192,256},{256,320},{320,384},{384,448},... | collective-permute-start | bytes 1179656 | tf_op jit(solution)/shard_map/ppermute | solution.py:31
  69.2 16.5 %collective-permute-start.17 = (bf16[4,192,256]{2,1,0:T(8,128)(2,1)S(1)}, bf16[4,192,256]{2,1,0:T(8,128)(2,1)S(1)}, u32[]{:S(2)}, u32[]{:S(2)}) collective-permute-start(bf16[4,192,256]{2,1,0:T(8,128)(2,1)S(1)} %collective-permute-done.16.refs_3_), channel_id=1, source_target_pairs={{0,448},{64,0},{128,64},{192,128},{256,192},{320,256},{384,320},{4... | collective-permute-start | bytes 1179656 | tf_op jit(solution)/shard_map/ppermute | solution.py:31
  73.7 12.0 %collective-permute-start.13 = (bf16[512,128]{1,0:T(8,128)(2,1)}, bf16[512,128]{1,0:T(8,128)(2,1)S(1)}, u32[]{:S(2)}, u32[]{:S(2)}) collective-permute-start(bf16[512,128]{1,0:T(8,128)(2,1)} %q0.1), channel_id=1, source_target_pairs={{256,64},{320,0},{384,192},{448,128},{257,65},{321,1},{385,193},{4... | collective-permute-start | bytes 393224 | tf_op jit(solution)/shard_map/ppermute | solution.py:44
  75.6 7.5 %collective-permute-start.12 = (f32[8,512]{1,0:T(8,128)S(1)}, f32[8,512]{1,0:T(8,128)S(1)}, u32[]{:S(2)}, u32[]{:S(2)}) collective-permute-start(f32[8,512]{1,0:T(8,128)S(1)} %shard_map.84.own_ref), channel_id=1, source_target_pairs={{0,1},{1,0},{2,3},{3,2},{4,5},{5,4},{6,7},{7,6},{8,9},{9,8},{10,11... | collective-permute-start | bytes 49160 | tf_op jit(solution)/shard_map/ppermute | solution.py:31
  87.5 18.3 %copy-start = (s32[16,16]{1,0:T(8,128)S(1)}, s32[16,16]{1,0:T(8,128)}, u32[]{:S(2)}) copy-start(s32[16,16]{1,0:T(8,128)} %visible_ref.11) | copy-start | bytes 3076
  87.5 18.3 %copy-start.2 = (bf16[512,128]{1,0:T(8,128)(2,1)S(1)}, bf16[512,128]{1,0:T(8,128)(2,1)}, u32[]{:S(2)}) copy-start(bf16[512,128]{1,0:T(8,128)(2,1)} %q0.1) | copy-start | bytes 393220
  87.6 18.3 %copy-start.5 = (s32[16]{0:T(128)S(1)}, s32[16]{0:T(128)}, u32[]{:S(2)}) copy-start(s32[16]{0:T(128)} %counts_ref.13) | copy-start | bytes 196
  87.6 6.6 %collective-permute-start.21 = (f32[512,256]{1,0:T(8,128)S(1)}, f32[512,256]{1,0:T(8,128)S(1)}, u32[]{:S(2)}, u32[]{:S(2)}) collective-permute-start(f32[512,256]{1,0:T(8,128)S(1)} %shard_map.88), channel_id=1, source_target_pairs={{0,1},{1,0},{2,3},{3,2},{4,5},{5,4},{6,7},{7,6},{8,9},{9,8},{10,11... | collective-permute-start | bytes 1572872 | tf_op jit(solution)/shard_map/ppermute | solution.py:31
  94.3 13.9 %collective-permute-start.22 = (bf16[1024,128]{1,0:T(8,128)(2,1)S(1)}, bf16[1024,128]{1,0:T(8,128)(2,1)S(1)}, u32[]{:S(2)}, u32[]{:S(2)}) collective-permute-start(bf16[1024,128]{1,0:T(8,128)(2,1)S(1)} %shard_map.89.kv_ref), channel_id=1, source_target_pairs={{0,64},{64,0},{1,65},{65,1},{2,66},{66,2},{3,67},{67,3},{4,68},{68... | collective-permute-start | bytes 786440 | tf_op jit(solution)/shard_map/ppermute | solution.py:31
  100.8 15.1 %collective-permute-start.23 = (bf16[1024,128]{1,0:T(8,128)(2,1)S(1)}, bf16[1024,128]{1,0:T(8,128)(2,1)S(1)}, u32[]{:S(2)}, u32[]{:S(2)}) collective-permute-start(bf16[1024,128]{1,0:T(8,128)(2,1)S(1)} %shard_map.89.kv_ref), channel_id=1, source_target_pairs={{0,32},{32,0},{1,33},{33,1},{2,34},{34,2},{3,35},{35,3},{4,36},{36... | collective-permute-start | bytes 786440 | tf_op jit(solution)/shard_map/ppermute | solution.py:31
  103.8 12.0 %collective-permute-start.24 = (bf16[1024,128]{1,0:T(8,128)(2,1)S(1)}, bf16[1024,128]{1,0:T(8,128)(2,1)S(1)}, u32[]{:S(2)}, u32[]{:S(2)}) collective-permute-start(bf16[1024,128]{1,0:T(8,128)(2,1)S(1)} %shard_map.89.kv_ref), channel_id=1, source_target_pairs={{0,96},{32,64},{64,32},{96,0},{1,97},{33,65},{65,33},{97,1},{2,98}... | collective-permute-start | bytes 786440 | tf_op jit(solution)/shard_map/ppermute | solution.py:325
  118.1 7.6 %collective-permute-start.25 = (bf16[528,128]{1,0:T(8,128)(2,1)S(1)}, bf16[528,128]{1,0:T(8,128)(2,1)S(1)}, u32[]{:S(2)}, u32[]{:S(2)}) collective-permute-start(bf16[528,128]{1,0:T(8,128)(2,1)S(1)} %shard_map.93), channel_id=1, source_target_pairs={{0,128},{64,192},{128,256},{192,320},{256,384},{320,448},{1,129},{... | collective-permute-start | bytes 405512 | tf_op jit(solution)/shard_map/ppermute | solution.py:44
  120.9 10.3 %collective-permute-start.26 = (bf16[528,128]{1,0:T(8,128)(2,1)S(1)}, bf16[528,128]{1,0:T(8,128)(2,1)S(1)}, u32[]{:S(2)}, u32[]{:S(2)}) collective-permute-start(bf16[528,128]{1,0:T(8,128)(2,1)S(1)} %shard_map.94), channel_id=1, source_target_pairs={{0,320},{64,256},{128,448},{192,384},{1,321},{65,257},{129,449},{1... | collective-permute-start | bytes 405512 | tf_op jit(solution)/shard_map/ppermute | solution.py:44
  123.6 10.5 %collective-permute-start.27 = (bf16[528,128]{1,0:T(8,128)(2,1)S(1)}, bf16[528,128]{1,0:T(8,128)(2,1)S(1)}, u32[]{:S(2)}, u32[]{:S(2)}) collective-permute-start(bf16[528,128]{1,0:T(8,128)(2,1)S(1)} %shard_map.95), channel_id=1, source_target_pairs={{0,384},{64,448},{1,385},{65,449},{2,386},{66,450},{3,387},{67,451... | collective-permute-start | bytes 405512 | tf_op jit(solution)/shard_map/ppermute | solution.py:44

commit v6 on v5

--- a/solution.py
+++ b/solution.py
@@ -42,6 +42,24 @@
             if 0 <= yh + by < QUAD:
                 pairs.append((2 * yh + yl, 2 * (yh + by) + turned(2 * yl, abs(by)) // 2))
     return lax.ppermute(value, ("yh", "yl"), pairs)
+
+
+def stack_kernel(*refs):
+    out_ref, first = refs[-1], 0
+    for ref in refs[:-1]:
+        out_ref[first : first + ref.shape[0]] = ref[...]
+        first += ref.shape[0]
+
+
+def stacked(*pieces):
+    rows = sum(piece.shape[0] for piece in pieces)
+    return pl.pallas_call(
+        stack_kernel,
+        out_shape=jax.ShapeDtypeStruct((rows,) + pieces[0].shape[1:], pieces[0].dtype),
+        in_specs=[VMEM] * len(pieces),
+        out_specs=VMEM,
+        compiler_params=params(),
+    )(*pieces)
 
 
 def split_kernel(ids_ref, key_ref, value_ref, own_ref, other_ref):
@@ -264,19 +282,20 @@
     span_len, feats = tokens.shape
     depth = key_weight.shape[0] // 2
 
-    w_type = jax.ShapeDtypeStruct((depth, 2 * HD), jnp.bfloat16)
-    w_own, w_other = pl.pallas_call(
-        split_kernel,
-        out_shape=(w_type, w_type),
-        in_specs=[SMEM, VMEM, VMEM],
-        out_specs=(VMEM, VMEM),
-        compiler_params=params(),
-    )(ids, key_weight, value_weight)
+    def rows_of(part):
+        first = part * depth
+        return jnp.concatenate(
+            [lax.dynamic_slice_in_dim(w, first, depth, 0) for w in (key_weight, value_weight)], axis=1
+        )
+
+    core = lax.axis_index("c")
+    w_own, w_other = rows_of(core), rows_of(1 - core)
+    w_other, ids = lax.optimization_barrier((w_other, ids))
     w_chip = jnp.stack([w_own, shifted(w_other, "c", 2, 1)])
-    w0 = jnp.concatenate([w_chip, shifted(w_chip, "xl", 2, 1)], axis=0)
+    w0 = stacked(w_chip, shifted(w_chip, "xl", 2, 1))
 
     a0 = jnp.transpose(tokens)
-    x0 = jnp.concatenate([a0, shifted(a0, "xh", 2, 1)], axis=0)
+    x0 = stacked(a0, shifted(a0, "xh", 2, 1))
 
     q1, q2, q3 = (moved(queries, -later) for later in (1, 2, 3))
     w0, q1, q3 = lax.optimization_barrier((w0, q1, q3))

time: 136 us -> 134 us (0.985)
  waiting for transfers between devices: 19.3 us -> 17.7 us
  transfers between devices with their start and end apart: 28 -> 28, of which waited for: 6 -> 6; matrix products, arithmetic and copies ran while one was open for 1% -> 0% of each run, Pallas kernels for 10% -> 11%
where the time goes in v6:
time: 134 us; the launch traced here: 133 us
  starting transfers between devices  93.6 us (70%)
  Pallas kernels  19.4 us (14%)
  waiting for transfers between devices  17.7 us (13%)
  local copies, waits for them, and re-layouts  1.96 us (1%)
    ppermute x21, starting transfers between devices, shifted(): lax.ppermute(value, axis, [(i, (i + by) % size) for i in range(size)])  83.7 us
    ppermute x6, waiting for transfers between devices, moved(): return lax.ppermute(value, ('yh', 'yl'), pairs)  9.17 us
    ppermute x21, waiting for transfers between devices, shifted(): lax.ppermute(value, axis, [(i, (i + by) % size) for i in range(size)])  8.57 us
    ppermute x6, starting transfers between devices, moved(): return lax.ppermute(value, ('yh', 'yl'), pairs)  7.92 us
    pallas_call x4, Pallas kernels, on_device(): pl.pallas_call(functools.partial(finish_kernel, later), out_shape=jax.Sha...  5.25 us
    pallas_call x2, Pallas kernels, project(): pl.pallas_call(functools.partial(project_kernel, head), out_shape=jax.Sha...  3.57 us
    pallas_call x1, Pallas kernels, on_device(): pl.pallas_call(begin_kernel, out_shape=(q_type, stat_type, acc_type), in_...  3.03 us
  transfers between devices with their start and end apart: 28, of which 6 were waited for; matrix products, arithmetic and copies ran while one was open for 0% of the time, Pallas kernels for 11%

profile of v6, /device:TPU:1, one launch (start us, length us, event | category | flops | bytes accessed | tf_op | source)
XLA Modules:
  0.0 133.3 jit_solution(4742838269266059347)
XLA Ops:
  0.0 0.9 constant_dynamic-slice_fusion
  1.1 8.8 %collective-permute-start = (bf16[192,256]{1,0:T(8,128)(2,1)S(1)}, bf16[192,256]{1,0:T(8,128)(2,1)S(1)}, u32[]{:S(2)}, u32[]{:S(2)}) collective-permute-start(bf16[192,256]{1,0:T(8,128)(2,1)S(1)} %pad_maximum_fusion.1), channel_id=1, source_target_pairs={{0,1},{1,0},{2,3},{3,2},{4,5},{5,4},{6,7},{7,6},{8,9},{9,8},{10,11... | collective-permute-start | bytes 294920 | tf_op jit(solution)/shard_map/ppermute | solution.py:31
  9.8 1.9 %collective-permute-start.4 = (bf16[192,512]{1,0:T(8,128)(2,1)}, bf16[192,512]{1,0:T(8,128)(2,1)S(1)}, u32[]{:S(2)}, u32[]{:S(2)}) collective-permute-start(bf16[192,512]{1,0:T(8,128)(2,1)} %bitcast.12), channel_id=1, source_target_pairs={{0,16},{16,0},{1,17},{17,1},{2,18},{18,2},{3,19},{19,3},{4,20},{20... | collective-permute-start | bytes 589832 | tf_op jit(solution)/shard_map/ppermute | solution.py:31
  11.8 1.9 %collective-permute-start.1 = (bf16[2,192,256]{2,1,0:T(8,128)(2,1)S(1)}, bf16[2,192,256]{2,1,0:T(8,128)(2,1)S(1)}, u32[]{:S(2)}, u32[]{:S(2)}) collective-permute-start(bf16[2,192,256]{2,1,0:T(8,128)(2,1)S(1)} %pad_maximum_fusion.refs_0_), channel_id=1, source_target_pairs={{0,32},{32,0},{1,33},{33,1},{2,34},{34,2},{3,35},{35,3},{4,36},{36... | collective-permute-start | bytes 589832 | tf_op jit(solution)/shard_map/ppermute | solution.py:31
  13.8 1.3 collective-permute-start.2
  15.1 1.3 collective-permute-start.3
  16.4 3.6 %collective-permute-done.4.refs_1_ = bf16[192,512]{1,0:T(8,128)(2,1)S(1)} collective-permute-done((bf16[192,512]{1,0:T(8,128)(2,1)}, bf16[192,512]{1,0:T(8,128)(2,1)S(1)}, u32[]{:S(2)}, u32[]{:S(2)}) %collective-permute-start.4) | collective-permute-done | bytes 196640 | tf_op jit(solution)/shard_map/ppermute | solution.py:31
  20.0 0.9 copy-done.2
  20.9 1.9 %collective-permute-start.5 = (bf16[384,512]{1,0:T(8,128)(2,1)S(1)}, bf16[384,512]{1,0:T(8,128)(2,1)S(1)}, u32[]{:S(2)}, u32[]{:S(2)}) collective-permute-start(bf16[384,512]{1,0:T(8,128)(2,1)S(1)} %shard_map.83.refs_0_), channel_id=1, source_target_pairs={{0,2},{2,4},{4,6},{6,8},{8,10},{10,12},{12,14},{14,0},{1,3},{3,5},... | collective-permute-start | bytes 1179656 | tf_op jit(solution)/shard_map/ppermute | solution.py:31
  22.9 0.8 collective-permute-done.2.q1
  23.7 0.2 collective-permute-done.3.q3
  23.9 3.0 %collective-permute-start.14 = (bf16[4,192,256]{2,1,0:T(8,128)(2,1)S(1)}, bf16[4,192,256]{2,1,0:T(8,128)(2,1)S(1)}, u32[]{:S(2)}, u32[]{:S(2)}) collective-permute-start(bf16[4,192,256]{2,1,0:T(8,128)(2,1)S(1)} %shard_map.82.refs_0_), channel_id=1, source_target_pairs={{0,448},{64,0},{128,64},{192,128},{256,192},{320,256},{384,320},{4... | collective-permute-start | bytes 1179656 | tf_op jit(solution)/shard_map/ppermute | solution.py:31
  26.9 10.8 %collective-permute-start.9 = (bf16[384,512]{1,0:T(8,128)(2,1)S(1)}, bf16[384,512]{1,0:T(8,128)(2,1)S(1)}, u32[]{:S(2)}, u32[]{:S(2)}) collective-permute-start(bf16[384,512]{1,0:T(8,128)(2,1)S(1)} %shard_map.83.refs_0_), channel_id=1, source_target_pairs={{0,14},{2,0},{4,2},{6,4},{8,6},{10,8},{12,10},{14,12},{1,15},{3,1}... | collective-permute-start | bytes 1179656 | tf_op jit(solution)/shard_map/ppermute | solution.py:31
  37.7 1.9 %collective-permute-start.6 = (bf16[384,512]{1,0:T(8,128)(2,1)S(1)}, bf16[384,512]{1,0:T(8,128)(2,1)S(1)}, u32[]{:S(2)}, u32[]{:S(2)}) collective-permute-start(bf16[384,512]{1,0:T(8,128)(2,1)S(1)} %collective-permute-done.5.refs_6_.refs_7_), channel_id=1, source_target_pairs={{0,2},{2,4},{4,6},{6,8},{8,10},{10,12},{12,14},{14,0},{1,3},{3,5},... | collective-permute-start | bytes 1179656 | tf_op jit(solution)/shard_map/ppermute | solution.py:31
  39.6 3.9 %collective-permute-start.18 = (bf16[4,192,256]{2,1,0:T(8,128)(2,1)S(1)}, bf16[4,192,256]{2,1,0:T(8,128)(2,1)S(1)}, u32[]{:S(2)}, u32[]{:S(2)}) collective-permute-start(bf16[4,192,256]{2,1,0:T(8,128)(2,1)S(1)} %shard_map.82.refs_0_), channel_id=1, source_target_pairs={{0,64},{64,128},{128,192},{192,256},{256,320},{320,384},{384,448},... | collective-permute-start | bytes 1179656 | tf_op jit(solution)/shard_map/ppermute | solution.py:31
  43.5 2.6 %collective-permute-start.15 = (bf16[4,192,256]{2,1,0:T(8,128)(2,1)S(1)}, bf16[4,192,256]{2,1,0:T(8,128)(2,1)S(1)}, u32[]{:S(2)}, u32[]{:S(2)}) collective-permute-start(bf16[4,192,256]{2,1,0:T(8,128)(2,1)S(1)} %collective-permute-done.14.refs_1_), channel_id=1, source_target_pairs={{0,448},{64,0},{128,64},{192,128},{256,192},{320,256},{384,320},{4... | collective-permute-start | bytes 1179656 | tf_op jit(solution)/shard_map/ppermute | solution.py:31
  46.1 4.6 %collective-permute-start.10 = (bf16[384,512]{1,0:T(8,128)(2,1)S(1)}, bf16[384,512]{1,0:T(8,128)(2,1)S(1)}, u32[]{:S(2)}, u32[]{:S(2)}) collective-permute-start(bf16[384,512]{1,0:T(8,128)(2,1)S(1)} %collective-permute-done.9.refs_1_), channel_id=1, source_target_pairs={{0,14},{2,0},{4,2},{6,4},{8,6},{10,8},{12,10},{14,12},{1,15},{3,1}... | collective-permute-start | bytes 1179656 | tf_op jit(solution)/shard_map/ppermute | solution.py:31
  50.7 1.9 %collective-permute-start.7 = (bf16[384,512]{1,0:T(8,128)(2,1)S(1)}, bf16[384,512]{1,0:T(8,128)(2,1)S(1)}, u32[]{:S(2)}, u32[]{:S(2)}) collective-permute-start(bf16[384,512]{1,0:T(8,128)(2,1)S(1)} %collective-permute-done.6.refs_5_.refs_6_), channel_id=1, source_target_pairs={{0,2},{2,4},{4,6},{6,8},{8,10},{10,12},{12,14},{14,0},{1,3},{3,5},... | collective-permute-start | bytes 1179656 | tf_op jit(solution)/shard_map/ppermute | solution.py:31
  52.7 3.2 %collective-permute-start.19 = (bf16[4,192,256]{2,1,0:T(8,128)(2,1)S(1)}, bf16[4,192,256]{2,1,0:T(8,128)(2,1)S(1)}, u32[]{:S(2)}, u32[]{:S(2)}) collective-permute-start(bf16[4,192,256]{2,1,0:T(8,128)(2,1)S(1)} %collective-permute-done.18.refs_7_), channel_id=1, source_target_pairs={{0,64},{64,128},{128,192},{192,256},{256,320},{320,384},{384,448},... | collective-permute-start | bytes 1179656 | tf_op jit(solution)/shard_map/ppermute | solution.py:31
  55.9 3.2 %collective-permute-start.16 = (bf16[4,192,256]{2,1,0:T(8,128)(2,1)S(1)}, bf16[4,192,256]{2,1,0:T(8,128)(2,1)S(1)}, u32[]{:S(2)}, u32[]{:S(2)}) collective-permute-start(bf16[4,192,256]{2,1,0:T(8,128)(2,1)S(1)} %collective-permute-done.15.refs_2_), channel_id=1, source_target_pairs={{0,448},{64,0},{128,64},{192,128},{256,192},{320,256},{384,320},{4... | collective-permute-start | bytes 1179656 | tf_op jit(solution)/shard_map/ppermute | solution.py:31
  59.2 4.6 %collective-permute-start.11 = (bf16[384,512]{1,0:T(8,128)(2,1)S(1)}, bf16[384,512]{1,0:T(8,128)(2,1)S(1)}, u32[]{:S(2)}, u32[]{:S(2)}) collective-permute-start(bf16[384,512]{1,0:T(8,128)(2,1)S(1)} %collective-permute-done.10.refs_2_), channel_id=1, source_target_pairs={{0,14},{2,0},{4,2},{6,4},{8,6},{10,8},{12,10},{14,12},{1,15},{3,1}... | collective-permute-start | bytes 1179656 | tf_op jit(solution)/shard_map/ppermute | solution.py:31
  63.8 1.9 %collective-permute-start.8 = (bf16[384,512]{1,0:T(8,128)(2,1)S(1)}, bf16[384,512]{1,0:T(8,128)(2,1)S(1)}, u32[]{:S(2)}, u32[]{:S(2)}) collective-permute-start(bf16[384,512]{1,0:T(8,128)(2,1)S(1)} %collective-permute-done.7.refs_4_.refs_5_), channel_id=1, source_target_pairs={{0,2},{2,4},{4,6},{6,8},{8,10},{10,12},{12,14},{14,0},{1,3},{3,5},... | collective-permute-start | bytes 1179656 | tf_op jit(solution)/shard_map/ppermute | solution.py:31
  65.7 2.0 %collective-permute-start.20 = (bf16[4,192,256]{2,1,0:T(8,128)(2,1)S(1)}, bf16[4,192,256]{2,1,0:T(8,128)(2,1)S(1)}, u32[]{:S(2)}, u32[]{:S(2)}) collective-permute-start(bf16[4,192,256]{2,1,0:T(8,128)(2,1)S(1)} %collective-permute-done.19.refs_6_), channel_id=1, source_target_pairs={{0,64},{64,128},{128,192},{192,256},{256,320},{320,384},{384,448},... | collective-permute-start | bytes 1179656 | tf_op jit(solution)/shard_map/ppermute | solution.py:31
  67.8 4.5 %collective-permute-start.17 = (bf16[4,192,256]{2,1,0:T(8,128)(2,1)S(1)}, bf16[4,192,256]{2,1,0:T(8,128)(2,1)S(1)}, u32[]{:S(2)}, u32[]{:S(2)}) collective-permute-start(bf16[4,192,256]{2,1,0:T(8,128)(2,1)S(1)} %collective-permute-done.16.refs_3_), channel_id=1, source_target_pairs={{0,448},{64,0},{128,64},{192,128},{256,192},{320,256},{384,320},{4... | collective-permute-start | bytes 1179656 | tf_op jit(solution)/shard_map/ppermute | solution.py:31
  72.2 1.3 collective-permute-start.13
  73.5 0.5 shard_map.84.refs_1_
  74.2 6.7 %collective-permute-start.12 = (f32[8,512]{1,0:T(8,128)S(1)}, f32[8,512]{1,0:T(8,128)S(1)}, u32[]{:S(2)}, u32[]{:S(2)}) collective-permute-start(f32[8,512]{1,0:T(8,128)S(1)} %shard_map.85.own_ref), channel_id=1, source_target_pairs={{0,1},{1,0},{2,3},{3,2},{4,5},{5,4},{6,7},{7,6},{8,9},{9,8},{10,11... | collective-permute-start | bytes 49160 | tf_op jit(solution)/shard_map/ppermute | solution.py:31
  80.9 0.7 shard_map.86.table_ref
  81.7 2.6 %shard_map.87.normed_ref = bf16[8,2,512,192]{3,2,1,0:T(8,128)(2,1)S(1)} custom-call(s32[8]{0:T(128)S(1)} %stack.44.ids_ref, f32[8,512]{1,0:T(8,128)S(1)} %shard_map.85.own_ref, f32[8,512]{1,0:T(8,128)S(1)} %collective-permute-done.12.other_ref, f32[64,192]{1,0:T(8,128)S(1)} %shard_map.86.table_ref, bf16[384,512]{1,0:T(8,128)(2,1)S(1)} %shard_map.83.refs_0_, ...), custom_call_target="tpu_custom_call" | custom-call | tf_op jit(solution)/shard_map/pallas_call | solution.py:324
  84.3 1.8 %shard_map.89 = f32[512,256]{1,0:T(8,128)S(1)} custom-call(s32[8]{0:T(128)S(1)} %stack.44.ids_ref, bf16[8,2,512,192]{3,2,1,0:T(8,128)(2,1)S(1)} %shard_map.87.normed_ref, bf16[4,192,256]{2,1,0:T(8,128)(2,1)S(1)} %shard_map.82.refs_0_, bf16[4,192,256]{2,1,0:T(8,128)(2,1)S(1)} %collective-permute-done.14.refs_1_, ...), custom_call_target="tpu_custom_call" | custom-call | tf_op jit(solution)/shard_map/pallas_call | solution.py:152
  86.1 4.8 %collective-permute-start.21 = (f32[512,256]{1,0:T(8,128)S(1)}, f32[512,256]{1,0:T(8,128)S(1)}, u32[]{:S(2)}, u32[]{:S(2)}) collective-permute-start(f32[512,256]{1,0:T(8,128)S(1)} %shard_map.89), channel_id=1, source_target_pairs={{0,1},{1,0},{2,3},{3,2},{4,5},{5,4},{6,7},{7,6},{8,9},{9,8},{10,11... | collective-permute-start | bytes 1572872 | tf_op jit(solution)/shard_map/ppermute | solution.py:31
  91.0 1.8 %shard_map.88.mine_ref = f32[512,256]{1,0:T(8,128)S(1)} custom-call(s32[8]{0:T(128)S(1)} %stack.44.ids_ref, bf16[8,2,512,192]{3,2,1,0:T(8,128)(2,1)S(1)} %shard_map.87.normed_ref, bf16[4,192,256]{2,1,0:T(8,128)(2,1)S(1)} %shard_map.82.refs_0_, bf16[4,192,256]{2,1,0:T(8,128)(2,1)S(1)} %collective-permute-done.14.refs_1_, ...), custom_call_target="tpu_custom_call" | custom-call | tf_op jit(solution)/shard_map/pallas_call | solution.py:152
  92.9 6.5 %collective-permute-start.22 = (bf16[1024,128]{1,0:T(8,128)(2,1)S(1)}, bf16[1024,128]{1,0:T(8,128)(2,1)S(1)}, u32[]{:S(2)}, u32[]{:S(2)}) collective-permute-start(bf16[1024,128]{1,0:T(8,128)(2,1)S(1)} %shard_map.90.kv_ref), channel_id=1, source_target_pairs={{0,64},{64,0},{1,65},{65,1},{2,66},{66,2},{3,67},{67,3},{4,68},{68... | collective-permute-start | bytes 786440 | tf_op jit(solution)/shard_map/ppermute | solution.py:31
  99.3 3.1 %collective-permute-start.23 = (bf16[1024,128]{1,0:T(8,128)(2,1)S(1)}, bf16[1024,128]{1,0:T(8,128)(2,1)S(1)}, u32[]{:S(2)}, u32[]{:S(2)}) collective-permute-start(bf16[1024,128]{1,0:T(8,128)(2,1)S(1)} %shard_map.90.kv_ref), channel_id=1, source_target_pairs={{0,32},{32,0},{1,33},{33,1},{2,34},{34,2},{3,35},{35,3},{4,36},{36... | collective-permute-start | bytes 786440 | tf_op jit(solution)/shard_map/ppermute | solution.py:31
  102.4 1.9 %collective-permute-start.24 = (bf16[1024,128]{1,0:T(8,128)(2,1)S(1)}, bf16[1024,128]{1,0:T(8,128)(2,1)S(1)}, u32[]{:S(2)}, u32[]{:S(2)}) collective-permute-start(bf16[1024,128]{1,0:T(8,128)(2,1)S(1)} %shard_map.90.kv_ref), channel_id=1, source_target_pairs={{0,96},{32,64},{64,32},{96,0},{1,97},{33,65},{65,33},{97,1},{2,98}... | collective-permute-start | bytes 786440 | tf_op jit(solution)/shard_map/ppermute | solution.py:344
  104.4 3.0 %shard_map.91 = (bf16[4,128,512]{2,1,0:T(8,128)(2,1)S(1)}, f32[4,16,512]{2,1,0:T(8,128)S(1)}, f32[4,128,512]{2,1,0:T(8,128)S(1)}) custom-call(s32[8]{0:T(128)S(1)} %stack.44.ids_ref, s32[16,16]{1,0:T(8,128)S(1)} %copy-done, s32[16]{0:T(128)S(1)} %copy-done.4, bf16[512,128]{1,0:T(8,128)(2,1)S(1)} %copy-done.3, ...), custom_call_target="tpu_custom_call" | custom-call | tf_op jit(solution)/shard_map/pallas_call | solution.py:349
  107.5 2.1 %shard_map.92 = (f32[4,16,512]{2,1,0:T(8,128)S(1)}, f32[4,128,512]{2,1,0:T(8,128)S(1)}) custom-call(s32[8]{0:T(128)S(1)} %stack.44.ids_ref, s32[16,16]{1,0:T(8,128)S(1)} %copy-done, s32[16]{0:T(128)S(1)} %copy-done.4, bf16[4,128,512]{2,1,0:T(8,128)(2,1)S(1)} %get-tuple-element.24.q_t, ...), custom_call_target="tpu_custom_call", output_to_operand_aliasing={{0}: (4, {}), {1}: (5, {})} | custom-call | tf_op jit(solution)/shard_map/pallas_call | solution.py:356
  109.5 4.9 %collective-permute-done.23.kv1 = bf16[1024,128]{1,0:T(8,128)(2,1)S(1)} collective-permute-done((bf16[1024,128]{1,0:T(8,128)(2,1)S(1)}, bf16[1024,128]{1,0:T(8,128)(2,1)S(1)}, u32[]{:S(2)}, u32[]{:S(2)}) %collective-permute-start.23) | collective-permute-done | bytes 262176 | tf_op jit(solution)/shard_map/ppermute | solution.py:31
  114.4 1.6 %shard_map.94 = bf16[528,128]{1,0:T(8,128)(2,1)S(1)} custom-call(s32[8]{0:T(128)S(1)} %stack.44.ids_ref, s32[16,16]{1,0:T(8,128)S(1)} %copy-done, s32[16]{0:T(128)S(1)} %copy-done.4, bf16[4,128,512]{2,1,0:T(8,128)(2,1)S(1)} %get-tuple-element.24.q_t, f32[4,16,512]{2,1,0:T(8,128)S(1)} %get-tuple-element.27.stat_in, ...), custom_call_target="tpu_custom_call" | custom-call | tf_op jit(solution)/shard_map/pallas_call | solution.py:366
  116.0 1.4 %collective-permute-start.25 = (bf16[528,128]{1,0:T(8,128)(2,1)S(1)}, bf16[528,128]{1,0:T(8,128)(2,1)S(1)}, u32[]{:S(2)}, u32[]{:S(2)}) collective-permute-start(bf16[528,128]{1,0:T(8,128)(2,1)S(1)} %shard_map.94), channel_id=1, source_target_pairs={{0,128},{64,192},{128,256},{192,320},{256,384},{320,448},{1,129},{... | collective-permute-start | bytes 405512 | tf_op jit(solution)/shard_map/ppermute | solution.py:44
  117.5 1.4 %shard_map.95 = bf16[528,128]{1,0:T(8,128)(2,1)S(1)} custom-call(s32[8]{0:T(128)S(1)} %stack.44.ids_ref, s32[16,16]{1,0:T(8,128)S(1)} %copy-done, s32[16]{0:T(128)S(1)} %copy-done.4, bf16[4,128,512]{2,1,0:T(8,128)(2,1)S(1)} %get-tuple-element.24.q_t, f32[4,16,512]{2,1,0:T(8,128)S(1)} %get-tuple-element.27.stat_in, ...), custom_call_target="tpu_custom_call" | custom-call | tf_op jit(solution)/shard_map/pallas_call | solution.py:366
  118.9 1.3 collective-permute-start.26
  120.2 1.4 %shard_map.96 = bf16[528,128]{1,0:T(8,128)(2,1)S(1)} custom-call(s32[8]{0:T(128)S(1)} %stack.44.ids_ref, s32[16,16]{1,0:T(8,128)S(1)} %copy-done, s32[16]{0:T(128)S(1)} %copy-done.4, bf16[4,128,512]{2,1,0:T(8,128)(2,1)S(1)} %get-tuple-element.24.q_t, f32[4,16,512]{2,1,0:T(8,128)S(1)} %get-tuple-element.27.stat_in, ...), custom_call_target="tpu_custom_call" | custom-call | tf_op jit(solution)/shard_map/pallas_call | solution.py:366
  121.7 1.3 collective-permute-start.27
  123.0 0.8 shard_map.93.part0
  123.8 5.3 %collective-permute-done.26.part2 = bf16[528,128]{1,0:T(8,128)(2,1)S(1)} collective-permute-done((bf16[528,128]{1,0:T(8,128)(2,1)S(1)}, bf16[528,128]{1,0:T(8,128)(2,1)S(1)}, u32[]{:S(2)}, u32[]{:S(2)}) %collective-permute-start.26) | collective-permute-done | bytes 135200 | tf_op jit(solution)/shard_map/ppermute | solution.py:44
  129.0 2.9 %collective-permute-done.27.part3 = bf16[528,128]{1,0:T(8,128)(2,1)S(1)} collective-permute-done((bf16[528,128]{1,0:T(8,128)(2,1)S(1)}, bf16[528,128]{1,0:T(8,128)(2,1)S(1)}, u32[]{:S(2)}, u32[]{:S(2)}) %collective-permute-start.27) | collective-permute-done | bytes 135200 | tf_op jit(solution)/shard_map/ppermute | solution.py:44
  131.9 1.4 %shard_map.97 = bf16[512,128]{1,0:T(8,128)(2,1)} custom-call(s32[8]{0:T(128)S(1)} %stack.44.ids_ref, s32[16]{0:T(128)S(1)} %copy-done.4, bf16[528,128]{1,0:T(8,128)(2,1)S(1)} %shard_map.93.part0, bf16[528,128]{1,0:T(8,128)(2,1)S(1)} %collective-permute-done.25.part1, bf16[528,128]{1,0:T(8,128)(2,1)S(1)} %collective-permute-done.26.part2, ...), custom_call_target="tpu_custom_call" | custom-call | tf_op jit(solution)/shard_map/pallas_call | solution.py:375
  (41 shorter events, 0.5 us)
Async XLA Ops:
  0.0 80.9 %copy-start.5 = (s32[16]{0:T(128)S(1)}, s32[16]{0:T(128)}, u32[]{:S(2)}) copy-start(s32[16]{0:T(128)} %levels_ref.1) | copy-start | bytes 196
  0.0 80.9 %copy-start.1 = (bf16[8,12288]{1,0:T(8,128)(2,1)S(1)}, bf16[8,12288]{1,0:T(8,128)(2,1)}, u32[]{:S(2)}) copy-start(bf16[8,12288]{1,0:T(8,128)(2,1)} %modulation_ref.1) | copy-start | bytes 589828
  1.1 10.7 %collective-permute-start = (bf16[192,256]{1,0:T(8,128)(2,1)S(1)}, bf16[192,256]{1,0:T(8,128)(2,1)S(1)}, u32[]{:S(2)}, u32[]{:S(2)}) collective-permute-start(bf16[192,256]{1,0:T(8,128)(2,1)S(1)} %pad_maximum_fusion.1), channel_id=1, source_target_pairs={{0,1},{1,0},{2,3},{3,2},{4,5},{5,4},{6,7},{7,6},{8,9},{9,8},{10,11... | collective-permute-start | bytes 294920 | tf_op jit(solution)/shard_map/ppermute | solution.py:31
  9.8 10.1 %collective-permute-start.4 = (bf16[192,512]{1,0:T(8,128)(2,1)}, bf16[192,512]{1,0:T(8,128)(2,1)S(1)}, u32[]{:S(2)}, u32[]{:S(2)}) collective-permute-start(bf16[192,512]{1,0:T(8,128)(2,1)} %bitcast.12), channel_id=1, source_target_pairs={{0,16},{16,0},{1,17},{17,1},{2,18},{18,2},{3,19},{19,3},{4,20},{20... | collective-permute-start | bytes 589832 | tf_op jit(solution)/shard_map/ppermute | solution.py:31
  11.8 11.0 %collective-permute-start.1 = (bf16[2,192,256]{2,1,0:T(8,128)(2,1)S(1)}, bf16[2,192,256]{2,1,0:T(8,128)(2,1)S(1)}, u32[]{:S(2)}, u32[]{:S(2)}) collective-permute-start(bf16[2,192,256]{2,1,0:T(8,128)(2,1)S(1)} %pad_maximum_fusion.refs_0_), channel_id=1, source_target_pairs={{0,32},{32,0},{1,33},{33,1},{2,34},{34,2},{3,35},{35,3},{4,36},{36... | collective-permute-start | bytes 589832 | tf_op jit(solution)/shard_map/ppermute | solution.py:31
  13.8 10.0 %collective-permute-start.2 = (bf16[512,128]{1,0:T(8,128)(2,1)}, bf16[512,128]{1,0:T(8,128)(2,1)S(1)}, u32[]{:S(2)}, u32[]{:S(2)}) collective-permute-start(bf16[512,128]{1,0:T(8,128)(2,1)} %q0.1), channel_id=1, source_target_pairs={{128,0},{192,64},{256,128},{320,192},{384,256},{448,320},{129,1},{... | collective-permute-start | bytes 393224 | tf_op jit(solution)/shard_map/ppermute | solution.py:44
  15.1 8.8 %collective-permute-start.3 = (bf16[512,128]{1,0:T(8,128)(2,1)}, bf16[512,128]{1,0:T(8,128)(2,1)S(1)}, u32[]{:S(2)}, u32[]{:S(2)}) collective-permute-start(bf16[512,128]{1,0:T(8,128)(2,1)} %q0.1), channel_id=1, source_target_pairs={{384,0},{448,64},{385,1},{449,65},{386,2},{450,66},{387,3},{451,67... | collective-permute-start | bytes 393224 | tf_op jit(solution)/shard_map/ppermute | solution.py:44
  20.0 0.9 copy-start.2
  20.9 16.7 %collective-permute-start.5 = (bf16[384,512]{1,0:T(8,128)(2,1)S(1)}, bf16[384,512]{1,0:T(8,128)(2,1)S(1)}, u32[]{:S(2)}, u32[]{:S(2)}) collective-permute-start(bf16[384,512]{1,0:T(8,128)(2,1)S(1)} %shard_map.83.refs_0_), channel_id=1, source_target_pairs={{0,2},{2,4},{4,6},{6,8},{8,10},{10,12},{12,14},{14,0},{1,3},{3,5},... | collective-permute-start | bytes 1179656 | tf_op jit(solution)/shard_map/ppermute | solution.py:31
  23.9 19.6 %collective-permute-start.14 = (bf16[4,192,256]{2,1,0:T(8,128)(2,1)S(1)}, bf16[4,192,256]{2,1,0:T(8,128)(2,1)S(1)}, u32[]{:S(2)}, u32[]{:S(2)}) collective-permute-start(bf16[4,192,256]{2,1,0:T(8,128)(2,1)S(1)} %shard_map.82.refs_0_), channel_id=1, source_target_pairs={{0,448},{64,0},{128,64},{192,128},{256,192},{320,256},{384,320},{4... | collective-permute-start | bytes 1179656 | tf_op jit(solution)/shard_map/ppermute | solution.py:31
  26.9 19.2 %collective-permute-start.9 = (bf16[384,512]{1,0:T(8,128)(2,1)S(1)}, bf16[384,512]{1,0:T(8,128)(2,1)S(1)}, u32[]{:S(2)}, u32[]{:S(2)}) collective-permute-start(bf16[384,512]{1,0:T(8,128)(2,1)S(1)} %shard_map.83.refs_0_), channel_id=1, source_target_pairs={{0,14},{2,0},{4,2},{6,4},{8,6},{10,8},{12,10},{14,12},{1,15},{3,1}... | collective-permute-start | bytes 1179656 | tf_op jit(solution)/shard_map/ppermute | solution.py:31
  37.7 13.0 %collective-permute-start.6 = (bf16[384,512]{1,0:T(8,128)(2,1)S(1)}, bf16[384,512]{1,0:T(8,128)(2,1)S(1)}, u32[]{:S(2)}, u32[]{:S(2)}) collective-permute-start(bf16[384,512]{1,0:T(8,128)(2,1)S(1)} %collective-permute-done.5.refs_6_.refs_7_), channel_id=1, source_target_pairs={{0,2},{2,4},{4,6},{6,8},{8,10},{10,12},{12,14},{14,0},{1,3},{3,5},... | collective-permute-start | bytes 1179656 | tf_op jit(solution)/shard_map/ppermute | solution.py:31
  39.6 13.1 %collective-permute-start.18 = (bf16[4,192,256]{2,1,0:T(8,128)(2,1)S(1)}, bf16[4,192,256]{2,1,0:T(8,128)(2,1)S(1)}, u32[]{:S(2)}, u32[]{:S(2)}) collective-permute-start(bf16[4,192,256]{2,1,0:T(8,128)(2,1)S(1)} %shard_map.82.refs_0_), channel_id=1, source_target_pairs={{0,64},{64,128},{128,192},{192,256},{256,320},{320,384},{384,448},... | collective-permute-start | bytes 1179656 | tf_op jit(solution)/shard_map/ppermute | solution.py:31
  43.5 12.4 %collective-permute-start.15 = (bf16[4,192,256]{2,1,0:T(8,128)(2,1)S(1)}, bf16[4,192,256]{2,1,0:T(8,128)(2,1)S(1)}, u32[]{:S(2)}, u32[]{:S(2)}) collective-permute-start(bf16[4,192,256]{2,1,0:T(8,128)(2,1)S(1)} %collective-permute-done.14.refs_1_), channel_id=1, source_target_pairs={{0,448},{64,0},{128,64},{192,128},{256,192},{320,256},{384,320},{4... | collective-permute-start | bytes 1179656 | tf_op jit(solution)/shard_map/ppermute | solution.py:31
  46.1 13.1 %collective-permute-start.10 = (bf16[384,512]{1,0:T(8,128)(2,1)S(1)}, bf16[384,512]{1,0:T(8,128)(2,1)S(1)}, u32[]{:S(2)}, u32[]{:S(2)}) collective-permute-start(bf16[384,512]{1,0:T(8,128)(2,1)S(1)} %collective-permute-done.9.refs_1_), channel_id=1, source_target_pairs={{0,14},{2,0},{4,2},{6,4},{8,6},{10,8},{12,10},{14,12},{1,15},{3,1}... | collective-permute-start | bytes 1179656 | tf_op jit(solution)/shard_map/ppermute | solution.py:31
  50.7 13.1 %collective-permute-start.7 = (bf16[384,512]{1,0:T(8,128)(2,1)S(1)}, bf16[384,512]{1,0:T(8,128)(2,1)S(1)}, u32[]{:S(2)}, u32[]{:S(2)}) collective-permute-start(bf16[384,512]{1,0:T(8,128)(2,1)S(1)} %collective-permute-done.6.refs_5_.refs_6_), channel_id=1, source_target_pairs={{0,2},{2,4},{4,6},{6,8},{8,10},{10,12},{12,14},{14,0},{1,3},{3,5},... | collective-permute-start | bytes 1179656 | tf_op jit(solution)/shard_map/ppermute | solution.py:31
  52.7 13.1 %collective-permute-start.19 = (bf16[4,192,256]{2,1,0:T(8,128)(2,1)S(1)}, bf16[4,192,256]{2,1,0:T(8,128)(2,1)S(1)}, u32[]{:S(2)}, u32[]{:S(2)}) collective-permute-start(bf16[4,192,256]{2,1,0:T(8,128)(2,1)S(1)} %collective-permute-done.18.refs_7_), channel_id=1, source_target_pairs={{0,64},{64,128},{128,192},{192,256},{256,320},{320,384},{384,448},... | collective-permute-start | bytes 1179656 | tf_op jit(solution)/shard_map/ppermute | solution.py:31
  55.9 11.8 %collective-permute-start.16 = (bf16[4,192,256]{2,1,0:T(8,128)(2,1)S(1)}, bf16[4,192,256]{2,1,0:T(8,128)(2,1)S(1)}, u32[]{:S(2)}, u32[]{:S(2)}) collective-permute-start(bf16[4,192,256]{2,1,0:T(8,128)(2,1)S(1)} %collective-permute-done.15.refs_2_), channel_id=1, source_target_pairs={{0,448},{64,0},{128,64},{192,128},{256,192},{320,256},{384,320},{4... | collective-permute-start | bytes 1179656 | tf_op jit(solution)/shard_map/ppermute | solution.py:31
  59.2 14.4 %collective-permute-start.11 = (bf16[384,512]{1,0:T(8,128)(2,1)S(1)}, bf16[384,512]{1,0:T(8,128)(2,1)S(1)}, u32[]{:S(2)}, u32[]{:S(2)}) collective-permute-start(bf16[384,512]{1,0:T(8,128)(2,1)S(1)} %collective-permute-done.10.refs_2_), channel_id=1, source_target_pairs={{0,14},{2,0},{4,2},{6,4},{8,6},{10,8},{12,10},{14,12},{1,15},{3,1}... | collective-permute-start | bytes 1179656 | tf_op jit(solution)/shard_map/ppermute | solution.py:31
  63.8 10.3 %collective-permute-start.8 = (bf16[384,512]{1,0:T(8,128)(2,1)S(1)}, bf16[384,512]{1,0:T(8,128)(2,1)S(1)}, u32[]{:S(2)}, u32[]{:S(2)}) collective-permute-start(bf16[384,512]{1,0:T(8,128)(2,1)S(1)} %collective-permute-done.7.refs_4_.refs_5_), channel_id=1, source_target_pairs={{0,2},{2,4},{4,6},{6,8},{8,10},{10,12},{12,14},{14,0},{1,3},{3,5},... | collective-permute-start | bytes 1179656 | tf_op jit(solution)/shard_map/ppermute | solution.py:31
  65.7 18.6 %collective-permute-start.20 = (bf16[4,192,256]{2,1,0:T(8,128)(2,1)S(1)}, bf16[4,192,256]{2,1,0:T(8,128)(2,1)S(1)}, u32[]{:S(2)}, u32[]{:S(2)}) collective-permute-start(bf16[4,192,256]{2,1,0:T(8,128)(2,1)S(1)} %collective-permute-done.19.refs_6_), channel_id=1, source_target_pairs={{0,64},{64,128},{128,192},{192,256},{256,320},{320,384},{384,448},... | collective-permute-start | bytes 1179656 | tf_op jit(solution)/shard_map/ppermute | solution.py:31
  67.8 16.5 %collective-permute-start.17 = (bf16[4,192,256]{2,1,0:T(8,128)(2,1)S(1)}, bf16[4,192,256]{2,1,0:T(8,128)(2,1)S(1)}, u32[]{:S(2)}, u32[]{:S(2)}) collective-permute-start(bf16[4,192,256]{2,1,0:T(8,128)(2,1)S(1)} %collective-permute-done.16.refs_3_), channel_id=1, source_target_pairs={{0,448},{64,0},{128,64},{192,128},{256,192},{320,256},{384,320},{4... | collective-permute-start | bytes 1179656 | tf_op jit(solution)/shard_map/ppermute | solution.py:31
  72.2 12.0 %collective-permute-start.13 = (bf16[512,128]{1,0:T(8,128)(2,1)}, bf16[512,128]{1,0:T(8,128)(2,1)S(1)}, u32[]{:S(2)}, u32[]{:S(2)}) collective-permute-start(bf16[512,128]{1,0:T(8,128)(2,1)} %q0.1), channel_id=1, source_target_pairs={{256,64},{320,0},{384,192},{448,128},{257,65},{321,1},{385,193},{4... | collective-permute-start | bytes 393224 | tf_op jit(solution)/shard_map/ppermute | solution.py:44
  74.2 7.5 %collective-permute-start.12 = (f32[8,512]{1,0:T(8,128)S(1)}, f32[8,512]{1,0:T(8,128)S(1)}, u32[]{:S(2)}, u32[]{:S(2)}) collective-permute-start(f32[8,512]{1,0:T(8,128)S(1)} %shard_map.85.own_ref), channel_id=1, source_target_pairs={{0,1},{1,0},{2,3},{3,2},{4,5},{5,4},{6,7},{7,6},{8,9},{9,8},{10,11... | collective-permute-start | bytes 49160 | tf_op jit(solution)/shard_map/ppermute | solution.py:31
  86.1 18.3 %copy-start = (s32[16,16]{1,0:T(8,128)S(1)}, s32[16,16]{1,0:T(8,128)}, u32[]{:S(2)}) copy-start(s32[16,16]{1,0:T(8,128)} %visible_ref.11) | copy-start | bytes 3076
  86.1 18.3 %copy-start.3 = (bf16[512,128]{1,0:T(8,128)(2,1)S(1)}, bf16[512,128]{1,0:T(8,128)(2,1)}, u32[]{:S(2)}) copy-start(bf16[512,128]{1,0:T(8,128)(2,1)} %q0.1) | copy-start | bytes 393220
  86.1 18.3 %copy-start.4 = (s32[16]{0:T(128)S(1)}, s32[16]{0:T(128)}, u32[]{:S(2)}) copy-start(s32[16]{0:T(128)} %counts_ref.13) | copy-start | bytes 196
  86.1 6.6 %collective-permute-start.21 = (f32[512,256]{1,0:T(8,128)S(1)}, f32[512,256]{1,0:T(8,128)S(1)}, u32[]{:S(2)}, u32[]{:S(2)}) collective-permute-start(f32[512,256]{1,0:T(8,128)S(1)} %shard_map.89), channel_id=1, source_target_pairs={{0,1},{1,0},{2,3},{3,2},{4,5},{5,4},{6,7},{7,6},{8,9},{9,8},{10,11... | collective-permute-start | bytes 1572872 | tf_op jit(solution)/shard_map/ppermute | solution.py:31
  92.9 14.6 %collective-permute-start.22 = (bf16[1024,128]{1,0:T(8,128)(2,1)S(1)}, bf16[1024,128]{1,0:T(8,128)(2,1)S(1)}, u32[]{:S(2)}, u32[]{:S(2)}) collective-permute-start(bf16[1024,128]{1,0:T(8,128)(2,1)S(1)} %shard_map.90.kv_ref), channel_id=1, source_target_pairs={{0,64},{64,0},{1,65},{65,1},{2,66},{66,2},{3,67},{67,3},{4,68},{68... | collective-permute-start | bytes 786440 | tf_op jit(solution)/shard_map/ppermute | solution.py:31
  99.3 15.1 %collective-permute-start.23 = (bf16[1024,128]{1,0:T(8,128)(2,1)S(1)}, bf16[1024,128]{1,0:T(8,128)(2,1)S(1)}, u32[]{:S(2)}, u32[]{:S(2)}) collective-permute-start(bf16[1024,128]{1,0:T(8,128)(2,1)S(1)} %shard_map.90.kv_ref), channel_id=1, source_target_pairs={{0,32},{32,0},{1,33},{33,1},{2,34},{34,2},{3,35},{35,3},{4,36},{36... | collective-permute-start | bytes 786440 | tf_op jit(solution)/shard_map/ppermute | solution.py:31
  102.4 12.0 %collective-permute-start.24 = (bf16[1024,128]{1,0:T(8,128)(2,1)S(1)}, bf16[1024,128]{1,0:T(8,128)(2,1)S(1)}, u32[]{:S(2)}, u32[]{:S(2)}) collective-permute-start(bf16[1024,128]{1,0:T(8,128)(2,1)S(1)} %shard_map.90.kv_ref), channel_id=1, source_target_pairs={{0,96},{32,64},{64,32},{96,0},{1,97},{33,65},{65,33},{97,1},{2,98}... | collective-permute-start | bytes 786440 | tf_op jit(solution)/shard_map/ppermute | solution.py:344
  116.0 7.7 %collective-permute-start.25 = (bf16[528,128]{1,0:T(8,128)(2,1)S(1)}, bf16[528,128]{1,0:T(8,128)(2,1)S(1)}, u32[]{:S(2)}, u32[]{:S(2)}) collective-permute-start(bf16[528,128]{1,0:T(8,128)(2,1)S(1)} %shard_map.94), channel_id=1, source_target_pairs={{0,128},{64,192},{128,256},{192,320},{256,384},{320,448},{1,129},{... | collective-permute-start | bytes 405512 | tf_op jit(solution)/shard_map/ppermute | solution.py:44
  118.9 10.1 %collective-permute-start.26 = (bf16[528,128]{1,0:T(8,128)(2,1)S(1)}, bf16[528,128]{1,0:T(8,128)(2,1)S(1)}, u32[]{:S(2)}, u32[]{:S(2)}) collective-permute-start(bf16[528,128]{1,0:T(8,128)(2,1)S(1)} %shard_map.95), channel_id=1, source_target_pairs={{0,320},{64,256},{128,448},{192,384},{1,321},{65,257},{129,449},{1... | collective-permute-start | bytes 405512 | tf_op jit(solution)/shard_map/ppermute | solution.py:44
  121.7 10.3 %collective-permute-start.27 = (bf16[528,128]{1,0:T(8,128)(2,1)S(1)}, bf16[528,128]{1,0:T(8,128)(2,1)S(1)}, u32[]{:S(2)}, u32[]{:S(2)}) collective-permute-start(bf16[528,128]{1,0:T(8,128)(2,1)S(1)} %shard_map.96), channel_id=1, source_target_pairs={{0,384},{64,448},{1,385},{65,449},{2,386},{66,450},{3,387},{67,451... | collective-permute-start | bytes 405512 | tf_op jit(solution)/shard_map/ppermute | solution.py:44

commit v7 on v6

--- a/solution.py
+++ b/solution.py
@@ -129,9 +129,9 @@
             normed_ref[slot, part] = block.astype(jnp.bfloat16)
 
 
-def project_kernel(head, ids_ref, normed_ref, *refs):
-    pieces, out_ref = refs[:RING], refs[RING]
-    for slot, weights in enumerate(pieces):
+def project_kernel(head, slots, has_earlier, ids_ref, normed_ref, *refs):
+    pieces, out_ref = refs[: len(slots)], refs[-1]
+    for k, (slot, weights) in enumerate(zip(slots, pieces)):
         y_at = lax.rem(ids_ref[Y] + slot, RING)
         half = y_at // (RING // 2)
         part = jnp.where(half == ids_ref[XH], 0, 1)
@@ -142,20 +142,20 @@
             place = lax.rem(z_at + RING - ids_ref[Z], RING)
             term = jnp.dot(normed_ref[place, part], weights[2 * side + head], preferred_element_type=jnp.float32)
             product = term if product is None else product + term
-        if slot == 0:
-            out_ref[...] = product
+        if k == 0:
+            out_ref[...] = refs[len(slots)][...] + product if has_earlier else product
         else:
             out_ref[...] += product
 
 
-def project(head, ids, normed, pieces):
+def project(head, slots, ids, normed, pieces, earlier=()):
     return pl.pallas_call(
-        functools.partial(project_kernel, head),
+        functools.partial(project_kernel, head, slots, bool(earlier)),
         out_shape=jax.ShapeDtypeStruct((normed.shape[2], 2 * HD), jnp.float32),
-        in_specs=[SMEM] + [VMEM] * (1 + RING),
-        out_specs=VMEM,
-        compiler_params=params(),
-    )(ids, normed, *pieces)
+        in_specs=[SMEM] + [VMEM] * (1 + len(pieces) + len(earlier)),
+        out_specs=VMEM,
+        compiler_params=params(),
+    )(ids, normed, *pieces, *earlier)
 
 
 def join_kernel(mine_ref, theirs_ref, out_ref):
@@ -328,9 +328,11 @@
         out_specs=VMEM,
         compiler_params=params(),
     )(ids, own_sums, other_sums, table, *x_slots)
-    normed, q2 = lax.optimization_barrier((normed, q2))
-    theirs = shifted(project(1, ids, normed, w_slots), "c", 2, 1)
-    mine = project(0, ids, normed, w_slots)
+    near, far = (0, 1, 2, 3, 5, 6, 7), (4,)
+    half = project(1, near, ids, normed, [w_slots[k] for k in near])
+    half, q2 = lax.optimization_barrier((half, q2))
+    theirs = shifted(project(1, far, ids, normed, [w_slots[4]], (half,)), "c", 2, 1)
+    mine = project(0, tuple(range(RING)), ids, normed, w_slots)
     kv0 = pl.pallas_call(
         join_kernel,
         out_shape=jax.ShapeDtypeStruct((2 * span_len, HD), jnp.bfloat16),

time: 134 us -> 133 us (level)
    ppermute x21, starting transfers between devices: 83.7 us -> 82.1 us  [shifted(): lax.ppermute(value, axis, [(i, (i + by) % size) for i in range(size)])]
    pallas_call x2 -> x3, Pallas kernels: 3.57 us -> 4.26 us  [project(): pl.pallas_call(functools.partial(project_kernel, head, slots, bool(earlie...]
  transfers between devices with their start and end apart: 28 -> 28, of which waited for: 6 -> 5; matrix products, arithmetic and copies ran while one was open for 0% -> 0% of each run, Pallas kernels for 11% -> 11%
where the time goes in v7:
time: 133 us; the launch traced here: 132 us
  starting transfers between devices  92.6 us (70%)
  Pallas kernels  18.8 us (14%)
  waiting for transfers between devices  18.6 us (14%)
  local copies, waits for them, and re-layouts  1.96 us (1%)
    ppermute x21, starting transfers between devices, shifted(): lax.ppermute(value, axis, [(i, (i + by) % size) for i in range(size)])  82.1 us
    ppermute x6, waiting for transfers between devices, moved(): return lax.ppermute(value, ('yh', 'yl'), pairs)  9.32 us
    ppermute x21, waiting for transfers between devices, shifted(): lax.ppermute(value, axis, [(i, (i + by) % size) for i in range(size)])  9.24 us
    ppermute x6, starting transfers between devices, moved(): return lax.ppermute(value, ('yh', 'yl'), pairs)  8.53 us
    pallas_call x4, Pallas kernels, on_device(): pl.pallas_call(functools.partial(finish_kernel, later), out_shape=jax.Sha...  4.58 us
    pallas_call x3, Pallas kernels, project(): pl.pallas_call(functools.partial(project_kernel, head, slots, bool(earlie...  4.26 us
  transfers between devices with their start and end apart: 28, of which 5 were waited for; matrix products, arithmetic and copies ran while one was open for 0% of the time, Pallas kernels for 11%

profile of v7, /device:TPU:1, one launch (start us, length us, event | category | flops | bytes accessed | tf_op | source)
XLA Modules:
  0.0 132.5 jit_solution(15959814336585454816)
XLA Ops:
  0.0 0.9 constant_dynamic-slice_fusion
  1.1 8.8 %collective-permute-start = (bf16[192,256]{1,0:T(8,128)(2,1)S(1)}, bf16[192,256]{1,0:T(8,128)(2,1)S(1)}, u32[]{:S(2)}, u32[]{:S(2)}) collective-permute-start(bf16[192,256]{1,0:T(8,128)(2,1)S(1)} %pad_maximum_fusion.1), channel_id=1, source_target_pairs={{0,1},{1,0},{2,3},{3,2},{4,5},{5,4},{6,7},{7,6},{8,9},{9,8},{10,11... | collective-permute-start | bytes 294920 | tf_op jit(solution)/shard_map/ppermute | solution.py:31
  9.8 1.9 %collective-permute-start.4 = (bf16[192,512]{1,0:T(8,128)(2,1)}, bf16[192,512]{1,0:T(8,128)(2,1)S(1)}, u32[]{:S(2)}, u32[]{:S(2)}) collective-permute-start(bf16[192,512]{1,0:T(8,128)(2,1)} %bitcast.12), channel_id=1, source_target_pairs={{0,16},{16,0},{1,17},{17,1},{2,18},{18,2},{3,19},{19,3},{4,20},{20... | collective-permute-start | bytes 589832 | tf_op jit(solution)/shard_map/ppermute | solution.py:31
  11.8 1.9 %collective-permute-start.1 = (bf16[2,192,256]{2,1,0:T(8,128)(2,1)S(1)}, bf16[2,192,256]{2,1,0:T(8,128)(2,1)S(1)}, u32[]{:S(2)}, u32[]{:S(2)}) collective-permute-start(bf16[2,192,256]{2,1,0:T(8,128)(2,1)S(1)} %pad_maximum_fusion.refs_0_), channel_id=1, source_target_pairs={{0,32},{32,0},{1,33},{33,1},{2,34},{34,2},{3,35},{35,3},{4,36},{36... | collective-permute-start | bytes 589832 | tf_op jit(solution)/shard_map/ppermute | solution.py:31
  13.8 1.3 collective-permute-start.2
  15.1 1.3 collective-permute-start.3
  16.4 3.6 %collective-permute-done.4.refs_1_ = bf16[192,512]{1,0:T(8,128)(2,1)S(1)} collective-permute-done((bf16[192,512]{1,0:T(8,128)(2,1)}, bf16[192,512]{1,0:T(8,128)(2,1)S(1)}, u32[]{:S(2)}, u32[]{:S(2)}) %collective-permute-start.4) | collective-permute-done | bytes 196640 | tf_op jit(solution)/shard_map/ppermute | solution.py:31
  20.0 0.9 copy-done.2
  20.9 1.9 %collective-permute-start.5 = (bf16[384,512]{1,0:T(8,128)(2,1)S(1)}, bf16[384,512]{1,0:T(8,128)(2,1)S(1)}, u32[]{:S(2)}, u32[]{:S(2)}) collective-permute-start(bf16[384,512]{1,0:T(8,128)(2,1)S(1)} %shard_map.83.refs_0_), channel_id=1, source_target_pairs={{0,2},{2,4},{4,6},{6,8},{8,10},{10,12},{12,14},{14,0},{1,3},{3,5},... | collective-permute-start | bytes 1179656 | tf_op jit(solution)/shard_map/ppermute | solution.py:31
  22.9 0.8 collective-permute-done.2.q1
  23.7 0.2 collective-permute-done.3.q3
  23.9 3.0 %collective-permute-start.13 = (bf16[4,192,256]{2,1,0:T(8,128)(2,1)S(1)}, bf16[4,192,256]{2,1,0:T(8,128)(2,1)S(1)}, u32[]{:S(2)}, u32[]{:S(2)}) collective-permute-start(bf16[4,192,256]{2,1,0:T(8,128)(2,1)S(1)} %shard_map.82.refs_0_), channel_id=1, source_target_pairs={{0,448},{64,0},{128,64},{192,128},{256,192},{320,256},{384,320},{4... | collective-permute-start | bytes 1179656 | tf_op jit(solution)/shard_map/ppermute | solution.py:31
  26.9 10.8 %collective-permute-start.9 = (bf16[384,512]{1,0:T(8,128)(2,1)S(1)}, bf16[384,512]{1,0:T(8,128)(2,1)S(1)}, u32[]{:S(2)}, u32[]{:S(2)}) collective-permute-start(bf16[384,512]{1,0:T(8,128)(2,1)S(1)} %shard_map.83.refs_0_), channel_id=1, source_target_pairs={{0,14},{2,0},{4,2},{6,4},{8,6},{10,8},{12,10},{14,12},{1,15},{3,1}... | collective-permute-start | bytes 1179656 | tf_op jit(solution)/shard_map/ppermute | solution.py:31
  37.7 1.9 %collective-permute-start.6 = (bf16[384,512]{1,0:T(8,128)(2,1)S(1)}, bf16[384,512]{1,0:T(8,128)(2,1)S(1)}, u32[]{:S(2)}, u32[]{:S(2)}) collective-permute-start(bf16[384,512]{1,0:T(8,128)(2,1)S(1)} %collective-permute-done.5.refs_6_.refs_7_), channel_id=1, source_target_pairs={{0,2},{2,4},{4,6},{6,8},{8,10},{10,12},{12,14},{14,0},{1,3},{3,5},... | collective-permute-start | bytes 1179656 | tf_op jit(solution)/shard_map/ppermute | solution.py:31
  39.6 3.9 %collective-permute-start.16 = (bf16[4,192,256]{2,1,0:T(8,128)(2,1)S(1)}, bf16[4,192,256]{2,1,0:T(8,128)(2,1)S(1)}, u32[]{:S(2)}, u32[]{:S(2)}) collective-permute-start(bf16[4,192,256]{2,1,0:T(8,128)(2,1)S(1)} %shard_map.82.refs_0_), channel_id=1, source_target_pairs={{0,64},{64,128},{128,192},{192,256},{256,320},{320,384},{384,448},... | collective-permute-start | bytes 1179656 | tf_op jit(solution)/shard_map/ppermute | solution.py:31
  43.5 2.6 %collective-permute-start.14 = (bf16[4,192,256]{2,1,0:T(8,128)(2,1)S(1)}, bf16[4,192,256]{2,1,0:T(8,128)(2,1)S(1)}, u32[]{:S(2)}, u32[]{:S(2)}) collective-permute-start(bf16[4,192,256]{2,1,0:T(8,128)(2,1)S(1)} %collective-permute-done.13.refs_1_), channel_id=1, source_target_pairs={{0,448},{64,0},{128,64},{192,128},{256,192},{320,256},{384,320},{4... | collective-permute-start | bytes 1179656 | tf_op jit(solution)/shard_map/ppermute | solution.py:31
  46.1 4.6 %collective-permute-start.10 = (bf16[384,512]{1,0:T(8,128)(2,1)S(1)}, bf16[384,512]{1,0:T(8,128)(2,1)S(1)}, u32[]{:S(2)}, u32[]{:S(2)}) collective-permute-start(bf16[384,512]{1,0:T(8,128)(2,1)S(1)} %collective-permute-done.9.refs_1_), channel_id=1, source_target_pairs={{0,14},{2,0},{4,2},{6,4},{8,6},{10,8},{12,10},{14,12},{1,15},{3,1}... | collective-permute-start | bytes 1179656 | tf_op jit(solution)/shard_map/ppermute | solution.py:31
  50.7 1.9 %collective-permute-start.7 = (bf16[384,512]{1,0:T(8,128)(2,1)S(1)}, bf16[384,512]{1,0:T(8,128)(2,1)S(1)}, u32[]{:S(2)}, u32[]{:S(2)}) collective-permute-start(bf16[384,512]{1,0:T(8,128)(2,1)S(1)} %collective-permute-done.6.refs_5_.refs_6_), channel_id=1, source_target_pairs={{0,2},{2,4},{4,6},{6,8},{8,10},{10,12},{12,14},{14,0},{1,3},{3,5},... | collective-permute-start | bytes 1179656 | tf_op jit(solution)/shard_map/ppermute | solution.py:31
  52.7 3.2 %collective-permute-start.17 = (bf16[4,192,256]{2,1,0:T(8,128)(2,1)S(1)}, bf16[4,192,256]{2,1,0:T(8,128)(2,1)S(1)}, u32[]{:S(2)}, u32[]{:S(2)}) collective-permute-start(bf16[4,192,256]{2,1,0:T(8,128)(2,1)S(1)} %collective-permute-done.16.refs_6_.refs_7_), channel_id=1, source_target_pairs={{0,64},{64,128},{128,192},{192,256},{256,320},{320,384},{384,448},... | collective-permute-start | bytes 1179656 | tf_op jit(solution)/shard_map/ppermute | solution.py:31
  55.9 3.2 %collective-permute-start.15 = (bf16[4,192,256]{2,1,0:T(8,128)(2,1)S(1)}, bf16[4,192,256]{2,1,0:T(8,128)(2,1)S(1)}, u32[]{:S(2)}, u32[]{:S(2)}) collective-permute-start(bf16[4,192,256]{2,1,0:T(8,128)(2,1)S(1)} %collective-permute-done.14.refs_2_), channel_id=1, source_target_pairs={{0,448},{64,0},{128,64},{192,128},{256,192},{320,256},{384,320},{4... | collective-permute-start | bytes 1179656 | tf_op jit(solution)/shard_map/ppermute | solution.py:31
  59.2 4.6 %collective-permute-start.11 = (bf16[384,512]{1,0:T(8,128)(2,1)S(1)}, bf16[384,512]{1,0:T(8,128)(2,1)S(1)}, u32[]{:S(2)}, u32[]{:S(2)}) collective-permute-start(bf16[384,512]{1,0:T(8,128)(2,1)S(1)} %collective-permute-done.10.refs_2_), channel_id=1, source_target_pairs={{0,14},{2,0},{4,2},{6,4},{8,6},{10,8},{12,10},{14,12},{1,15},{3,1}... | collective-permute-start | bytes 1179656 | tf_op jit(solution)/shard_map/ppermute | solution.py:31
  63.8 1.9 %collective-permute-start.8 = (bf16[384,512]{1,0:T(8,128)(2,1)S(1)}, bf16[384,512]{1,0:T(8,128)(2,1)S(1)}, u32[]{:S(2)}, u32[]{:S(2)}) collective-permute-start(bf16[384,512]{1,0:T(8,128)(2,1)S(1)} %collective-permute-done.7.refs_4_.refs_5_), channel_id=1, source_target_pairs={{0,2},{2,4},{4,6},{6,8},{8,10},{10,12},{12,14},{14,0},{1,3},{3,5},... | collective-permute-start | bytes 1179656 | tf_op jit(solution)/shard_map/ppermute | solution.py:31
  65.7 2.0 %collective-permute-start.18 = (bf16[4,192,256]{2,1,0:T(8,128)(2,1)S(1)}, bf16[4,192,256]{2,1,0:T(8,128)(2,1)S(1)}, u32[]{:S(2)}, u32[]{:S(2)}) collective-permute-start(bf16[4,192,256]{2,1,0:T(8,128)(2,1)S(1)} %collective-permute-done.17.refs_5_.refs_6_), channel_id=1, source_target_pairs={{0,64},{64,128},{128,192},{192,256},{256,320},{320,384},{384,448},... | collective-permute-start | bytes 1179656 | tf_op jit(solution)/shard_map/ppermute | solution.py:31
  67.8 4.5 %collective-permute-start.20 = (bf16[4,192,256]{2,1,0:T(8,128)(2,1)S(1)}, bf16[4,192,256]{2,1,0:T(8,128)(2,1)S(1)}, u32[]{:S(2)}, u32[]{:S(2)}) collective-permute-start(bf16[4,192,256]{2,1,0:T(8,128)(2,1)S(1)} %collective-permute-done.15.refs_3_), channel_id=1, source_target_pairs={{0,448},{64,0},{128,64},{192,128},{256,192},{320,256},{384,320},{4... | collective-permute-start | bytes 1179656 | tf_op jit(solution)/shard_map/ppermute | solution.py:31
  72.2 1.3 collective-permute-start.19
  73.5 0.5 shard_map.84.refs_1_
  74.2 6.7 %collective-permute-start.12 = (f32[8,512]{1,0:T(8,128)S(1)}, f32[8,512]{1,0:T(8,128)S(1)}, u32[]{:S(2)}, u32[]{:S(2)}) collective-permute-start(f32[8,512]{1,0:T(8,128)S(1)} %shard_map.85.own_ref), channel_id=1, source_target_pairs={{0,1},{1,0},{2,3},{3,2},{4,5},{5,4},{6,7},{7,6},{8,9},{9,8},{10,11... | collective-permute-start | bytes 49160 | tf_op jit(solution)/shard_map/ppermute | solution.py:31
  80.9 0.7 shard_map.86.table_ref
  81.7 2.6 %shard_map.87.normed_ref = bf16[8,2,512,192]{3,2,1,0:T(8,128)(2,1)S(1)} custom-call(s32[8]{0:T(128)S(1)} %stack.44.ids_ref, f32[8,512]{1,0:T(8,128)S(1)} %shard_map.85.own_ref, f32[8,512]{1,0:T(8,128)S(1)} %collective-permute-done.12.other_ref, f32[64,192]{1,0:T(8,128)S(1)} %shard_map.86.table_ref, bf16[384,512]{1,0:T(8,128)(2,1)S(1)} %shard_map.83.refs_0_, ...), custom_call_target="tpu_custom_call" | custom-call | tf_op jit(solution)/shard_map/pallas_call | solution.py:324
  84.3 1.6 %shard_map.88.refs_1_ = f32[512,256]{1,0:T(8,128)S(1)} custom-call(s32[8]{0:T(128)S(1)} %stack.44.ids_ref, bf16[8,2,512,192]{3,2,1,0:T(8,128)(2,1)S(1)} %shard_map.87.normed_ref, bf16[4,192,256]{2,1,0:T(8,128)(2,1)S(1)} %shard_map.82.refs_0_, bf16[4,192,256]{2,1,0:T(8,128)(2,1)S(1)} %collective-permute-done.13.refs_1_, ...), custom_call_target="tpu_custom_call" | custom-call | tf_op jit(solution)/shard_map/pallas_call | solution.py:152
  86.0 0.8 shard_map.90
  86.8 3.2 %collective-permute-start.21 = (f32[512,256]{1,0:T(8,128)S(1)}, f32[512,256]{1,0:T(8,128)S(1)}, u32[]{:S(2)}, u32[]{:S(2)}) collective-permute-start(f32[512,256]{1,0:T(8,128)S(1)} %shard_map.90), channel_id=1, source_target_pairs={{0,1},{1,0},{2,3},{3,2},{4,5},{5,4},{6,7},{7,6},{8,9},{9,8},{10,11... | collective-permute-start | bytes 1572872 | tf_op jit(solution)/shard_map/ppermute | solution.py:31
  90.0 1.8 %shard_map.89.mine_ref = f32[512,256]{1,0:T(8,128)S(1)} custom-call(s32[8]{0:T(128)S(1)} %stack.44.ids_ref, bf16[8,2,512,192]{3,2,1,0:T(8,128)(2,1)S(1)} %shard_map.87.normed_ref, bf16[4,192,256]{2,1,0:T(8,128)(2,1)S(1)} %shard_map.82.refs_0_, bf16[4,192,256]{2,1,0:T(8,128)(2,1)S(1)} %collective-permute-done.13.refs_1_, ...), custom_call_target="tpu_custom_call" | custom-call | tf_op jit(solution)/shard_map/pallas_call | solution.py:152
  91.9 6.5 %collective-permute-start.22 = (bf16[1024,128]{1,0:T(8,128)(2,1)S(1)}, bf16[1024,128]{1,0:T(8,128)(2,1)S(1)}, u32[]{:S(2)}, u32[]{:S(2)}) collective-permute-start(bf16[1024,128]{1,0:T(8,128)(2,1)S(1)} %shard_map.91.kv_ref), channel_id=1, source_target_pairs={{0,64},{64,0},{1,65},{65,1},{2,66},{66,2},{3,67},{67,3},{4,68},{68... | collective-permute-start | bytes 786440 | tf_op jit(solution)/shard_map/ppermute | solution.py:31
  98.4 3.1 %collective-permute-start.23 = (bf16[1024,128]{1,0:T(8,128)(2,1)S(1)}, bf16[1024,128]{1,0:T(8,128)(2,1)S(1)}, u32[]{:S(2)}, u32[]{:S(2)}) collective-permute-start(bf16[1024,128]{1,0:T(8,128)(2,1)S(1)} %shard_map.91.kv_ref), channel_id=1, source_target_pairs={{0,32},{32,0},{1,33},{33,1},{2,34},{34,2},{3,35},{35,3},{4,36},{36... | collective-permute-start | bytes 786440 | tf_op jit(solution)/shard_map/ppermute | solution.py:31
  101.5 1.9 %collective-permute-start.24 = (bf16[1024,128]{1,0:T(8,128)(2,1)S(1)}, bf16[1024,128]{1,0:T(8,128)(2,1)S(1)}, u32[]{:S(2)}, u32[]{:S(2)}) collective-permute-start(bf16[1024,128]{1,0:T(8,128)(2,1)S(1)} %shard_map.91.kv_ref), channel_id=1, source_target_pairs={{0,96},{32,64},{64,32},{96,0},{1,97},{33,65},{65,33},{97,1},{2,98}... | collective-permute-start | bytes 786440 | tf_op jit(solution)/shard_map/ppermute | solution.py:346
  103.4 2.4 %shard_map.92 = (bf16[4,128,512]{2,1,0:T(8,128)(2,1)S(1)}, f32[4,16,512]{2,1,0:T(8,128)S(1)}, f32[4,128,512]{2,1,0:T(8,128)S(1)}) custom-call(s32[8]{0:T(128)S(1)} %stack.44.ids_ref, s32[16,16]{1,0:T(8,128)S(1)} %copy-done, s32[16]{0:T(128)S(1)} %copy-done.4, bf16[512,128]{1,0:T(8,128)(2,1)S(1)} %copy-done.3, ...), custom_call_target="tpu_custom_call" | custom-call | tf_op jit(solution)/shard_map/pallas_call | solution.py:351
  105.8 2.1 %shard_map.93 = (f32[4,16,512]{2,1,0:T(8,128)S(1)}, f32[4,128,512]{2,1,0:T(8,128)S(1)}) custom-call(s32[8]{0:T(128)S(1)} %stack.44.ids_ref, s32[16,16]{1,0:T(8,128)S(1)} %copy-done, s32[16]{0:T(128)S(1)} %copy-done.4, bf16[4,128,512]{2,1,0:T(8,128)(2,1)S(1)} %get-tuple-element.24.q_t, ...), custom_call_target="tpu_custom_call", output_to_operand_aliasing={{0}: (4, {}), {1}: (5, {})} | custom-call | tf_op jit(solution)/shard_map/pallas_call | solution.py:358
  107.9 5.5 %collective-permute-done.23.kv1 = bf16[1024,128]{1,0:T(8,128)(2,1)S(1)} collective-permute-done((bf16[1024,128]{1,0:T(8,128)(2,1)S(1)}, bf16[1024,128]{1,0:T(8,128)(2,1)S(1)}, u32[]{:S(2)}, u32[]{:S(2)}) %collective-permute-start.23) | collective-permute-done | bytes 262176 | tf_op jit(solution)/shard_map/ppermute | solution.py:31
  113.4 1.6 %shard_map.95 = bf16[528,128]{1,0:T(8,128)(2,1)S(1)} custom-call(s32[8]{0:T(128)S(1)} %stack.44.ids_ref, s32[16,16]{1,0:T(8,128)S(1)} %copy-done, s32[16]{0:T(128)S(1)} %copy-done.4, bf16[4,128,512]{2,1,0:T(8,128)(2,1)S(1)} %get-tuple-element.24.q_t, f32[4,16,512]{2,1,0:T(8,128)S(1)} %get-tuple-element.27.stat_in, ...), custom_call_target="tpu_custom_call" | custom-call | tf_op jit(solution)/shard_map/pallas_call | solution.py:368
  115.1 1.5 %collective-permute-start.25 = (bf16[528,128]{1,0:T(8,128)(2,1)S(1)}, bf16[528,128]{1,0:T(8,128)(2,1)S(1)}, u32[]{:S(2)}, u32[]{:S(2)}) collective-permute-start(bf16[528,128]{1,0:T(8,128)(2,1)S(1)} %shard_map.95), channel_id=1, source_target_pairs={{0,128},{64,192},{128,256},{192,320},{256,384},{320,448},{1,129},{... | collective-permute-start | bytes 405512 | tf_op jit(solution)/shard_map/ppermute | solution.py:44
  116.5 1.4 %shard_map.96 = bf16[528,128]{1,0:T(8,128)(2,1)S(1)} custom-call(s32[8]{0:T(128)S(1)} %stack.44.ids_ref, s32[16,16]{1,0:T(8,128)S(1)} %copy-done, s32[16]{0:T(128)S(1)} %copy-done.4, bf16[4,128,512]{2,1,0:T(8,128)(2,1)S(1)} %get-tuple-element.24.q_t, f32[4,16,512]{2,1,0:T(8,128)S(1)} %get-tuple-element.27.stat_in, ...), custom_call_target="tpu_custom_call" | custom-call | tf_op jit(solution)/shard_map/pallas_call | solution.py:368
  118.0 1.9 %collective-permute-start.26 = (bf16[528,128]{1,0:T(8,128)(2,1)S(1)}, bf16[528,128]{1,0:T(8,128)(2,1)S(1)}, u32[]{:S(2)}, u32[]{:S(2)}) collective-permute-start(bf16[528,128]{1,0:T(8,128)(2,1)S(1)} %shard_map.96), channel_id=1, source_target_pairs={{0,320},{64,256},{128,448},{192,384},{1,321},{65,257},{129,449},{1... | collective-permute-start | bytes 405512 | tf_op jit(solution)/shard_map/ppermute | solution.py:44
  119.9 0.8 shard_map.97
  120.6 1.3 collective-permute-start.27
  122.0 0.8 shard_map.94.part0
  122.8 8.3 %collective-permute-done.27.part3 = bf16[528,128]{1,0:T(8,128)(2,1)S(1)} collective-permute-done((bf16[528,128]{1,0:T(8,128)(2,1)S(1)}, bf16[528,128]{1,0:T(8,128)(2,1)S(1)}, u32[]{:S(2)}, u32[]{:S(2)}) %collective-permute-start.27) | collective-permute-done | bytes 135200 | tf_op jit(solution)/shard_map/ppermute | solution.py:44
  131.1 1.4 %shard_map.98 = bf16[512,128]{1,0:T(8,128)(2,1)} custom-call(s32[8]{0:T(128)S(1)} %stack.44.ids_ref, s32[16]{0:T(128)S(1)} %copy-done.4, bf16[528,128]{1,0:T(8,128)(2,1)S(1)} %shard_map.94.part0, bf16[528,128]{1,0:T(8,128)(2,1)S(1)} %collective-permute-done.25.part1, bf16[528,128]{1,0:T(8,128)(2,1)S(1)} %collective-permute-done.26.part2, ...), custom_call_target="tpu_custom_call" | custom-call | tf_op jit(solution)/shard_map/pallas_call | solution.py:377
  (42 shorter events, 0.5 us)
Async XLA Ops:
  0.0 80.9 %copy-start.5 = (s32[16]{0:T(128)S(1)}, s32[16]{0:T(128)}, u32[]{:S(2)}) copy-start(s32[16]{0:T(128)} %levels_ref.1) | copy-start | bytes 196
  0.0 80.9 %copy-start.1 = (bf16[8,12288]{1,0:T(8,128)(2,1)S(1)}, bf16[8,12288]{1,0:T(8,128)(2,1)}, u32[]{:S(2)}) copy-start(bf16[8,12288]{1,0:T(8,128)(2,1)} %modulation_ref.1) | copy-start | bytes 589828
  1.1 10.7 %collective-permute-start = (bf16[192,256]{1,0:T(8,128)(2,1)S(1)}, bf16[192,256]{1,0:T(8,128)(2,1)S(1)}, u32[]{:S(2)}, u32[]{:S(2)}) collective-permute-start(bf16[192,256]{1,0:T(8,128)(2,1)S(1)} %pad_maximum_fusion.1), channel_id=1, source_target_pairs={{0,1},{1,0},{2,3},{3,2},{4,5},{5,4},{6,7},{7,6},{8,9},{9,8},{10,11... | collective-permute-start | bytes 294920 | tf_op jit(solution)/shard_map/ppermute | solution.py:31
  9.8 10.1 %collective-permute-start.4 = (bf16[192,512]{1,0:T(8,128)(2,1)}, bf16[192,512]{1,0:T(8,128)(2,1)S(1)}, u32[]{:S(2)}, u32[]{:S(2)}) collective-permute-start(bf16[192,512]{1,0:T(8,128)(2,1)} %bitcast.12), channel_id=1, source_target_pairs={{0,16},{16,0},{1,17},{17,1},{2,18},{18,2},{3,19},{19,3},{4,20},{20... | collective-permute-start | bytes 589832 | tf_op jit(solution)/shard_map/ppermute | solution.py:31
  11.8 11.0 %collective-permute-start.1 = (bf16[2,192,256]{2,1,0:T(8,128)(2,1)S(1)}, bf16[2,192,256]{2,1,0:T(8,128)(2,1)S(1)}, u32[]{:S(2)}, u32[]{:S(2)}) collective-permute-start(bf16[2,192,256]{2,1,0:T(8,128)(2,1)S(1)} %pad_maximum_fusion.refs_0_), channel_id=1, source_target_pairs={{0,32},{32,0},{1,33},{33,1},{2,34},{34,2},{3,35},{35,3},{4,36},{36... | collective-permute-start | bytes 589832 | tf_op jit(solution)/shard_map/ppermute | solution.py:31
  13.8 10.0 %collective-permute-start.2 = (bf16[512,128]{1,0:T(8,128)(2,1)}, bf16[512,128]{1,0:T(8,128)(2,1)S(1)}, u32[]{:S(2)}, u32[]{:S(2)}) collective-permute-start(bf16[512,128]{1,0:T(8,128)(2,1)} %q0.1), channel_id=1, source_target_pairs={{128,0},{192,64},{256,128},{320,192},{384,256},{448,320},{129,1},{... | collective-permute-start | bytes 393224 | tf_op jit(solution)/shard_map/ppermute | solution.py:44
  15.1 8.8 %collective-permute-start.3 = (bf16[512,128]{1,0:T(8,128)(2,1)}, bf16[512,128]{1,0:T(8,128)(2,1)S(1)}, u32[]{:S(2)}, u32[]{:S(2)}) collective-permute-start(bf16[512,128]{1,0:T(8,128)(2,1)} %q0.1), channel_id=1, source_target_pairs={{384,0},{448,64},{385,1},{449,65},{386,2},{450,66},{387,3},{451,67... | collective-permute-start | bytes 393224 | tf_op jit(solution)/shard_map/ppermute | solution.py:44
  20.0 0.9 copy-start.2
  20.9 16.7 %collective-permute-start.5 = (bf16[384,512]{1,0:T(8,128)(2,1)S(1)}, bf16[384,512]{1,0:T(8,128)(2,1)S(1)}, u32[]{:S(2)}, u32[]{:S(2)}) collective-permute-start(bf16[384,512]{1,0:T(8,128)(2,1)S(1)} %shard_map.83.refs_0_), channel_id=1, source_target_pairs={{0,2},{2,4},{4,6},{6,8},{8,10},{10,12},{12,14},{14,0},{1,3},{3,5},... | collective-permute-start | bytes 1179656 | tf_op jit(solution)/shard_map/ppermute | solution.py:31
  23.9 19.6 %collective-permute-start.13 = (bf16[4,192,256]{2,1,0:T(8,128)(2,1)S(1)}, bf16[4,192,256]{2,1,0:T(8,128)(2,1)S(1)}, u32[]{:S(2)}, u32[]{:S(2)}) collective-permute-start(bf16[4,192,256]{2,1,0:T(8,128)(2,1)S(1)} %shard_map.82.refs_0_), channel_id=1, source_target_pairs={{0,448},{64,0},{128,64},{192,128},{256,192},{320,256},{384,320},{4... | collective-permute-start | bytes 1179656 | tf_op jit(solution)/shard_map/ppermute | solution.py:31
  26.9 19.2 %collective-permute-start.9 = (bf16[384,512]{1,0:T(8,128)(2,1)S(1)}, bf16[384,512]{1,0:T(8,128)(2,1)S(1)}, u32[]{:S(2)}, u32[]{:S(2)}) collective-permute-start(bf16[384,512]{1,0:T(8,128)(2,1)S(1)} %shard_map.83.refs_0_), channel_id=1, source_target_pairs={{0,14},{2,0},{4,2},{6,4},{8,6},{10,8},{12,10},{14,12},{1,15},{3,1}... | collective-permute-start | bytes 1179656 | tf_op jit(solution)/shard_map/ppermute | solution.py:31
  37.7 13.0 %collective-permute-start.6 = (bf16[384,512]{1,0:T(8,128)(2,1)S(1)}, bf16[384,512]{1,0:T(8,128)(2,1)S(1)}, u32[]{:S(2)}, u32[]{:S(2)}) collective-permute-start(bf16[384,512]{1,0:T(8,128)(2,1)S(1)} %collective-permute-done.5.refs_6_.refs_7_), channel_id=1, source_target_pairs={{0,2},{2,4},{4,6},{6,8},{8,10},{10,12},{12,14},{14,0},{1,3},{3,5},... | collective-permute-start | bytes 1179656 | tf_op jit(solution)/shard_map/ppermute | solution.py:31
  39.6 13.1 %collective-permute-start.16 = (bf16[4,192,256]{2,1,0:T(8,128)(2,1)S(1)}, bf16[4,192,256]{2,1,0:T(8,128)(2,1)S(1)}, u32[]{:S(2)}, u32[]{:S(2)}) collective-permute-start(bf16[4,192,256]{2,1,0:T(8,128)(2,1)S(1)} %shard_map.82.refs_0_), channel_id=1, source_target_pairs={{0,64},{64,128},{128,192},{192,256},{256,320},{320,384},{384,448},... | collective-permute-start | bytes 1179656 | tf_op jit(solution)/shard_map/ppermute | solution.py:31
  43.5 12.4 %collective-permute-start.14 = (bf16[4,192,256]{2,1,0:T(8,128)(2,1)S(1)}, bf16[4,192,256]{2,1,0:T(8,128)(2,1)S(1)}, u32[]{:S(2)}, u32[]{:S(2)}) collective-permute-start(bf16[4,192,256]{2,1,0:T(8,128)(2,1)S(1)} %collective-permute-done.13.refs_1_), channel_id=1, source_target_pairs={{0,448},{64,0},{128,64},{192,128},{256,192},{320,256},{384,320},{4... | collective-permute-start | bytes 1179656 | tf_op jit(solution)/shard_map/ppermute | solution.py:31
  46.1 13.1 %collective-permute-start.10 = (bf16[384,512]{1,0:T(8,128)(2,1)S(1)}, bf16[384,512]{1,0:T(8,128)(2,1)S(1)}, u32[]{:S(2)}, u32[]{:S(2)}) collective-permute-start(bf16[384,512]{1,0:T(8,128)(2,1)S(1)} %collective-permute-done.9.refs_1_), channel_id=1, source_target_pairs={{0,14},{2,0},{4,2},{6,4},{8,6},{10,8},{12,10},{14,12},{1,15},{3,1}... | collective-permute-start | bytes 1179656 | tf_op jit(solution)/shard_map/ppermute | solution.py:31
  50.7 13.1 %collective-permute-start.7 = (bf16[384,512]{1,0:T(8,128)(2,1)S(1)}, bf16[384,512]{1,0:T(8,128)(2,1)S(1)}, u32[]{:S(2)}, u32[]{:S(2)}) collective-permute-start(bf16[384,512]{1,0:T(8,128)(2,1)S(1)} %collective-permute-done.6.refs_5_.refs_6_), channel_id=1, source_target_pairs={{0,2},{2,4},{4,6},{6,8},{8,10},{10,12},{12,14},{14,0},{1,3},{3,5},... | collective-permute-start | bytes 1179656 | tf_op jit(solution)/shard_map/ppermute | solution.py:31
  52.7 13.1 %collective-permute-start.17 = (bf16[4,192,256]{2,1,0:T(8,128)(2,1)S(1)}, bf16[4,192,256]{2,1,0:T(8,128)(2,1)S(1)}, u32[]{:S(2)}, u32[]{:S(2)}) collective-permute-start(bf16[4,192,256]{2,1,0:T(8,128)(2,1)S(1)} %collective-permute-done.16.refs_6_.refs_7_), channel_id=1, source_target_pairs={{0,64},{64,128},{128,192},{192,256},{256,320},{320,384},{384,448},... | collective-permute-start | bytes 1179656 | tf_op jit(solution)/shard_map/ppermute | solution.py:31
  55.9 11.8 %collective-permute-start.15 = (bf16[4,192,256]{2,1,0:T(8,128)(2,1)S(1)}, bf16[4,192,256]{2,1,0:T(8,128)(2,1)S(1)}, u32[]{:S(2)}, u32[]{:S(2)}) collective-permute-start(bf16[4,192,256]{2,1,0:T(8,128)(2,1)S(1)} %collective-permute-done.14.refs_2_), channel_id=1, source_target_pairs={{0,448},{64,0},{128,64},{192,128},{256,192},{320,256},{384,320},{4... | collective-permute-start | bytes 1179656 | tf_op jit(solution)/shard_map/ppermute | solution.py:31
  59.2 14.4 %collective-permute-start.11 = (bf16[384,512]{1,0:T(8,128)(2,1)S(1)}, bf16[384,512]{1,0:T(8,128)(2,1)S(1)}, u32[]{:S(2)}, u32[]{:S(2)}) collective-permute-start(bf16[384,512]{1,0:T(8,128)(2,1)S(1)} %collective-permute-done.10.refs_2_), channel_id=1, source_target_pairs={{0,14},{2,0},{4,2},{6,4},{8,6},{10,8},{12,10},{14,12},{1,15},{3,1}... | collective-permute-start | bytes 1179656 | tf_op jit(solution)/shard_map/ppermute | solution.py:31
  63.8 10.3 %collective-permute-start.8 = (bf16[384,512]{1,0:T(8,128)(2,1)S(1)}, bf16[384,512]{1,0:T(8,128)(2,1)S(1)}, u32[]{:S(2)}, u32[]{:S(2)}) collective-permute-start(bf16[384,512]{1,0:T(8,128)(2,1)S(1)} %collective-permute-done.7.refs_4_.refs_5_), channel_id=1, source_target_pairs={{0,2},{2,4},{4,6},{6,8},{8,10},{10,12},{12,14},{14,0},{1,3},{3,5},... | collective-permute-start | bytes 1179656 | tf_op jit(solution)/shard_map/ppermute | solution.py:31
  65.7 18.6 %collective-permute-start.18 = (bf16[4,192,256]{2,1,0:T(8,128)(2,1)S(1)}, bf16[4,192,256]{2,1,0:T(8,128)(2,1)S(1)}, u32[]{:S(2)}, u32[]{:S(2)}) collective-permute-start(bf16[4,192,256]{2,1,0:T(8,128)(2,1)S(1)} %collective-permute-done.17.refs_5_.refs_6_), channel_id=1, source_target_pairs={{0,64},{64,128},{128,192},{192,256},{256,320},{320,384},{384,448},... | collective-permute-start | bytes 1179656 | tf_op jit(solution)/shard_map/ppermute | solution.py:31
  67.8 18.2 %collective-permute-start.20 = (bf16[4,192,256]{2,1,0:T(8,128)(2,1)S(1)}, bf16[4,192,256]{2,1,0:T(8,128)(2,1)S(1)}, u32[]{:S(2)}, u32[]{:S(2)}) collective-permute-start(bf16[4,192,256]{2,1,0:T(8,128)(2,1)S(1)} %collective-permute-done.15.refs_3_), channel_id=1, source_target_pairs={{0,448},{64,0},{128,64},{192,128},{256,192},{320,256},{384,320},{4... | collective-permute-start | bytes 1179656 | tf_op jit(solution)/shard_map/ppermute | solution.py:31
  72.2 13.7 %collective-permute-start.19 = (bf16[512,128]{1,0:T(8,128)(2,1)}, bf16[512,128]{1,0:T(8,128)(2,1)S(1)}, u32[]{:S(2)}, u32[]{:S(2)}) collective-permute-start(bf16[512,128]{1,0:T(8,128)(2,1)} %q0.1), channel_id=1, source_target_pairs={{256,64},{320,0},{384,192},{448,128},{257,65},{321,1},{385,193},{4... | collective-permute-start | bytes 393224 | tf_op jit(solution)/shard_map/ppermute | solution.py:44
  74.2 7.5 %collective-permute-start.12 = (f32[8,512]{1,0:T(8,128)S(1)}, f32[8,512]{1,0:T(8,128)S(1)}, u32[]{:S(2)}, u32[]{:S(2)}) collective-permute-start(f32[8,512]{1,0:T(8,128)S(1)} %shard_map.85.own_ref), channel_id=1, source_target_pairs={{0,1},{1,0},{2,3},{3,2},{4,5},{5,4},{6,7},{7,6},{8,9},{9,8},{10,11... | collective-permute-start | bytes 49160 | tf_op jit(solution)/shard_map/ppermute | solution.py:31
  86.8 16.6 %copy-start = (s32[16,16]{1,0:T(8,128)S(1)}, s32[16,16]{1,0:T(8,128)}, u32[]{:S(2)}) copy-start(s32[16,16]{1,0:T(8,128)} %visible_ref.11) | copy-start | bytes 3076
  86.8 16.6 %copy-start.3 = (bf16[512,128]{1,0:T(8,128)(2,1)S(1)}, bf16[512,128]{1,0:T(8,128)(2,1)}, u32[]{:S(2)}) copy-start(bf16[512,128]{1,0:T(8,128)(2,1)} %q0.1) | copy-start | bytes 393220
  86.8 16.6 %copy-start.4 = (s32[16]{0:T(128)S(1)}, s32[16]{0:T(128)}, u32[]{:S(2)}) copy-start(s32[16]{0:T(128)} %counts_ref.13) | copy-start | bytes 196
  86.8 5.0 %collective-permute-start.21 = (f32[512,256]{1,0:T(8,128)S(1)}, f32[512,256]{1,0:T(8,128)S(1)}, u32[]{:S(2)}, u32[]{:S(2)}) collective-permute-start(f32[512,256]{1,0:T(8,128)S(1)} %shard_map.90), channel_id=1, source_target_pairs={{0,1},{1,0},{2,3},{3,2},{4,5},{5,4},{6,7},{7,6},{8,9},{9,8},{10,11... | collective-permute-start | bytes 1572872 | tf_op jit(solution)/shard_map/ppermute | solution.py:31
  91.9 13.9 %collective-permute-start.22 = (bf16[1024,128]{1,0:T(8,128)(2,1)S(1)}, bf16[1024,128]{1,0:T(8,128)(2,1)S(1)}, u32[]{:S(2)}, u32[]{:S(2)}) collective-permute-start(bf16[1024,128]{1,0:T(8,128)(2,1)S(1)} %shard_map.91.kv_ref), channel_id=1, source_target_pairs={{0,64},{64,0},{1,65},{65,1},{2,66},{66,2},{3,67},{67,3},{4,68},{68... | collective-permute-start | bytes 786440 | tf_op jit(solution)/shard_map/ppermute | solution.py:31
  98.4 15.1 %collective-permute-start.23 = (bf16[1024,128]{1,0:T(8,128)(2,1)S(1)}, bf16[1024,128]{1,0:T(8,128)(2,1)S(1)}, u32[]{:S(2)}, u32[]{:S(2)}) collective-permute-start(bf16[1024,128]{1,0:T(8,128)(2,1)S(1)} %shard_map.91.kv_ref), channel_id=1, source_target_pairs={{0,32},{32,0},{1,33},{33,1},{2,34},{34,2},{3,35},{35,3},{4,36},{36... | collective-permute-start | bytes 786440 | tf_op jit(solution)/shard_map/ppermute | solution.py:31
  101.5 12.0 %collective-permute-start.24 = (bf16[1024,128]{1,0:T(8,128)(2,1)S(1)}, bf16[1024,128]{1,0:T(8,128)(2,1)S(1)}, u32[]{:S(2)}, u32[]{:S(2)}) collective-permute-start(bf16[1024,128]{1,0:T(8,128)(2,1)S(1)} %shard_map.91.kv_ref), channel_id=1, source_target_pairs={{0,96},{32,64},{64,32},{96,0},{1,97},{33,65},{65,33},{97,1},{2,98}... | collective-permute-start | bytes 786440 | tf_op jit(solution)/shard_map/ppermute | solution.py:346
  115.1 7.7 %collective-permute-start.25 = (bf16[528,128]{1,0:T(8,128)(2,1)S(1)}, bf16[528,128]{1,0:T(8,128)(2,1)S(1)}, u32[]{:S(2)}, u32[]{:S(2)}) collective-permute-start(bf16[528,128]{1,0:T(8,128)(2,1)S(1)} %shard_map.95), channel_id=1, source_target_pairs={{0,128},{64,192},{128,256},{192,320},{256,384},{320,448},{1,129},{... | collective-permute-start | bytes 405512 | tf_op jit(solution)/shard_map/ppermute | solution.py:44
  118.0 4.8 %collective-permute-start.26 = (bf16[528,128]{1,0:T(8,128)(2,1)S(1)}, bf16[528,128]{1,0:T(8,128)(2,1)S(1)}, u32[]{:S(2)}, u32[]{:S(2)}) collective-permute-start(bf16[528,128]{1,0:T(8,128)(2,1)S(1)} %shard_map.96), channel_id=1, source_target_pairs={{0,320},{64,256},{128,448},{192,384},{1,321},{65,257},{129,449},{1... | collective-permute-start | bytes 405512 | tf_op jit(solution)/shard_map/ppermute | solution.py:44
  120.6 10.4 %collective-permute-start.27 = (bf16[528,128]{1,0:T(8,128)(2,1)S(1)}, bf16[528,128]{1,0:T(8,128)(2,1)S(1)}, u32[]{:S(2)}, u32[]{:S(2)}) collective-permute-start(bf16[528,128]{1,0:T(8,128)(2,1)S(1)} %shard_map.97), channel_id=1, source_target_pairs={{0,384},{64,448},{1,385},{65,449},{2,386},{66,450},{3,387},{67,451... | collective-permute-start | bytes 405512 | tf_op jit(solution)/shard_map/ppermute | solution.py:44
